TPU v7x, 32 devices: a whole 2x2x4 slice. The times are simulated.
32 devices in a mesh: rep: 2 (over y), node: 4 (over z), local: 4 (over x, core).
Axes of the slice: x: 2, y: 2, z: 4, core: 2. Of those that a mesh axis runs over, the one named last changes fastest.
Arguments:
- tokens: bfloat16 [4096, 3584], P(('rep', 'node', 'local')), parts along dimension 0, may hold values from -6 to 6
- routes: int32 [4096, 2], P(('rep', 'node', 'local')), parts along dimension 0, may hold values from 0 to 7, all different within a row; in each aligned block of 128 rows (0 to 127, 128 to 255, ...) at most 40 rows name the same one
- gates: float32 [4096, 2], P(('rep', 'node', 'local')), parts along dimension 0, may hold values from 0.1 to 1.5
- placement: int32 [8], replicated, may hold values from 0 to 7, each once
- upstream: bfloat16 [4096, 3584], P(('rep', 'node', 'local')), parts along dimension 0, may hold values from -6 to 6
- w_gate: bfloat16 [16, 3584, 512], P(('node', 'local')), may hold values from -0.09375 to 0.09375
- w_up: bfloat16 [16, 3584, 512], P(('node', 'local')), may hold values from -0.09375 to 0.09375
- w_down: bfloat16 [16, 512, 3584], P(('node', 'local')), may hold values from -0.1875 to 0.1875
Outputs:
- grad_tokens: bfloat16 [4096, 3584], P(('rep', 'node', 'local')), parts along dimension 0
- grad_gates: float32 [4096, 2], P(('rep', 'node', 'local')), parts along dimension 0
There are 2 independent parts, one for each index of `rep`. A program takes and returns all parts, laid end to end along the dimension named above; an argument that names none is the same for every part. Nothing has to cross between parts.
Inputs may be any that keep to these rules, and one draw needn't show every extreme that they name: `routes`: each row names 2 different experts; among the 128 rows of one device no expert is named by more than 40 rows, a bound that some block reaches. `placement`: A permutation of the slots.
All inputs are finite; a program needn't handle non-finite values.
Results may differ from a plain program's by a relative error of at most 0.015.
Values may be sent and summed in bfloat16 or wider, within the bound.
No kernel may reach another device: no remote copies, remote signals or barrier semaphores. Data moves between devices by JAX's collectives and lax.ppermute only.
A program may use at most 128 MiB of HBM per device.

v0:
```python
import jax
import jax.numpy as jnp
from jax import lax
from jax.sharding import PartitionSpec as P


def expert_piece(got_tokens, got_upstream, gate_col, gate_piece, up_piece, down_piece):
    gate_lin = jnp.dot(got_tokens, gate_piece, preferred_element_type=jnp.float32)
    up_lin = jnp.dot(got_tokens, up_piece, preferred_element_type=jnp.float32)
    sigmoid_g = jax.nn.sigmoid(gate_lin)
    activated = gate_lin * sigmoid_g
    hidden = (activated * up_lin).astype(jnp.bfloat16)
    projected = lax.dot_general(
        got_upstream, down_piece, (((1,), (1,)), ((), ())), preferred_element_type=jnp.float32
    )
    part_grad = jnp.sum(projected * hidden.astype(jnp.float32), axis=1)
    grad_hidden = gate_col[:, None] * projected
    d_gate = (grad_hidden * up_lin * sigmoid_g * (1.0 + gate_lin * (1.0 - sigmoid_g))).astype(
        jnp.bfloat16
    )
    d_up = (grad_hidden * activated).astype(jnp.bfloat16)
    piece_grad = lax.dot_general(
        d_gate, gate_piece, (((1,), (1,)), ((), ())), preferred_element_type=jnp.float32
    )
    piece_grad = piece_grad + lax.dot_general(
        d_up, up_piece, (((1,), (1,)), ((), ())), preferred_element_type=jnp.float32
    )
    return (piece_grad.astype(jnp.bfloat16), part_grad)


def per_device(tokens, routes, gates, placement, upstream, w_gate, w_up, w_down):
    tok_dev, width = tokens.shape
    top_count = routes.shape[1]
    experts = placement.shape[0]
    node_count = lax.axis_size("node")
    local_count = lax.axis_size("local")
    pieces = node_count * local_count
    slices = pieces // experts
    capacity = 5 * tok_dev * top_count // (4 * experts)
    pair_count = tok_dev * top_count
    nrows = experts * capacity
    flat_expert = routes.reshape(pair_count)
    expert_hits = (flat_expert[:, None] == jnp.arange(experts, dtype=jnp.int32)[None, :]).astype(
        jnp.int32
    )
    rank_in = jnp.sum((jnp.cumsum(expert_hits, axis=0) - expert_hits) * expert_hits, axis=1)
    slot_index = jnp.sum(expert_hits * placement[None, :], axis=1)
    row_index = slot_index * capacity + rank_in
    pair_hit = (jnp.arange(nrows, dtype=jnp.int32)[:, None] == row_index[None, :]).astype(
        jnp.float32
    )
    dispatch = jnp.sum(pair_hit.reshape(nrows, tok_dev, top_count), axis=2).astype(jnp.bfloat16)
    sent_tokens = jnp.dot(dispatch, tokens, preferred_element_type=jnp.float32).astype(jnp.bfloat16)
    sent_upstream = jnp.dot(dispatch, upstream, preferred_element_type=jnp.float32).astype(
        jnp.bfloat16
    )
    gate_rows = jnp.dot(pair_hit, gates.reshape(pair_count), precision=lax.Precision.HIGHEST)

    def spread(values):
        shaped = values.reshape((experts, 1, capacity) + values.shape[1:])
        wide = jnp.broadcast_to(shaped, (experts, slices, capacity) + values.shape[1:])
        return wide.reshape((pieces, capacity) + values.shape[1:])

    got_tokens, got_upstream, got_gates = (
        lax.all_to_all(
            spread(sent_tokens), ("node", "local"), split_axis=0, concat_axis=0, tiled=True
        ),
        lax.all_to_all(
            spread(sent_upstream), ("node", "local"), split_axis=0, concat_axis=0, tiled=True
        ),
        lax.all_to_all(
            spread(gate_rows).astype(jnp.bfloat16),
            ("node", "local"),
            split_axis=0,
            concat_axis=0,
            tiled=True,
        ).astype(jnp.float32),
    )
    work_got_tokens = got_tokens.reshape(pieces * capacity, width)
    work_got_upstream = got_upstream.reshape(pieces * capacity, width)
    work_got_gates = got_gates.reshape(pieces * capacity)
    piece_grad, part_grad = expert_piece(
        work_got_tokens, work_got_upstream, work_got_gates, w_gate[0], w_up[0], w_down[0]
    )
    back_grad, back_gate = (
        lax.all_to_all(
            piece_grad.reshape(pieces, capacity, width),
            ("node", "local"),
            split_axis=0,
            concat_axis=0,
            tiled=True,
        ),
        lax.all_to_all(
            part_grad.reshape(pieces, capacity).astype(jnp.bfloat16),
            ("node", "local"),
            split_axis=0,
            concat_axis=0,
            tiled=True,
        ).astype(jnp.float32),
    )
    expert_grad = jnp.sum(
        back_grad.reshape(experts, slices, capacity, width), axis=1, dtype=jnp.float32
    ).astype(jnp.bfloat16)
    expert_gate = jnp.sum(back_gate.reshape(experts, slices, capacity), axis=1)
    grad_tokens = lax.dot_general(
        dispatch,
        expert_grad.reshape(nrows, width),
        (((0,), (0,)), ((), ())),
        preferred_element_type=jnp.float32,
    ).astype(jnp.bfloat16)
    grad_gates = jnp.dot(
        expert_gate.reshape(nrows), pair_hit, precision=lax.Precision.HIGHEST
    ).reshape(tok_dev, top_count)
    return (grad_tokens, grad_gates)


def solution(mesh):
    return jax.shard_map(
        per_device,
        mesh=mesh,
        in_specs=(
            P(("rep", "node", "local"), None),
            P(("rep", "node", "local"), None),
            P(("rep", "node", "local"), None),
            P(),
            P(("rep", "node", "local"), None),
            P(("node", "local"), None, None),
            P(("node", "local"), None, None),
            P(("node", "local"), None, None),
        ),
        out_specs=(P(("rep", "node", "local"), None), P(("rep", "node", "local"), None)),
        check_vma=False,
    )
```

profile of v0, /device:TPU:8, one launch (start us, length us, event | category | flops | bytes accessed | tf_op | source)
XLA Modules:
  0.0 367.3 jit_solution(1662018730059421989)
XLA Ops:
  0.7 0.9 copy.22
  1.7 0.1 eq.72
  1.8 0.6 reduce-window.6
  2.4 0.2 slice_reduce_fusion
  2.7 0.8 copy.25
  3.5 0.1 reshape.173
  3.6 0.7 select_reduce_fusion
  4.3 0.4 fusion.14
  4.8 0.6 copy.26
  5.4 6.3 %all-to-all-start = ((bf16[16,1,40]{2,1,0:T(2,128)(2,1)}), bf16[16,1,40]{2,1,0:T(2,128)(2,1)S(1)}, u32[]{:S(2)}, u32[]{:S(2)}) async-start(bf16[16,1,40]{2,1,0:T(2,128)(2,1)} %copy.26), calls=%async_computation | async-start | bytes 16384 | tf_op jit(solution)/shard_map/all_to_all | solution.py:71
  12.0 0.7 convolution_convert_fusion
  12.7 4.0 %all-to-all-done = bf16[16,1,40]{2,1,0:T(2,128)(2,1)S(1)} async-done(((bf16[16,1,40]{2,1,0:T(2,128)(2,1)}), bf16[16,1,40]{2,1,0:T(2,128)(2,1)S(1)}, u32[]{:S(2)}, u32[]{:S(2)}) %all-to-all-start) | async-done | bytes 1312 | tf_op jit(solution)/shard_map/all_to_all | solution.py:71
  16.7 2.5 broadcast_in_dim.27
  19.2 5.8 %all-to-all-start.2 = ((bf16[16,40,3584]{2,1,0:T(8,128)(2,1)}), bf16[16,40,3584]{2,1,0:T(8,128)(2,1)}, u32[]{:S(2)}, u32[]{:S(2)}) async-start(bf16[16,40,3584]{2,1,0:T(8,128)(2,1)} %bitcast.52), calls=%async_computation.2 | async-start | bytes 9175040 | tf_op jit(solution)/shard_map/all_to_all | solution.py:65
  25.0 1.9 convolution_convert_fusion.1
  27.0 97.3 %all-to-all-done.2 = bf16[16,40,3584]{2,1,0:T(8,128)(2,1)} async-done(((bf16[16,40,3584]{2,1,0:T(8,128)(2,1)}), bf16[16,40,3584]{2,1,0:T(8,128)(2,1)}, u32[]{:S(2)}, u32[]{:S(2)}) %all-to-all-start.2) | async-done | bytes 4587552 | tf_op jit(solution)/shard_map/all_to_all | solution.py:65
  124.3 2.6 broadcast_in_dim.12
  126.8 6.6 %all-to-all-start.1 = ((bf16[16,40,3584]{2,1,0:T(8,128)(2,1)}), bf16[16,40,3584]{2,1,0:T(8,128)(2,1)}, u32[]{:S(2)}, u32[]{:S(2)}) async-start(bf16[16,40,3584]{2,1,0:T(8,128)(2,1)} %bitcast.51), calls=%async_computation.1 | async-start | bytes 9175040 | tf_op jit(solution)/shard_map/all_to_all | solution.py:68
  133.5 6.6 %fusion.2 = f32[640,512]{0,1:T(8,128)S(1)} fusion(bf16[640,3584]{1,0:T(8,128)(2,1)} %bitcast.12, bf16[1,3584,512]{2,1,0:T(8,128)(2,1)} %param.13), kind=kOutput, calls=%fused_computation.7 | convolution fusion | flops 2348810240 | bytes 9568256 | tf_op jit(solution)/shard_map/dot_general | solution.py:8
  140.1 6.5 %fusion.5 = f32[640,512]{0,1:T(8,128)} fusion(bf16[640,3584]{1,0:T(8,128)(2,1)} %bitcast.12, bf16[1,3584,512]{2,1,0:T(8,128)(2,1)S(1)} %copy-done.1), kind=kOutput, calls=%fused_computation.10 | convolution fusion | flops 2348810240 | bytes 9568256 | tf_op jit(solution)/shard_map/dot_general | solution.py:9
  146.7 86.0 %all-to-all-done.1 = bf16[16,40,3584]{2,1,0:T(8,128)(2,1)} async-done(((bf16[16,40,3584]{2,1,0:T(8,128)(2,1)}), bf16[16,40,3584]{2,1,0:T(8,128)(2,1)}, u32[]{:S(2)}, u32[]{:S(2)}) %all-to-all-start.1) | async-done | bytes 4587552 | tf_op jit(solution)/shard_map/all_to_all | solution.py:68
  232.6 6.8 %multiply_reduce_fusion = (bf16[640]{0:T(1024)(128)(2,1)S(1)}, f32[640,512]{0,1:T(8,128)S(1)}) fusion(f32[640,512]{0,1:T(8,128)} %fusion.5, f32[640,512]{0,1:T(8,128)S(1)} %fusion.2, bf16[640,3584]{1,0:T(8,128)(2,1)} %bitcast.8, bf16[1,512,3584]{2,1,0:T(8,128)(2,1)} %param.15), kind=kOutput, calls=%fused_computation.14 | convolution fusion | flops 2351758848 | bytes 12190976 | tf_op jit(solution)/shard_map/dot_general | solution.py:13
  239.4 0.7 convert_element_type.110
  240.1 6.7 %all-to-all-start.4 = ((bf16[16,1,40]{2,1,0:T(2,128)(2,1)}), bf16[16,1,40]{2,1,0:T(2,128)(2,1)S(1)}, u32[]{:S(2)}, u32[]{:S(2)}) async-start(bf16[16,1,40]{2,1,0:T(2,128)(2,1)} %convert_element_type.110), calls=%async_computation.4 | async-start | bytes 16384 | tf_op jit(solution)/shard_map/all_to_all | solution.py:93
  246.9 5.5 %fusion = f32[640,3584]{1,0:T(8,128)S(1)} fusion(bf16[1,3584,512]{2,1,0:T(8,128)(2,1)} %param.13, f32[640,512]{0,1:T(8,128)S(1)} %fusion.2, f32[640,512]{0,1:T(8,128)} %fusion.5, f32[640,512]{0,1:T(8,128)S(1)} %get-tuple-element.5, f32[640]{0:T(1024)S(1)} %reshape.171), kind=kOutput, calls=%fused_computation.5 | convolution fusion | flops 2352414720 | bytes 16779776 | tf_op jit(solution)/shard_map/dot_general | solution.py:22
  252.4 4.8 %add_convert_fusion = bf16[640,3584]{1,0:T(8,128)(2,1)} fusion(f32[640,3584]{1,0:T(8,128)S(1)} %fusion, bf16[1,3584,512]{2,1,0:T(8,128)(2,1)S(1)} %copy-done.2, f32[640,512]{0,1:T(8,128)S(1)} %get-tuple-element.5, f32[640]{0:T(1024)S(1)} %reshape.171, f32[640,512]{0,1:T(8,128)S(1)} %fusion.2), kind=kOutput, calls=%fused_computation | convolution fusion | flops 2355691520 | bytes 20056576 | tf_op jit(solution)/shard_map/dot_general | solution.py:25
  257.2 6.0 %all-to-all-start.3 = ((bf16[16,40,3584]{2,1,0:T(8,128)(2,1)}), bf16[16,40,3584]{2,1,0:T(8,128)(2,1)}, u32[]{:S(2)}, u32[]{:S(2)}) async-start(bf16[16,40,3584]{2,1,0:T(8,128)(2,1)} %bitcast.53), calls=%async_computation.3 | async-start | bytes 9175040 | tf_op jit(solution)/shard_map/all_to_all | solution.py:86
  263.6 0.4 fusion.13
  264.0 0.6 copy.33
  264.6 97.9 %all-to-all-done.3 = bf16[16,40,3584]{2,1,0:T(8,128)(2,1)} async-done(((bf16[16,40,3584]{2,1,0:T(8,128)(2,1)}), bf16[16,40,3584]{2,1,0:T(8,128)(2,1)}, u32[]{:S(2)}, u32[]{:S(2)}) %all-to-all-start.3) | async-done | bytes 4587552 | tf_op jit(solution)/shard_map/all_to_all | solution.py:86
  362.5 3.2 bitcast_reduce_fusion
  365.7 1.6 convolution_convert_fusion.2
  (29 shorter events, 1.0 us)
Async XLA Ops:
  0.6 11.3 %copy-start = (bf16[128,3584]{1,0:T(8,128)(2,1)S(1)}, bf16[128,3584]{1,0:T(8,128)(2,1)}, u32[]{:S(2)}) copy-start(bf16[128,3584]{1,0:T(8,128)(2,1)} %param.8) | copy-start | bytes 2752516
  5.4 11.3 %all-to-all-start = ((bf16[16,1,40]{2,1,0:T(2,128)(2,1)}), bf16[16,1,40]{2,1,0:T(2,128)(2,1)S(1)}, u32[]{:S(2)}, u32[]{:S(2)}) async-start(bf16[16,1,40]{2,1,0:T(2,128)(2,1)} %copy.26), calls=%async_computation | async-start | bytes 16384 | tf_op jit(solution)/shard_map/all_to_all | solution.py:71
  12.0 13.0 %copy-start.3 = (bf16[320,128]{1,0:T(8,128)(2,1)}, bf16[320,128]{1,0:T(8,128)(2,1)S(1)}, u32[]{:S(2)}) copy-start(bf16[320,128]{1,0:T(8,128)(2,1)S(1)} %convert_reduce_fusion) | copy-start | bytes 245764
  19.2 105.1 %all-to-all-start.2 = ((bf16[16,40,3584]{2,1,0:T(8,128)(2,1)}), bf16[16,40,3584]{2,1,0:T(8,128)(2,1)}, u32[]{:S(2)}, u32[]{:S(2)}) async-start(bf16[16,40,3584]{2,1,0:T(8,128)(2,1)} %bitcast.52), calls=%async_computation.2 | async-start | bytes 9175040 | tf_op jit(solution)/shard_map/all_to_all | solution.py:65
  126.8 105.8 %all-to-all-start.1 = ((bf16[16,40,3584]{2,1,0:T(8,128)(2,1)}), bf16[16,40,3584]{2,1,0:T(8,128)(2,1)}, u32[]{:S(2)}, u32[]{:S(2)}) async-start(bf16[16,40,3584]{2,1,0:T(8,128)(2,1)} %bitcast.51), calls=%async_computation.1 | async-start | bytes 9175040 | tf_op jit(solution)/shard_map/all_to_all | solution.py:68
  133.5 6.6 %copy-start.1 = (bf16[1,3584,512]{2,1,0:T(8,128)(2,1)S(1)}, bf16[1,3584,512]{2,1,0:T(8,128)(2,1)}, u32[]{:S(2)}) copy-start(bf16[1,3584,512]{2,1,0:T(8,128)(2,1)} %param.14) | copy-start | bytes 11010052
  240.1 17.1 %all-to-all-start.4 = ((bf16[16,1,40]{2,1,0:T(2,128)(2,1)}), bf16[16,1,40]{2,1,0:T(2,128)(2,1)S(1)}, u32[]{:S(2)}, u32[]{:S(2)}) async-start(bf16[16,1,40]{2,1,0:T(2,128)(2,1)} %convert_element_type.110), calls=%async_computation.4 | async-start | bytes 16384 | tf_op jit(solution)/shard_map/all_to_all | solution.py:93
  246.9 5.5 %copy-start.2 = (bf16[1,3584,512]{2,1,0:T(8,128)(2,1)S(1)}, bf16[1,3584,512]{2,1,0:T(8,128)(2,1)}, u32[]{:S(2)}) copy-start(bf16[1,3584,512]{2,1,0:T(8,128)(2,1)} %param.14) | copy-start | bytes 11010052
  257.2 105.3 %all-to-all-start.3 = ((bf16[16,40,3584]{2,1,0:T(8,128)(2,1)}), bf16[16,40,3584]{2,1,0:T(8,128)(2,1)}, u32[]{:S(2)}, u32[]{:S(2)}) async-start(bf16[16,40,3584]{2,1,0:T(8,128)(2,1)} %bitcast.53), calls=%async_computation.3 | async-start | bytes 9175040 | tf_op jit(solution)/shard_map/all_to_all | solution.py:86
  264.6 101.1 %copy-start.4 = (bf16[320,128]{1,0:T(8,128)(2,1)S(1)}, bf16[320,128]{1,0:T(8,128)(2,1)}, u32[]{:S(2)}) copy-start(bf16[320,128]{1,0:T(8,128)(2,1)} %copy-done.3) | copy-start | bytes 245764
where the time goes:
time: 370 us; the launch traced here: 367 us
  waiting for transfers between devices  285 us (77%)
  matrix products  34.9 us (9%)
  starting transfers between devices  31.4 us (8%)
  local copies, waits for them, and re-layouts  9.82 us (3%)
  other arithmetic  5.23 us (1%)
    all_to_all x1, waiting for transfers between devices, per_device(): lax.all_to_all(piece_grad.reshape(pieces, capacity, width), ('node', 'loc...  97.9 us
    all_to_all x1, waiting for transfers between devices, per_device(): lax.all_to_all(spread(sent_tokens), ('node', 'local'), split_axis=0, conc...  97.3 us
    all_to_all x1, waiting for transfers between devices, per_device(): lax.all_to_all(spread(sent_upstream), ('node', 'local'), split_axis=0, co...  86 us
  transfers between devices with their start and end apart: 5, of which 4 were waited for; matrix products, arithmetic and copies ran while one was open for 8% of the time, Pallas kernels for 0%

commit v1 on v0

v1 whole, which is shorter than its diff:
```python
import jax
import jax.numpy as jnp
from jax import lax
from jax.sharding import Mesh
from jax.sharding import PartitionSpec as P

BF16 = jnp.bfloat16
F32 = jnp.float32
CHIPS = ("node", "chip")
ROWS = ("rep", "node", "chip", "core")
PIECES = ("node", "chip", "core")


def nt(left, right):
    return lax.dot_general(left, right, (((1,), (1,)), ((), ())), preferred_element_type=F32)


def nn(left, right):
    return jnp.dot(left, right, preferred_element_type=F32)


def forward_lins(rows, gate_piece, up_piece):
    return nn(rows, gate_piece), nn(rows, up_piece)


def backward_lins(gate_lin, up_lin, projected):
    sigmoid_g = jax.nn.sigmoid(gate_lin)
    activated = gate_lin * sigmoid_g
    hidden = (activated * up_lin).astype(BF16).astype(F32)
    part_grad = jnp.sum(projected * hidden, axis=1)
    d_gate = (projected * up_lin * sigmoid_g * (1.0 + gate_lin * (1.0 - sigmoid_g))).astype(BF16)
    d_up = (projected * activated).astype(BF16)
    return d_gate, d_up, part_grad


def swap_cores(values):
    return lax.ppermute(values, "core", [(0, 1), (1, 0)])


def to_chips(values):
    return lax.all_to_all(values, CHIPS, split_axis=0, concat_axis=0, tiled=True)


def per_device(tokens, routes, gates, placement, upstream, w_gate, w_up, w_down):
    tok_dev, width = tokens.shape
    top_count = routes.shape[1]
    experts = placement.shape[0]
    capacity = 5 * tok_dev * top_count // (4 * experts)
    nrows = experts * capacity
    hit = (routes[:, :, None] == jnp.arange(experts, dtype=jnp.int32)).astype(jnp.int32)
    named = jnp.sum(hit, axis=1)
    before = jnp.cumsum(named, axis=0) - named
    rank = jnp.sum(hit * before[:, None, :], axis=2)
    slot = jnp.sum(hit * placement, axis=2)
    row_index = slot * capacity + rank
    rows = jnp.arange(nrows, dtype=jnp.int32)
    pair_hit = rows[:, None, None] == row_index.T[None]
    dispatch = jnp.any(pair_hit, axis=1).astype(BF16)

    sent_tokens = nn(dispatch, tokens).astype(BF16).reshape(experts, capacity, width)
    sent_upstream = nn(dispatch, upstream).astype(BF16).reshape(experts, capacity, width)
    own_tokens = to_chips(sent_tokens).reshape(nrows, width)
    own_upstream = to_chips(sent_upstream).reshape(nrows, width)
    other_tokens = swap_cores(own_tokens)
    other_upstream = swap_cores(own_upstream)

    gate_piece, up_piece, down_piece = w_gate[0], w_up[0], w_down[0]

    def piece(got_tokens, got_upstream):
        gate_lin, up_lin = forward_lins(got_tokens, gate_piece, up_piece)
        d_gate, d_up, part = backward_lins(gate_lin, up_lin, nt(got_upstream, down_piece))
        return (nt(d_gate, gate_piece) + nt(d_up, up_piece)).astype(BF16), part

    other_grad, other_part = piece(other_tokens, other_upstream)
    own_grad, own_part = piece(own_tokens, own_upstream)
    expert_grad = (own_grad.astype(F32) + swap_cores(other_grad).astype(F32)).astype(BF16)
    part_sum = own_part + swap_cores(other_part)

    back_grad = to_chips(expert_grad.reshape(experts, capacity, width)).reshape(nrows, width)
    parts = lax.all_gather(part_sum.reshape(experts, capacity), CHIPS, axis=0, tiled=False)
    chip = lax.axis_index("node") * lax.axis_size("chip") + lax.axis_index("chip")
    back_part = lax.dynamic_index_in_dim(parts, chip, axis=1, keepdims=False).reshape(nrows)

    grad_gates = jnp.sum(jnp.where(pair_hit, back_part[:, None, None], 0.0), axis=0).T
    combine = jnp.sum(jnp.where(pair_hit, gates.T[None], 0.0), axis=1)
    weighted = combine.T
    high = weighted.astype(BF16)
    low = (weighted - high.astype(F32)).astype(BF16)
    grad_tokens = (nn(high, back_grad) + nn(low, back_grad)).astype(BF16)
    return grad_tokens, grad_gates


def solution(mesh):
    shape = mesh.devices.shape
    split = Mesh(
        mesh.devices.reshape(shape[0], shape[1], shape[2] // 2, 2), ("rep", "node", "chip", "core")
    )
    return jax.shard_map(
        per_device,
        mesh=split,
        in_specs=(
            P(ROWS, None),
            P(ROWS, None),
            P(ROWS, None),
            P(),
            P(ROWS, None),
            P(PIECES, None, None),
            P(PIECES, None, None),
            P(PIECES, None, None),
        ),
        out_specs=(P(ROWS, None), P(ROWS, None)),
        check_vma=False,
    )
```

time: 370 us -> 224 us (0.61)
  the two profiles are of different devices: /device:TPU:8 before, /device:TPU:0 now
where the time goes in v1:
time: 224 us
  waiting for transfers between devices  102 us (46%)
  blocking collectives  71.4 us (32%)
  matrix products  29.7 us (13%)
  starting transfers between devices  16.1 us (7%)
  other arithmetic  2.49 us (1%)
    all_to_all x3, waiting for transfers between devices, to_chips(): lax.all_to_all(values, CHIPS, split_axis=0, concat_axis=0, tiled=True)  101 us
    all_gather x1, blocking collectives, per_device(): lax.all_gather(part_sum.reshape(experts, capacity), CHIPS, axis=0, tiled=...  71.4 us
    dot_general x8, matrix products, nn(): return jnp.dot(left, right, preferred_element_type=F32)  17.7 us
    all_to_all x3, starting transfers between devices, to_chips(): lax.all_to_all(values, CHIPS, split_axis=0, concat_axis=0, tiled=True)  15.6 us
    dot_general x6, matrix products, nt(): lax.dot_general(left, right, (((1,), (1,)), ((), ())), preferred_element_...  12 us
  transfers between devices with their start and end apart: 7, of which 3 were waited for; matrix products, arithmetic and copies ran while one was open for 8% of the time, Pallas kernels for 0%

profile of v1, /device:TPU:0, one launch (start us, length us, event | category | flops | bytes accessed | tf_op | source)
XLA Modules:
  0.0 223.6 jit_solution(2244937223298718900)
XLA Ops:
  0.6 0.0 copy-start
  0.6 0.8 convert_reduce_fusion
  1.4 0.1 copy.12
  1.5 0.2 reduce_window_sum.11
  1.7 0.8 select_reduce_fusion.3
  2.6 2.1 convolution_convert_fusion
  4.7 7.3 %all-to-all-start.1 = ((bf16[8,40,3584]{2,1,0:T(8,128)(2,1)}), bf16[8,40,3584]{2,1,0:T(8,128)(2,1)S(1)}, u32[]{:S(2)}, u32[]{:S(2)}) async-start(bf16[8,40,3584]{2,1,0:T(8,128)(2,1)} %bitcast.6), calls=%async_computation.1 | async-start | bytes 4587520 | tf_op jit(solution)/shard_map/all_to_all | solution.py:41
  12.0 3.3 %convolution_convert_fusion.1 = bf16[320,3584]{1,0:T(8,128)(2,1)} fusion(pred[320,128]{1,0:T(8,128)(4,1)S(1)} %fusion.28, bf16[128,3584]{1,0:T(8,128)(2,1)} %param.12), kind=kOutput, calls=%fused_computation.6 | convolution fusion | flops 294748160 | bytes 3252224 | tf_op jit(solution)/shard_map/dot_general | solution.py:19
  15.3 49.2 %all-to-all-done.1 = bf16[8,40,3584]{2,1,0:T(8,128)(2,1)S(1)} async-done(((bf16[8,40,3584]{2,1,0:T(8,128)(2,1)}), bf16[8,40,3584]{2,1,0:T(8,128)(2,1)S(1)}, u32[]{:S(2)}, u32[]{:S(2)}) %all-to-all-start.1) | async-done | bytes 2293792 | tf_op jit(solution)/shard_map/all_to_all | solution.py:41
  64.4 4.4 %all-to-all-start = ((bf16[8,40,3584]{2,1,0:T(8,128)(2,1)}), bf16[8,40,3584]{2,1,0:T(8,128)(2,1)}, u32[]{:S(2)}, u32[]{:S(2)}) async-start(bf16[8,40,3584]{2,1,0:T(8,128)(2,1)} %bitcast.3), calls=%async_computation | async-start | bytes 4587520 | tf_op jit(solution)/shard_map/all_to_all | solution.py:41
  68.8 0.1 collective-permute-start.1
  68.9 51.9 %all-to-all-done = bf16[8,40,3584]{2,1,0:T(8,128)(2,1)} async-done(((bf16[8,40,3584]{2,1,0:T(8,128)(2,1)}), bf16[8,40,3584]{2,1,0:T(8,128)(2,1)}, u32[]{:S(2)}, u32[]{:S(2)}) %all-to-all-start) | async-done | bytes 2293792 | tf_op jit(solution)/shard_map/all_to_all | solution.py:41
  120.8 4.2 %fusion.6 = f32[320,512]{1,0:T(8,128)S(1)} fusion(bf16[320,3584]{1,0:T(8,128)(2,1)} %collective-permute-done.1, bf16[1,3584,512]{2,1,0:T(8,128)(2,1)} %param.13), kind=kOutput, calls=%fused_computation.12 | convolution fusion | flops 1174405120 | bytes 6619136 | tf_op jit(solution)/shard_map/dot_general | solution.py:19
  125.1 3.1 %fusion.13 = f32[320,512]{1,0:T(8,128)S(1)} fusion(bf16[320,3584]{1,0:T(8,128)(2,1)} %collective-permute-done.1, bf16[1,3584,512]{2,1,0:T(8,128)(2,1)S(1)} %copy-done.2), kind=kOutput, calls=%fused_computation.19 | convolution fusion | flops 1174405120 | bytes 6619136 | tf_op jit(solution)/shard_map/dot_general | solution.py:19
  128.3 1.5 multiply_reduce_fusion
  129.8 0.5 copy-done.1
  130.3 1.5 fusion.4
  131.8 1.4 fusion.2
  133.2 0.4 collective-permute-start.2
  133.6 1.3 fusion.10
  135.0 1.3 fusion.16
  136.3 3.2 %multiply_reduce_fusion.1 = (f32[320]{0:T(512)S(1)}, f32[320,512]{1,0:T(8,128)S(1)}) fusion(f32[320,512]{1,0:T(8,128)S(1)} %fusion.16, f32[320,512]{1,0:T(8,128)S(1)} %fusion.10, bf16[320,3584]{1,0:T(8,128)(2,1)} %bitcast.4, bf16[1,512,3584]{2,1,0:T(8,128)(2,1)S(1)} %copy-done.4), kind=kOutput, calls=%fused_computation.30 | convolution fusion | flops 1175879424 | bytes 7931136 | tf_op jit(solution)/shard_map/dot_general | solution.py:15
  139.5 1.5 fusion.8
  141.0 2.8 %add_convert_fusion = bf16[320,3584]{1,0:T(8,128)(2,1)} fusion(bf16[320,3584]{1,0:T(8,128)(2,1)S(1)} %collective-permute-done.2, f32[320,3584]{1,0:T(8,128)S(1)} %fusion.8, bf16[1,3584,512]{2,1,0:T(8,128)(2,1)S(1)} %copy-done.2, f32[320,512]{1,0:T(8,128)S(1)} %get-tuple-element.7, f32[320,512]{1,0:T(8,128)S(1)} %fusion.10), kind=kOutput, calls=%fused_computation.9 | convolution fusion | flops 1182269440 | bytes 14155776 | tf_op jit(solution)/shard_map/dot_general | solution.py:15
  143.9 4.0 %all-to-all-start.2 = ((bf16[8,40,3584]{2,1,0:T(8,128)(2,1)}), bf16[8,40,3584]{2,1,0:T(8,128)(2,1)S(1)}, u32[]{:S(2)}, u32[]{:S(2)}) async-start(bf16[8,40,3584]{2,1,0:T(8,128)(2,1)} %bitcast.72), calls=%async_computation.2 | async-start | bytes 4587520 | tf_op jit(solution)/shard_map/all_to_all | solution.py:41
  147.9 1.1 collective-permute-done.3
  149.0 0.1 all_gather_reshape.3
  149.1 71.4 %all_gather.3 = f32[8,8,40]{2,1,0:T(8,128)S(1)} all-gather(f32[1,8,40]{2,1,0:T(8,128)S(1)} %all_gather_reshape.3), channel_id=1, replica_groups=mesh['rep'=2,'node'=4,'chip'=2,'core'=2] {'node','chip'}, dimensions={0}, use_global_device_ids=true | all-gather | bytes 11520 | tf_op jit(solution)/shard_map/all_gather | solution.py:80
  220.5 0.1 broadcast_in_dim.33
  220.6 0.7 select_reduce_fusion
  221.3 0.7 fusion.39
  222.0 1.6 fusion.3
  (20 shorter events, 0.2 us)
Async XLA Ops:
  0.6 2.0 copy-start
  4.7 59.7 %all-to-all-start.1 = ((bf16[8,40,3584]{2,1,0:T(8,128)(2,1)}), bf16[8,40,3584]{2,1,0:T(8,128)(2,1)S(1)}, u32[]{:S(2)}, u32[]{:S(2)}) async-start(bf16[8,40,3584]{2,1,0:T(8,128)(2,1)} %bitcast.6), calls=%async_computation.1 | async-start | bytes 4587520 | tf_op jit(solution)/shard_map/all_to_all | solution.py:41
  64.4 56.4 %all-to-all-start = ((bf16[8,40,3584]{2,1,0:T(8,128)(2,1)}), bf16[8,40,3584]{2,1,0:T(8,128)(2,1)}, u32[]{:S(2)}, u32[]{:S(2)}) async-start(bf16[8,40,3584]{2,1,0:T(8,128)(2,1)} %bitcast.3), calls=%async_computation | async-start | bytes 4587520 | tf_op jit(solution)/shard_map/all_to_all | solution.py:41
  68.8 52.0 %collective-permute-start.1 = (bf16[320,3584]{1,0:T(8,128)(2,1)S(1)}, bf16[320,3584]{1,0:T(8,128)(2,1)}, u32[]{:S(2)}, u32[]{:S(2)}) collective-permute-start(bf16[320,3584]{1,0:T(8,128)(2,1)S(1)} %bitcast.73), channel_id=1, source_target_pairs={{0,1},{1,0},{2,3},{3,2},{4,5},{5,4},{6,7},{7,6},{8,9},{9,8},{10,11... | collective-permute-start | bytes 6881288 | tf_op jit(solution)/shard_map/ppermute | solution.py:37
  120.8 4.2 %copy-start.2 = (bf16[1,3584,512]{2,1,0:T(8,128)(2,1)S(1)}, bf16[1,3584,512]{2,1,0:T(8,128)(2,1)}, u32[]{:S(2)}) copy-start(bf16[1,3584,512]{2,1,0:T(8,128)(2,1)} %param.14) | copy-start | bytes 11010052
  120.8 7.4 %collective-permute-start = (bf16[320,3584]{1,0:T(8,128)(2,1)}, bf16[320,3584]{1,0:T(8,128)(2,1)S(1)}, u32[]{:S(2)}, u32[]{:S(2)}) collective-permute-start(bf16[320,3584]{1,0:T(8,128)(2,1)} %bitcast.4), channel_id=1, source_target_pairs={{0,1},{1,0},{2,3},{3,2},{4,5},{5,4},{6,7},{7,6},{8,9},{9,8},{10,11... | collective-permute-start | bytes 6881288 | tf_op jit(solution)/shard_map/ppermute | solution.py:37
  125.1 3.2 %copy-start.4 = (bf16[1,512,3584]{2,1,0:T(8,128)(2,1)S(1)}, bf16[1,512,3584]{2,1,0:T(8,128)(2,1)}, u32[]{:S(2)}) copy-start(bf16[1,512,3584]{2,1,0:T(8,128)(2,1)} %param.15) | copy-start | bytes 11010052
  128.2 2.0 copy-start.1
  133.2 7.8 %collective-permute-start.2 = (bf16[320,3584]{1,0:T(8,128)(2,1)S(1)}, bf16[320,3584]{1,0:T(8,128)(2,1)S(1)}, u32[]{:S(2)}, u32[]{:S(2)}) collective-permute-start(bf16[320,3584]{1,0:T(8,128)(2,1)S(1)} %fusion.2), channel_id=1, source_target_pairs={{0,1},{1,0},{2,3},{3,2},{4,5},{5,4},{6,7},{7,6},{8,9},{9,8},{10,11... | collective-permute-start | bytes 6881288 | tf_op jit(solution)/shard_map/ppermute | solution.py:37
  143.9 76.7 %copy-start.3 = (f32[128,2]{0,1:T(2,128)S(1)}, f32[128,2]{0,1:T(2,128)}, u32[]{:S(2)}) copy-start(f32[128,2]{0,1:T(2,128)} %param.10) | copy-start | bytes 3076
  143.9 77.4 %all-to-all-start.2 = ((bf16[8,40,3584]{2,1,0:T(8,128)(2,1)}), bf16[8,40,3584]{2,1,0:T(8,128)(2,1)S(1)}, u32[]{:S(2)}, u32[]{:S(2)}) async-start(bf16[8,40,3584]{2,1,0:T(8,128)(2,1)} %bitcast.72), calls=%async_computation.2 | async-start | bytes 4587520 | tf_op jit(solution)/shard_map/all_to_all | solution.py:41
  147.9 1.2 collective-permute-start.3

commit v2 on v1

v2 whole, which is shorter than its diff:
```python
import functools

import jax
import jax.numpy as jnp
from jax import lax
from jax.experimental import pallas as pl
from jax.experimental.pallas import tpu as pltpu
from jax.sharding import Mesh
from jax.sharding import PartitionSpec as P

BF16 = jnp.bfloat16
F32 = jnp.float32
CHIPS = ("node", "chip")
ROWS = ("rep", "node", "chip", "core")
PIECES = ("node", "chip", "core")
LANES = 128
VMEM = pl.BlockSpec(memory_space=pltpu.VMEM)
SMALL = pl.CostEstimate(flops=1, bytes_accessed=1, transcendentals=0)


def nt(left, right):
    return lax.dot_general(left, right, (((1,), (1,)), ((), ())), preferred_element_type=F32)


def nn(left, right):
    return jnp.dot(left, right, preferred_element_type=F32)


def swap_cores(values):
    return lax.ppermute(values, "core", [(0, 1), (1, 0)])


def dispatch_kernel(offsets, capacity, index_ref, tokens_ref, upstream_ref, *out_refs):
    count = tokens_ref.shape[0]
    for offset, out_ref in zip(offsets, out_refs):
        rows = lax.broadcasted_iota(jnp.int32, (capacity, count), 0) + offset * capacity
        hits = jnp.zeros((capacity, count), F32)
        for choice in range(index_ref.shape[0]):
            hits = hits + jnp.where(rows == index_ref[choice : choice + 1, :], 1.0, 0.0)
        hits = hits.astype(BF16)
        out_ref[0] = nn(hits, tokens_ref[...]).astype(BF16)
        out_ref[1] = nn(hits, upstream_ref[...]).astype(BF16)


def dispatch(row_index, tokens, upstream, offsets, capacity):
    width = tokens.shape[1]
    return pl.pallas_call(
        functools.partial(dispatch_kernel, offsets, capacity),
        out_shape=[jax.ShapeDtypeStruct((2, capacity, width), BF16)] * len(offsets),
        in_specs=[VMEM] * 3,
        out_specs=[VMEM] * len(offsets),
        compiler_params=pltpu.CompilerParams(vmem_limit_bytes=48 << 20),
        cost_estimate=SMALL,
        name="dispatch",
    )(row_index, tokens, upstream)


def expert_kernel(tiles, tokens_ref, upstream_ref, *refs):
    own_refs, other_refs, (out_ref, total, part) = refs[:3], refs[3:6], refs[6:]
    step = pl.program_id(0)
    width = tokens_ref.shape[1]

    @pl.when(step == 0)
    def _():
        total[...] = jnp.zeros_like(total)
        part[...] = jnp.zeros_like(part)

    def tile(gate_ref, up_ref, down_ref):
        tokens = tokens_ref[...]
        gate_piece, up_piece = gate_ref[0], up_ref[0]
        gate_lin = nn(tokens, gate_piece)
        up_lin = nn(tokens, up_piece)
        projected = nt(upstream_ref[...], down_ref[0])
        sigmoid_g = jax.nn.sigmoid(gate_lin)
        activated = gate_lin * sigmoid_g
        hidden = (activated * up_lin).astype(BF16).astype(F32)
        part[...] += jnp.sum(projected * hidden, axis=1, keepdims=True)
        slope = sigmoid_g * (1.0 + gate_lin * (1.0 - sigmoid_g))
        d_gate = (projected * up_lin * slope).astype(BF16)
        d_up = (projected * activated).astype(BF16)
        total[...] += nt(d_gate, gate_piece) + nt(d_up, up_piece)

    pl.when(step < tiles)(lambda: tile(*own_refs))
    pl.when(step >= tiles)(lambda: tile(*other_refs))

    @pl.when(step == pl.num_programs(0) - 1)
    def _():
        out_ref[:, :width] = total[...].astype(BF16)
        out_ref[:, width:] = jnp.broadcast_to(part[...], (part.shape[0], LANES)).astype(BF16)


def expert(tokens, upstream, own, other):
    rows, width = tokens.shape
    hidden = own[0].shape[2]
    tile = min(256, hidden)
    tiles = hidden // tile

    def weights(place):
        return [
            pl.BlockSpec((1, width, tile), lambda h: (0, 0, place(h))),
            pl.BlockSpec((1, width, tile), lambda h: (0, 0, place(h))),
            pl.BlockSpec((1, tile, width), lambda h: (0, place(h), 0)),
        ]

    return pl.pallas_call(
        functools.partial(expert_kernel, tiles),
        out_shape=jax.ShapeDtypeStruct((rows, width + LANES), BF16),
        grid=(2 * tiles,),
        in_specs=[pl.BlockSpec((rows, width), lambda h: (0, 0))] * 2
        + weights(lambda h: jnp.minimum(h, tiles - 1))
        + weights(lambda h: jnp.maximum(h - tiles, 0)),
        out_specs=pl.BlockSpec((rows, width + LANES), lambda h: (0, 0)),
        scratch_shapes=[pltpu.VMEM((rows, width), F32), pltpu.VMEM((rows, 1), F32)],
        compiler_params=pltpu.CompilerParams(vmem_limit_bytes=56 << 20),
        cost_estimate=SMALL,
        name="expert",
    )(tokens, upstream, *own, *other)


def per_device(tokens, routes, gates, placement, upstream, w_gate, w_up, w_down):
    tok_dev, width = tokens.shape
    top_count = routes.shape[1]
    experts = placement.shape[0]
    nodes, node_chips = lax.axis_size("node"), lax.axis_size("chip")
    chips = nodes * node_chips
    assert chips == experts and chips & (chips - 1) == 0 and nodes % 4 == 0
    capacity = 5 * tok_dev * top_count // (4 * experts)
    me = lax.axis_index("node") * node_chips + lax.axis_index("chip")

    hit = (routes[:, :, None] == jnp.arange(experts, dtype=jnp.int32)).astype(jnp.int32)
    named = jnp.sum(hit, axis=1)
    before = jnp.cumsum(named, axis=0) - named
    rank = jnp.sum(hit * before[:, None, :], axis=2)
    slot = jnp.sum(hit * placement, axis=2)
    row_index = ((slot ^ me) * capacity + rank).T

    def move(sent, offsets):
        return [
            lax.ppermute(rows, CHIPS, [(i, i ^ offset) for i in range(chips)]) if offset else rows
            for rows, offset in zip(sent, offsets)
        ]

    def work(got, weights):
        both = jnp.stack(got, axis=1).reshape(2, len(got) * capacity, width)
        out = expert(both[0], both[1], *weights)
        return [out[i * capacity : (i + 1) * capacity] for i in range(len(got))]

    def combine(back, offsets):
        rows = jnp.arange(capacity, dtype=jnp.int32)
        hits = jnp.concatenate(
            [(rows + o * capacity)[:, None, None] == row_index[None] for o in offsets]
        )
        weighted = jnp.sum(jnp.where(hits, gates.T[None], 0.0), axis=1).T
        high = weighted.astype(BF16)
        low = (weighted - high.astype(F32)).astype(BF16)
        rows = jnp.concatenate(back)
        part = rows[:, width].astype(F32)
        rows = rows[:, :width]
        return nn(high, rows) + nn(low, rows), jnp.sum(
            jnp.where(hits, part[:, None, None], 0.0), axis=0
        ).T

    near1 = list(range(3 * chips // 8))
    near2 = list(range(3 * chips // 8, chips // 2))
    far1 = list(range(chips // 2, 3 * chips // 4))
    far2 = list(range(3 * chips // 4, chips))
    half = len(far1) // 2
    tie = lax.optimization_barrier

    s_far1 = dispatch(row_index, tokens, upstream, far1, capacity)
    row_index_later, s_far1 = tie((row_index, s_far1))
    s_rest = dispatch(row_index_later, tokens, upstream, far2 + near1 + near2, capacity)
    s_far2, s_near1 = s_rest[: len(far2)], s_rest[len(far2) : len(far2) + len(near1)]
    s_near2 = s_rest[len(far2) + len(near1) :]
    own = (w_gate, w_up, w_down)
    d_far1 = move(s_far1, far1)
    other = tuple(swap_cores(piece) for piece in own)
    s_near1, other = tie((s_near1, other))
    d_near1 = move(s_near1, near1)

    d_far1, d_near1, s_far2, s_near2 = tie((d_far1, d_near1, s_far2, s_near2))
    d_far2 = move(s_far2, far2)
    d_near2 = move(s_near2, near2)
    first = work(d_far1 + d_near1, (own, other))
    b_near1 = move(first[len(far1) :], near1)
    d_far2, d_near2, first, b_near1 = tie((d_far2, d_near2, first, b_near1))

    b_far1 = move(first[: len(far1)], far1)
    second = work(d_far2 + d_near2, (own, other))
    b_far1, second = tie((b_far1, second))

    second = move(second, far2 + near2)
    early, gate_early = combine(b_far1 + b_near1, far1 + near1)
    late, gate_late = combine(second, far2 + near2)
    return (early + late).astype(BF16), gate_early + gate_late


def solution(mesh):
    shape = mesh.devices.shape
    split = Mesh(
        mesh.devices.reshape(shape[0], shape[1], shape[2] // 2, 2), ("rep", "node", "chip", "core")
    )
    return jax.shard_map(
        per_device,
        mesh=split,
        in_specs=(
            P(ROWS, None),
            P(ROWS, None),
            P(ROWS, None),
            P(),
            P(ROWS, None),
            P(PIECES, None, None),
            P(PIECES, None, None),
            P(PIECES, None, None),
        ),
        out_specs=(P(ROWS, None), P(ROWS, None)),
        check_vma=False,
    )
```

time: 224 us -> 183 us (0.82)
  the two profiles are of different devices: /device:TPU:0 before, /device:TPU:8 now
where the time goes in v2:
time: 183 us; the launch traced here: 182 us
  waiting for transfers between devices  98.9 us (54%)
  Pallas kernels  42.9 us (23%)
  starting transfers between devices  25.1 us (14%)
  local copies, waits for them, and re-layouts  8.64 us (5%)
  other arithmetic  3.23 us (2%)
  matrix products  2.73 us (1%)
    ppermute x14, waiting for transfers between devices, move(): lax.ppermute(rows, CHIPS, [(i, i ^ offset) for i in range(chips)])  92.7 us
    pallas_call x2, Pallas kernels, expert(): pl.pallas_call(functools.partial(expert_kernel, tiles), out_shape=jax.Sha...  40.7 us
    ppermute x14, starting transfers between devices, move(): lax.ppermute(rows, CHIPS, [(i, i ^ offset) for i in range(chips)])  24.4 us
    ppermute x3, waiting for transfers between devices, swap_cores(): return lax.ppermute(values, 'core', [(0, 1), (1, 0)])  6.24 us
  transfers between devices with their start and end apart: 17, of which 8 were waited for; matrix products, arithmetic and copies ran while one was open for 3% of the time, Pallas kernels for 24%

profile of v2, /device:TPU:8, one launch (start us, length us, event | category | flops | bytes accessed | tf_op | source)
XLA Modules:
  0.0 182.4 jit_solution(2786775627520146027)
XLA Ops:
  0.7 0.5 collective-permute-start.3
  1.3 0.7 convert_reduce_fusion.2
  2.3 0.8 select_reduce_fusion.5
  3.1 1.2 copy-done
  4.3 1.2 copy-done.1
  5.5 0.6 dispatch.2
  6.1 2.6 %collective-permute-start = (bf16[2,40,3584]{2,1,0:T(8,128)(2,1)S(1)}, bf16[2,40,3584]{2,1,0:T(8,128)(2,1)S(1)}, u32[]{:S(2)}, u32[]{:S(2)}) collective-permute-start(bf16[2,40,3584]{2,1,0:T(8,128)(2,1)S(1)} %get-tuple-element.42), channel_id=1, source_target_pairs={{0,8},{2,10},{4,12},{6,14},{8,0},{10,2},{12,4},{14,6},{1,9},{3,11}... | collective-permute-start | bytes 1720328 | tf_op jit(solution)/shard_map/ppermute | solution.py:139
  8.7 1.3 collective-permute-start.1
  10.0 1.6 dispatch.3
  11.7 1.0 collective-permute-done.3.refs_4_
  12.7 5.2 %collective-permute-done.4.refs_5_ = bf16[1,512,3584]{2,1,0:T(8,128)(2,1)} collective-permute-done((bf16[1,512,3584]{2,1,0:T(8,128)(2,1)}, bf16[1,512,3584]{2,1,0:T(8,128)(2,1)}, u32[]{:S(2)}, u32[]{:S(2)}) %collective-permute-start.4) | collective-permute-done | bytes 3670048 | tf_op jit(solution)/shard_map/ppermute | solution.py:30
  17.9 1.5 collective-permute-start.5
  20.1 26.0 %collective-permute-done = bf16[2,40,3584]{2,1,0:T(8,128)(2,1)S(1)} collective-permute-done((bf16[2,40,3584]{2,1,0:T(8,128)(2,1)S(1)}, bf16[2,40,3584]{2,1,0:T(8,128)(2,1)S(1)}, u32[]{:S(2)}, u32[]{:S(2)}) %collective-permute-start) | collective-permute-done | bytes 573472 | tf_op jit(solution)/shard_map/ppermute | solution.py:139
  46.1 12.3 %collective-permute-done.1 = bf16[2,40,3584]{2,1,0:T(8,128)(2,1)S(1)} collective-permute-done((bf16[2,40,3584]{2,1,0:T(8,128)(2,1)S(1)}, bf16[2,40,3584]{2,1,0:T(8,128)(2,1)S(1)}, u32[]{:S(2)}, u32[]{:S(2)}) %collective-permute-start.1) | collective-permute-done | bytes 573472 | tf_op jit(solution)/shard_map/ppermute | solution.py:139
  58.6 1.8 fusion.15
  60.4 3.0 %collective-permute-start.8 = (bf16[2,40,3584]{2,1,0:T(8,128)(2,1)S(1)}, bf16[2,40,3584]{2,1,0:T(8,128)(2,1)S(1)}, u32[]{:S(2)}, u32[]{:S(2)}) collective-permute-start(bf16[2,40,3584]{2,1,0:T(8,128)(2,1)S(1)} %get-tuple-element.55), channel_id=1, source_target_pairs={{0,14},{2,12},{4,10},{6,8},{8,6},{10,4},{12,2},{14,0},{1,15},{3,13... | collective-permute-start | bytes 1720328 | tf_op jit(solution)/shard_map/ppermute | solution.py:139
  63.3 4.0 %collective-permute-start.9 = (bf16[2,40,3584]{2,1,0:T(8,128)(2,1)S(1)}, bf16[2,40,3584]{2,1,0:T(8,128)(2,1)S(1)}, u32[]{:S(2)}, u32[]{:S(2)}) collective-permute-start(bf16[2,40,3584]{2,1,0:T(8,128)(2,1)S(1)} %get-tuple-element.56), channel_id=1, source_target_pairs={{0,6},{2,4},{4,2},{6,0},{8,14},{10,12},{12,10},{14,8},{1,7},{3,5},... | collective-permute-start | bytes 1720328 | tf_op jit(solution)/shard_map/ppermute | solution.py:139
  67.4 21.2 %expert.2 = bf16[200,3712]{1,0:T(8,128)(2,1)} custom-call(bf16[200,3584]{1,0:T(8,128)(2,1)} %bitcast.61, bf16[200,3584]{1,0:T(8,128)(2,1)} %bitcast.60, bf16[1,3584,512]{2,1,0:T(8,128)(2,1)} %refs_0_.3, bf16[1,3584,512]{2,1,0:T(8,128)(2,1)} %refs_1_.3, bf16[1,512,3584]{2,1,0:T(8,128)(2,1)} %refs_2_.3, bf16[1,3584,512]{2,1,0:T(8,128)(2,1)} %collective-permute-done.2.refs_3_, ...), custom_call_target="tpu_custom_call" | custom-call | flops 1 | bytes 1 | tf_op jit(solution)/shard_map/expert/pallas_call | solution.py:105
  88.6 1.4 fusion.17
  90.0 0.5 collective-permute-start.10
  90.9 31.2 %collective-permute-done.10 = bf16[40,3712]{1,0:T(8,128)(2,1)S(1)} collective-permute-done((bf16[40,3712]{1,0:T(8,128)(2,1)S(1)}, bf16[40,3712]{1,0:T(8,128)(2,1)S(1)}, u32[]{:S(2)}, u32[]{:S(2)}) %collective-permute-start.10) | collective-permute-done | bytes 296992 | tf_op jit(solution)/shard_map/ppermute | solution.py:139
  122.4 1.3 fusion.16
  123.7 3.4 %collective-permute-start.13 = (bf16[40,3712]{1,0:T(8,128)(2,1)S(1)}, bf16[40,3712]{1,0:T(8,128)(2,1)S(1)}, u32[]{:S(2)}, u32[]{:S(2)}) collective-permute-start(bf16[40,3712]{1,0:T(8,128)(2,1)S(1)} %get-tuple-element.66), channel_id=1, source_target_pairs={{0,10},{2,8},{4,14},{6,12},{8,2},{10,0},{12,6},{14,4},{1,11},{3,9}... | collective-permute-start | bytes 890888 | tf_op jit(solution)/shard_map/ppermute | solution.py:139
  127.1 19.5 %expert.3 = bf16[120,3712]{1,0:T(8,128)(2,1)} custom-call(bf16[120,3584]{1,0:T(8,128)(2,1)} %bitcast.63, bf16[120,3584]{1,0:T(8,128)(2,1)} %bitcast.62, bf16[1,3584,512]{2,1,0:T(8,128)(2,1)} %refs_0_.3, bf16[1,3584,512]{2,1,0:T(8,128)(2,1)} %refs_1_.3, bf16[1,512,3584]{2,1,0:T(8,128)(2,1)} %refs_2_.3, bf16[1,3584,512]{2,1,0:T(8,128)(2,1)} %collective-permute-done.2.refs_3_, ...), custom_call_target="tpu_custom_call" | custom-call | flops 1 | bytes 1 | tf_op jit(solution)/shard_map/expert/pallas_call | solution.py:105
  146.6 1.2 fusion.18
  147.8 1.5 collective-permute-done.13
  149.3 1.9 %collective-permute-start.15 = (bf16[40,3712]{1,0:T(8,128)(2,1)S(1)}, bf16[40,3712]{1,0:T(8,128)(2,1)S(1)}, u32[]{:S(2)}, u32[]{:S(2)}) collective-permute-start(bf16[40,3712]{1,0:T(8,128)(2,1)S(1)} %get-tuple-element.76), channel_id=1, source_target_pairs={{0,14},{2,12},{4,10},{6,8},{8,6},{10,4},{12,2},{14,0},{1,15},{3,13... | collective-permute-start | bytes 890888 | tf_op jit(solution)/shard_map/ppermute | solution.py:139
  151.3 5.4 %collective-permute-start.16 = (bf16[40,3712]{1,0:T(8,128)(2,1)S(1)}, bf16[40,3712]{1,0:T(8,128)(2,1)S(1)}, u32[]{:S(2)}, u32[]{:S(2)}) collective-permute-start(bf16[40,3712]{1,0:T(8,128)(2,1)S(1)} %get-tuple-element.77), channel_id=1, source_target_pairs={{0,6},{2,4},{4,2},{6,0},{8,14},{10,12},{12,10},{14,8},{1,7},{3,5},... | collective-permute-start | bytes 890888 | tf_op jit(solution)/shard_map/ppermute | solution.py:139
  158.0 14.0 %collective-permute-done.14 = bf16[40,3712]{1,0:T(8,128)(2,1)S(1)} collective-permute-done((bf16[40,3712]{1,0:T(8,128)(2,1)S(1)}, bf16[40,3712]{1,0:T(8,128)(2,1)S(1)}, u32[]{:S(2)}, u32[]{:S(2)}) %collective-permute-start.14) | collective-permute-done | bytes 296992 | tf_op jit(solution)/shard_map/ppermute | solution.py:139
  172.1 7.6 %collective-permute-done.15 = bf16[40,3712]{1,0:T(8,128)(2,1)S(1)} collective-permute-done((bf16[40,3712]{1,0:T(8,128)(2,1)S(1)}, bf16[40,3712]{1,0:T(8,128)(2,1)S(1)}, u32[]{:S(2)}, u32[]{:S(2)}) %collective-permute-start.15) | collective-permute-done | bytes 296992 | tf_op jit(solution)/shard_map/ppermute | solution.py:139
  180.4 0.6 add_bitcast_fusion
  181.0 1.4 fusion.1
  (56 shorter events, 4.0 us)
Async XLA Ops:
  0.6 11.1 %collective-permute-start.2 = (bf16[1,3584,512]{2,1,0:T(8,128)(2,1)}, bf16[1,3584,512]{2,1,0:T(8,128)(2,1)}, u32[]{:S(2)}, u32[]{:S(2)}) collective-permute-start(bf16[1,3584,512]{2,1,0:T(8,128)(2,1)} %refs_0_.3), channel_id=1, source_target_pairs={{0,1},{1,0},{2,3},{3,2},{4,5},{5,4},{6,7},{7,6},{8,9},{9,8},{10,11... | collective-permute-start | bytes 11010056 | tf_op jit(solution)/shard_map/ppermute | solution.py:30
  0.7 12.0 %collective-permute-start.3 = (bf16[1,3584,512]{2,1,0:T(8,128)(2,1)}, bf16[1,3584,512]{2,1,0:T(8,128)(2,1)}, u32[]{:S(2)}, u32[]{:S(2)}) collective-permute-start(bf16[1,3584,512]{2,1,0:T(8,128)(2,1)} %refs_1_.3), channel_id=1, source_target_pairs={{0,1},{1,0},{2,3},{3,2},{4,5},{5,4},{6,7},{7,6},{8,9},{9,8},{10,11... | collective-permute-start | bytes 11010056 | tf_op jit(solution)/shard_map/ppermute | solution.py:30
  1.2 16.7 %collective-permute-start.4 = (bf16[1,512,3584]{2,1,0:T(8,128)(2,1)}, bf16[1,512,3584]{2,1,0:T(8,128)(2,1)}, u32[]{:S(2)}, u32[]{:S(2)}) collective-permute-start(bf16[1,512,3584]{2,1,0:T(8,128)(2,1)} %refs_2_.3), channel_id=1, source_target_pairs={{0,1},{1,0},{2,3},{3,2},{4,5},{5,4},{6,7},{7,6},{8,9},{9,8},{10,11... | collective-permute-start | bytes 11010056 | tf_op jit(solution)/shard_map/ppermute | solution.py:30
  3.1 1.2 copy-start
  4.3 1.2 copy-start.1
  6.1 40.0 %collective-permute-start = (bf16[2,40,3584]{2,1,0:T(8,128)(2,1)S(1)}, bf16[2,40,3584]{2,1,0:T(8,128)(2,1)S(1)}, u32[]{:S(2)}, u32[]{:S(2)}) collective-permute-start(bf16[2,40,3584]{2,1,0:T(8,128)(2,1)S(1)} %get-tuple-element.42), channel_id=1, source_target_pairs={{0,8},{2,10},{4,12},{6,14},{8,0},{10,2},{12,4},{14,6},{1,9},{3,11}... | collective-permute-start | bytes 1720328 | tf_op jit(solution)/shard_map/ppermute | solution.py:139
  8.7 49.6 %collective-permute-start.1 = (bf16[2,40,3584]{2,1,0:T(8,128)(2,1)S(1)}, bf16[2,40,3584]{2,1,0:T(8,128)(2,1)S(1)}, u32[]{:S(2)}, u32[]{:S(2)}) collective-permute-start(bf16[2,40,3584]{2,1,0:T(8,128)(2,1)S(1)} %get-tuple-element.43), channel_id=1, source_target_pairs={{0,10},{2,8},{4,14},{6,12},{8,2},{10,0},{12,6},{14,4},{1,11},{3,9}... | collective-permute-start | bytes 1720328 | tf_op jit(solution)/shard_map/ppermute | solution.py:139
  17.9 40.4 %collective-permute-start.5 = (bf16[2,40,3584]{2,1,0:T(8,128)(2,1)S(1)}, bf16[2,40,3584]{2,1,0:T(8,128)(2,1)S(1)}, u32[]{:S(2)}, u32[]{:S(2)}) collective-permute-start(bf16[2,40,3584]{2,1,0:T(8,128)(2,1)S(1)} %get-tuple-element.49), channel_id=1, source_target_pairs={{0,2},{2,0},{4,6},{6,4},{8,10},{10,8},{12,14},{14,12},{1,3},{3,1},... | collective-permute-start | bytes 1720328 | tf_op jit(solution)/shard_map/ppermute | solution.py:139
  19.4 38.9 %collective-permute-start.6 = (bf16[2,40,3584]{2,1,0:T(8,128)(2,1)S(1)}, bf16[2,40,3584]{2,1,0:T(8,128)(2,1)S(1)}, u32[]{:S(2)}, u32[]{:S(2)}) collective-permute-start(bf16[2,40,3584]{2,1,0:T(8,128)(2,1)S(1)} %get-tuple-element.50), channel_id=1, source_target_pairs={{0,4},{2,6},{4,0},{6,2},{8,12},{10,14},{12,8},{14,10},{1,5},{3,7},... | collective-permute-start | bytes 1720328 | tf_op jit(solution)/shard_map/ppermute | solution.py:139
  60.4 61.8 %collective-permute-start.7 = (bf16[2,40,3584]{2,1,0:T(8,128)(2,1)S(1)}, bf16[2,40,3584]{2,1,0:T(8,128)(2,1)S(1)}, u32[]{:S(2)}, u32[]{:S(2)}) collective-permute-start(bf16[2,40,3584]{2,1,0:T(8,128)(2,1)S(1)} %get-tuple-element.54), channel_id=1, source_target_pairs={{0,12},{2,14},{4,8},{6,10},{8,4},{10,6},{12,0},{14,2},{1,13},{3,15... | collective-permute-start | bytes 1720328 | tf_op jit(solution)/shard_map/ppermute | solution.py:139
  60.4 61.8 %collective-permute-start.8 = (bf16[2,40,3584]{2,1,0:T(8,128)(2,1)S(1)}, bf16[2,40,3584]{2,1,0:T(8,128)(2,1)S(1)}, u32[]{:S(2)}, u32[]{:S(2)}) collective-permute-start(bf16[2,40,3584]{2,1,0:T(8,128)(2,1)S(1)} %get-tuple-element.55), channel_id=1, source_target_pairs={{0,14},{2,12},{4,10},{6,8},{8,6},{10,4},{12,2},{14,0},{1,15},{3,13... | collective-permute-start | bytes 1720328 | tf_op jit(solution)/shard_map/ppermute | solution.py:139
  63.3 58.8 %collective-permute-start.9 = (bf16[2,40,3584]{2,1,0:T(8,128)(2,1)S(1)}, bf16[2,40,3584]{2,1,0:T(8,128)(2,1)S(1)}, u32[]{:S(2)}, u32[]{:S(2)}) collective-permute-start(bf16[2,40,3584]{2,1,0:T(8,128)(2,1)S(1)} %get-tuple-element.56), channel_id=1, source_target_pairs={{0,6},{2,4},{4,2},{6,0},{8,14},{10,12},{12,10},{14,8},{1,7},{3,5},... | collective-permute-start | bytes 1720328 | tf_op jit(solution)/shard_map/ppermute | solution.py:139
  90.0 32.1 %collective-permute-start.10 = (bf16[40,3712]{1,0:T(8,128)(2,1)S(1)}, bf16[40,3712]{1,0:T(8,128)(2,1)S(1)}, u32[]{:S(2)}, u32[]{:S(2)}) collective-permute-start(bf16[40,3712]{1,0:T(8,128)(2,1)S(1)} %get-tuple-element.90), channel_id=1, source_target_pairs={{0,2},{2,0},{4,6},{6,4},{8,10},{10,8},{12,14},{14,12},{1,3},{3,1},... | collective-permute-start | bytes 890888 | tf_op jit(solution)/shard_map/ppermute | solution.py:139
  90.6 31.6 %collective-permute-start.11 = (bf16[40,3712]{1,0:T(8,128)(2,1)S(1)}, bf16[40,3712]{1,0:T(8,128)(2,1)S(1)}, u32[]{:S(2)}, u32[]{:S(2)}) collective-permute-start(bf16[40,3712]{1,0:T(8,128)(2,1)S(1)} %get-tuple-element.89), channel_id=1, source_target_pairs={{0,4},{2,6},{4,0},{6,2},{8,12},{10,14},{12,8},{14,10},{1,5},{3,7},... | collective-permute-start | bytes 890888 | tf_op jit(solution)/shard_map/ppermute | solution.py:139
  123.7 24.1 %collective-permute-start.12 = (bf16[40,3712]{1,0:T(8,128)(2,1)S(1)}, bf16[40,3712]{1,0:T(8,128)(2,1)S(1)}, u32[]{:S(2)}, u32[]{:S(2)}) collective-permute-start(bf16[40,3712]{1,0:T(8,128)(2,1)S(1)} %get-tuple-element.65), channel_id=1, source_target_pairs={{0,8},{2,10},{4,12},{6,14},{8,0},{10,2},{12,4},{14,6},{1,9},{3,11}... | collective-permute-start | bytes 890888 | tf_op jit(solution)/shard_map/ppermute | solution.py:139
  123.7 25.6 %collective-permute-start.13 = (bf16[40,3712]{1,0:T(8,128)(2,1)S(1)}, bf16[40,3712]{1,0:T(8,128)(2,1)S(1)}, u32[]{:S(2)}, u32[]{:S(2)}) collective-permute-start(bf16[40,3712]{1,0:T(8,128)(2,1)S(1)} %get-tuple-element.66), channel_id=1, source_target_pairs={{0,10},{2,8},{4,14},{6,12},{8,2},{10,0},{12,6},{14,4},{1,11},{3,9}... | collective-permute-start | bytes 890888 | tf_op jit(solution)/shard_map/ppermute | solution.py:139
  147.8 9.2 %copy-start.2 = (f32[128,2]{0,1:T(2,128)S(1)}, f32[128,2]{0,1:T(2,128)}, u32[]{:S(2)}) copy-start(f32[128,2]{0,1:T(2,128)} %param.10) | copy-start | bytes 3076
  149.3 22.7 %collective-permute-start.14 = (bf16[40,3712]{1,0:T(8,128)(2,1)S(1)}, bf16[40,3712]{1,0:T(8,128)(2,1)S(1)}, u32[]{:S(2)}, u32[]{:S(2)}) collective-permute-start(bf16[40,3712]{1,0:T(8,128)(2,1)S(1)} %get-tuple-element.75), channel_id=1, source_target_pairs={{0,12},{2,14},{4,8},{6,10},{8,4},{10,6},{12,0},{14,2},{1,13},{3,15... | collective-permute-start | bytes 890888 | tf_op jit(solution)/shard_map/ppermute | solution.py:139
  149.3 30.4 %collective-permute-start.15 = (bf16[40,3712]{1,0:T(8,128)(2,1)S(1)}, bf16[40,3712]{1,0:T(8,128)(2,1)S(1)}, u32[]{:S(2)}, u32[]{:S(2)}) collective-permute-start(bf16[40,3712]{1,0:T(8,128)(2,1)S(1)} %get-tuple-element.76), channel_id=1, source_target_pairs={{0,14},{2,12},{4,10},{6,8},{8,6},{10,4},{12,2},{14,0},{1,15},{3,13... | collective-permute-start | bytes 890888 | tf_op jit(solution)/shard_map/ppermute | solution.py:139
  151.3 28.5 %collective-permute-start.16 = (bf16[40,3712]{1,0:T(8,128)(2,1)S(1)}, bf16[40,3712]{1,0:T(8,128)(2,1)S(1)}, u32[]{:S(2)}, u32[]{:S(2)}) collective-permute-start(bf16[40,3712]{1,0:T(8,128)(2,1)S(1)} %get-tuple-element.77), channel_id=1, source_target_pairs={{0,6},{2,4},{4,2},{6,0},{8,14},{10,12},{12,10},{14,8},{1,7},{3,5},... | collective-permute-start | bytes 890888 | tf_op jit(solution)/shard_map/ppermute | solution.py:139

commit v3 on v2

v3 whole, which is shorter than its diff:
```python
import functools

import jax
import jax.numpy as jnp
from jax import lax
from jax.experimental import pallas as pl
from jax.experimental.pallas import tpu as pltpu
from jax.sharding import Mesh
from jax.sharding import PartitionSpec as P

BF16 = jnp.bfloat16
F32 = jnp.float32
CHIPS = ("node", "chip")
ROWS = ("rep", "node", "chip", "core")
PIECES = ("node", "chip", "core")
LANES = 128
VMEM = pl.BlockSpec(memory_space=pltpu.VMEM)
SMALL = pl.CostEstimate(flops=1, bytes_accessed=1, transcendentals=0)


def nt(left, right):
    return lax.dot_general(left, right, (((1,), (1,)), ((), ())), preferred_element_type=F32)


def nn(left, right):
    return jnp.dot(left, right, preferred_element_type=F32)


def swap_cores(values):
    return lax.ppermute(values, "core", [(0, 1), (1, 0)])


def dispatch_kernel(offsets, capacity, index_ref, *refs):
    sources, out_refs = refs[: -len(offsets)], refs[-len(offsets) :]
    count = index_ref.shape[1]
    for offset, out_ref in zip(offsets, out_refs):
        rows = lax.broadcasted_iota(jnp.int32, (capacity, count), 0) + offset * capacity
        hits = jnp.zeros((capacity, count), F32)
        for choice in range(index_ref.shape[0]):
            hits = hits + jnp.where(rows == index_ref[choice : choice + 1, :], 1.0, 0.0)
        hits = hits.astype(BF16)
        for place, source in enumerate(sources):
            out_ref[place] = nn(hits, source[...]).astype(BF16)


def dispatch(row_index, sources, offsets, capacity):
    width = sources[0].shape[1]
    shape = (len(sources), capacity, width)
    return pl.pallas_call(
        functools.partial(dispatch_kernel, offsets, capacity),
        out_shape=[jax.ShapeDtypeStruct(shape, BF16)] * len(offsets),
        in_specs=[VMEM] * (1 + len(sources)),
        out_specs=[VMEM] * len(offsets),
        compiler_params=pltpu.CompilerParams(vmem_limit_bytes=48 << 20),
        cost_estimate=SMALL,
        name="dispatch",
    )(row_index, *sources)


def expert_kernel(tile, tokens_ref, upstream_ref, *refs):
    pieces, (out_ref, total, part) = (refs[:3], refs[3:6]), refs[6:]
    width = tokens_ref.shape[1]
    total[...] = jnp.zeros_like(total)
    part[...] = jnp.zeros_like(part)
    for gate_ref, up_ref, down_ref in pieces:
        for start in range(0, gate_ref.shape[2], tile):
            units = slice(start, start + tile)
            tokens = tokens_ref[...]
            gate_piece, up_piece = gate_ref[0, :, units], up_ref[0, :, units]
            gate_lin = nn(tokens, gate_piece)
            up_lin = nn(tokens, up_piece)
            projected = nt(upstream_ref[...], down_ref[0, units, :])
            sigmoid_g = jax.nn.sigmoid(gate_lin)
            activated = gate_lin * sigmoid_g
            hidden = (activated * up_lin).astype(BF16).astype(F32)
            part[...] += jnp.sum(projected * hidden, axis=1, keepdims=True)
            slope = sigmoid_g * (1.0 + gate_lin * (1.0 - sigmoid_g))
            d_gate = (projected * up_lin * slope).astype(BF16)
            d_up = (projected * activated).astype(BF16)
            total[...] += nt(d_gate, gate_piece) + nt(d_up, up_piece)
    out_ref[:, :width] = total[...].astype(BF16)
    out_ref[:, width:] = jnp.broadcast_to(part[...], (part.shape[0], LANES)).astype(BF16)


def expert(tokens, upstream, own, other):
    rows, width = tokens.shape
    return pl.pallas_call(
        functools.partial(expert_kernel, min(256, own[0].shape[2])),
        out_shape=jax.ShapeDtypeStruct((rows, width + LANES), BF16),
        in_specs=[VMEM] * 8,
        out_specs=VMEM,
        scratch_shapes=[pltpu.VMEM((rows, width), F32), pltpu.VMEM((rows, 1), F32)],
        compiler_params=pltpu.CompilerParams(vmem_limit_bytes=38 << 20),
        cost_estimate=SMALL,
        name="expert",
    )(tokens, upstream, *own, *other)


def per_device(tokens, routes, gates, placement, upstream, w_gate, w_up, w_down):
    tok_dev, width = tokens.shape
    top_count = routes.shape[1]
    experts = placement.shape[0]
    nodes, node_chips = lax.axis_size("node"), lax.axis_size("chip")
    chips = nodes * node_chips
    assert chips == experts and chips & (chips - 1) == 0 and nodes % 4 == 0
    capacity = 5 * tok_dev * top_count // (4 * experts)
    me = lax.axis_index("node") * node_chips + lax.axis_index("chip")

    hit = (routes[:, :, None] == jnp.arange(experts, dtype=jnp.int32)).astype(jnp.int32)
    named = jnp.sum(hit, axis=1)
    before = jnp.cumsum(named, axis=0) - named
    rank = jnp.sum(hit * before[:, None, :], axis=2)
    slot = jnp.sum(hit * placement, axis=2)
    row_index = ((slot ^ me) * capacity + rank).T

    def move(sent, offsets):
        return [
            lax.ppermute(rows, CHIPS, [(i, i ^ offset) for i in range(chips)]) if offset else rows
            for rows, offset in zip(sent, offsets)
        ]

    def work(got_tokens, got_upstream, weights):
        out = expert(jnp.concatenate(got_tokens), jnp.concatenate(got_upstream), *weights)
        return [out[i * capacity : (i + 1) * capacity] for i in range(len(got_tokens))]

    def combine(back, offsets):
        rows = jnp.arange(capacity, dtype=jnp.int32)
        hits = jnp.concatenate(
            [(rows + o * capacity)[:, None, None] == row_index[None] for o in offsets]
        )
        weighted = jnp.sum(jnp.where(hits, gates.T[None], 0.0), axis=1).T
        high = weighted.astype(BF16)
        low = (weighted - high.astype(F32)).astype(BF16)
        rows = jnp.concatenate(back)
        part = rows[:, width].astype(F32)
        rows = rows[:, :width]
        return nn(high, rows) + nn(low, rows), jnp.sum(
            jnp.where(hits, part[:, None, None], 0.0), axis=0
        ).T

    half = chips // 2
    near = list(range(half))
    far1, far2 = list(range(half, half + half // 2)), list(range(half + half // 2, chips))
    side = list(range(half // 2))
    cross = list(range(half // 2, half))
    tie = lax.optimization_barrier
    weights = ((w_gate, w_up, w_down), tuple(swap_cores(piece) for piece in (w_gate, w_up, w_down)))

    mirror_tokens = move([tokens], [half])[0]
    sent = dispatch(row_index, [tokens, upstream], near, capacity)
    sent_far = [rows[0] for rows in dispatch(row_index, [upstream], far1 + far2, capacity)]
    sent_side, sent_cross = sent[: len(side)], sent[len(side) :]
    sent_side, index, weights = tie((sent_side, row_index, weights))
    cut = len(cross) // 2
    got_side = move(sent_side, side)
    got_cross = move(sent_cross[:cut], cross[:cut])
    mirror_index = move([index], [half])[0]

    first_up, mirror_tokens = tie((sent_far[:cut], mirror_tokens))
    up_far1 = move(first_up, far1[:cut])
    mirror_tokens, mirror_index, got_cross, got_side, sent_last, rest_up = tie(
        (mirror_tokens, mirror_index, got_cross, got_side, sent_cross[cut:], sent_far[cut:])
    )
    up_far1 += move(rest_up[: len(far1) - cut], far1[cut:])
    sent_far = rest_up[len(far1) - cut :]
    passed = [rows[0] for rows in dispatch(mirror_index, [mirror_tokens], far1 + far2, capacity)]
    pass_far1 = move(passed[: len(far1)], side)
    got_cross += move(sent_last, cross[cut:])
    up_far1, sent_far = tie((up_far1, sent_far))
    up_far2 = move(sent_far, far2)
    up_far1, pass_far1, got_side, got_cross, passed = tie(
        (up_far1, pass_far1, got_side, got_cross, passed[len(far1) :])
    )
    pass_far2 = move(passed, cross)
    got = got_side + got_cross
    first = work(
        pass_far1 + [rows[0] for rows in got], up_far1 + [rows[1] for rows in got], weights
    )
    up_far2, pass_far2, first = tie((up_far2, pass_far2, first))
    back_far1 = move(first[: len(far1)], far1)
    back_near = move(first[len(far1) :], near)
    second = work(pass_far2, up_far2, weights)
    back_far1, second = tie((back_far1, second))
    back_far2 = move(second, far2)
    early, gate_early = combine(back_far1, far1)
    late, gate_late = combine(back_far2 + back_near, far2 + near)
    return (early + late).astype(BF16), gate_early + gate_late


def solution(mesh):
    shape = mesh.devices.shape
    split = Mesh(
        mesh.devices.reshape(shape[0], shape[1], shape[2] // 2, 2), ("rep", "node", "chip", "core")
    )
    return jax.shard_map(
        per_device,
        mesh=split,
        in_specs=(
            P(ROWS, None),
            P(ROWS, None),
            P(ROWS, None),
            P(),
            P(ROWS, None),
            P(PIECES, None, None),
            P(PIECES, None, None),
            P(PIECES, None, None),
        ),
        out_specs=(P(ROWS, None), P(ROWS, None)),
        check_vma=False,
    )
```

time: 183 us -> 162 us (0.89)
  waiting for transfers between devices: 98.9 us -> 83.6 us
  Pallas kernels: 42.9 us -> 34.2 us
  starting transfers between devices: 25.1 us -> 30.5 us
    ppermute x14 -> x19, waiting for transfers between devices: 92.7 us -> 75.5 us  [move(): lax.ppermute(rows, CHIPS, [(i, i ^ offset) for i in range(chips)])]
    pallas_call x2, Pallas kernels: 40.7 us -> 31.9 us  [expert(): pl.pallas_call(functools.partial(expert_kernel, min(256, own[0].shape[2])...]
    slice x4 -> x2, local copies, waits for them, and re-layouts: 5.72 us -> 0.17 us  [work(): out[i * capacity:(i + 1) * capacity]]
    ppermute x14 -> x19, starting transfers between devices: 24.4 us -> 29.8 us  [move(): lax.ppermute(rows, CHIPS, [(i, i ^ offset) for i in range(chips)])]
    unnamed x16 -> x24, local copies, waits for them, and re-layouts: 2.67 us -> 6.59 us
    ppermute x3, waiting for transfers between devices: 6.24 us -> 8.08 us  [swap_cores(): return lax.ppermute(values, 'core', [(0, 1), (1, 0)])]
  transfers between devices with their start and end apart: 17 -> 22, of which waited for: 8 -> 10; matrix products, arithmetic and copies ran while one was open for 3% -> 2% of each run, Pallas kernels for 24% -> 21%
where the time goes in v3:
time: 162 us
  waiting for transfers between devices  83.6 us (52%)
  Pallas kernels  34.2 us (21%)
  starting transfers between devices  30.5 us (19%)
  local copies, waits for them, and re-layouts  7.01 us (4%)
  other arithmetic  3.2 us (2%)
  matrix products  2.72 us (2%)
    ppermute x19, waiting for transfers between devices, move(): lax.ppermute(rows, CHIPS, [(i, i ^ offset) for i in range(chips)])  75.5 us
    pallas_call x2, Pallas kernels, expert(): pl.pallas_call(functools.partial(expert_kernel, min(256, own[0].shape[2])...  31.9 us
    ppermute x19, starting transfers between devices, move(): lax.ppermute(rows, CHIPS, [(i, i ^ offset) for i in range(chips)])  29.8 us
    ppermute x3, waiting for transfers between devices, swap_cores(): return lax.ppermute(values, 'core', [(0, 1), (1, 0)])  8.08 us
    unnamed x24, local copies, waits for them, and re-layouts  6.59 us
  transfers between devices with their start and end apart: 22, of which 10 were waited for; matrix products, arithmetic and copies ran while one was open for 2% of the time, Pallas kernels for 21%

profile of v3, /device:TPU:8, one launch (start us, length us, event | category | flops | bytes accessed | tf_op | source)
XLA Modules:
  0.0 162.1 jit_solution(12239551007769655784)
XLA Ops:
  1.3 2.6 %collective-permute-start = (bf16[128,3584]{1,0:T(8,128)(2,1)}, bf16[128,3584]{1,0:T(8,128)(2,1)S(1)}, u32[]{:S(2)}, u32[]{:S(2)}) collective-permute-start(bf16[128,3584]{1,0:T(8,128)(2,1)} %refs_0_.3), channel_id=1, source_target_pairs={{0,8},{2,10},{4,12},{6,14},{8,0},{10,2},{12,4},{14,6},{1,9},{3,11}... | collective-permute-start | bytes 2752520 | tf_op jit(solution)/shard_map/ppermute | solution.py:118
  4.9 0.8 select_reduce_fusion.5
  5.7 1.2 copy-done.3
  6.9 1.2 copy-done.4
  8.1 1.1 dispatch.4
  9.9 2.8 %collective-permute-done.3.refs_4_ = bf16[1,3584,512]{2,1,0:T(8,128)(2,1)} collective-permute-done((bf16[1,3584,512]{2,1,0:T(8,128)(2,1)}, bf16[1,3584,512]{2,1,0:T(8,128)(2,1)}, u32[]{:S(2)}, u32[]{:S(2)}) %collective-permute-start.3) | collective-permute-done | bytes 3670048 | tf_op jit(solution)/shard_map/ppermute | solution.py:30
  12.7 5.2 %collective-permute-done.4.refs_5_ = bf16[1,512,3584]{2,1,0:T(8,128)(2,1)} collective-permute-done((bf16[1,512,3584]{2,1,0:T(8,128)(2,1)}, bf16[1,512,3584]{2,1,0:T(8,128)(2,1)}, u32[]{:S(2)}, u32[]{:S(2)}) %collective-permute-start.4) | collective-permute-done | bytes 3670048 | tf_op jit(solution)/shard_map/ppermute | solution.py:30
  17.9 1.5 collective-permute-start.7
  19.5 2.7 %collective-permute-start.5 = (s32[2,128]{1,0:T(2,128)S(1)}, s32[2,128]{1,0:T(2,128)S(1)}, u32[]{:S(2)}, u32[]{:S(2)}) collective-permute-start(s32[2,128]{1,0:T(2,128)S(1)} %add_bitcast_fusion.1.index_ref), channel_id=1, source_target_pairs={{0,8},{2,10},{4,12},{6,14},{8,0},{10,2},{12,4},{14,6},{1,9},{3,11}... | collective-permute-start | bytes 3080 | tf_op jit(solution)/shard_map/ppermute | solution.py:118
  22.8 21.2 %collective-permute-done.refs_0_ = bf16[128,3584]{1,0:T(8,128)(2,1)S(1)} collective-permute-done((bf16[128,3584]{1,0:T(8,128)(2,1)}, bf16[128,3584]{1,0:T(8,128)(2,1)S(1)}, u32[]{:S(2)}, u32[]{:S(2)}) %collective-permute-start) | collective-permute-done | bytes 917536 | tf_op jit(solution)/shard_map/ppermute | solution.py:118
  44.0 2.2 %collective-permute-start.12 = (bf16[2,40,3584]{2,1,0:T(8,128)(2,1)S(1)}, bf16[2,40,3584]{2,1,0:T(8,128)(2,1)S(1)}, u32[]{:S(2)}, u32[]{:S(2)}) collective-permute-start(bf16[2,40,3584]{2,1,0:T(8,128)(2,1)S(1)} %get-tuple-element.89), channel_id=1, source_target_pairs={{0,6},{2,4},{4,2},{6,0},{8,14},{10,12},{12,10},{14,8},{1,7},{3,5},... | collective-permute-start | bytes 1720328 | tf_op jit(solution)/shard_map/ppermute | solution.py:118
  46.3 1.2 collective-permute-start.1
  47.5 1.7 %collective-permute-start.8 = (bf16[40,3584]{1,0:T(8,128)(2,1)S(1)}, bf16[40,3584]{1,0:T(8,128)(2,1)S(1)}, u32[]{:S(2)}, u32[]{:S(2)}) collective-permute-start(bf16[40,3584]{1,0:T(8,128)(2,1)S(1)} %bitcast.72), channel_id=1, source_target_pairs={{0,10},{2,8},{4,14},{6,12},{8,2},{10,0},{12,6},{14,4},{1,11},{3,9}... | collective-permute-start | bytes 860168 | tf_op jit(solution)/shard_map/ppermute | solution.py:118
  49.9 1.6 %collective-permute-start.11 = (bf16[40,3584]{1,0:T(8,128)(2,1)S(1)}, bf16[40,3584]{1,0:T(8,128)(2,1)S(1)}, u32[]{:S(2)}, u32[]{:S(2)}) collective-permute-start(bf16[40,3584]{1,0:T(8,128)(2,1)S(1)} %bitcast.74), channel_id=1, source_target_pairs={{0,2},{2,0},{4,6},{6,4},{8,10},{10,8},{12,14},{14,12},{1,3},{3,1},... | collective-permute-start | bytes 860168 | tf_op jit(solution)/shard_map/ppermute | solution.py:118
  51.6 15.8 %collective-permute-done.1 = bf16[40,3584]{1,0:T(8,128)(2,1)S(1)} collective-permute-done((bf16[40,3584]{1,0:T(8,128)(2,1)S(1)}, bf16[40,3584]{1,0:T(8,128)(2,1)S(1)}, u32[]{:S(2)}, u32[]{:S(2)}) %collective-permute-start.1) | collective-permute-done | bytes 286752 | tf_op jit(solution)/shard_map/ppermute | solution.py:118
  67.4 6.5 %collective-permute-done.8 = bf16[40,3584]{1,0:T(8,128)(2,1)S(1)} collective-permute-done((bf16[40,3584]{1,0:T(8,128)(2,1)S(1)}, bf16[40,3584]{1,0:T(8,128)(2,1)S(1)}, u32[]{:S(2)}, u32[]{:S(2)}) %collective-permute-start.8) | collective-permute-done | bytes 286752 | tf_op jit(solution)/shard_map/ppermute | solution.py:118
  73.9 2.0 %collective-permute-start.10 = (bf16[40,3584]{1,0:T(8,128)(2,1)S(1)}, bf16[40,3584]{1,0:T(8,128)(2,1)S(1)}, u32[]{:S(2)}, u32[]{:S(2)}) collective-permute-start(bf16[40,3584]{1,0:T(8,128)(2,1)S(1)} %bitcast.68), channel_id=1, source_target_pairs={{0,14},{2,12},{4,10},{6,8},{8,6},{10,4},{12,2},{14,0},{1,15},{3,13... | collective-permute-start | bytes 860168 | tf_op jit(solution)/shard_map/ppermute | solution.py:118
  75.9 4.6 %collective-permute-start.13 = (bf16[40,3584]{1,0:T(8,128)(2,1)S(1)}, bf16[40,3584]{1,0:T(8,128)(2,1)S(1)}, u32[]{:S(2)}, u32[]{:S(2)}) collective-permute-start(bf16[40,3584]{1,0:T(8,128)(2,1)S(1)} %bitcast.71), channel_id=1, source_target_pairs={{0,4},{2,6},{4,0},{6,2},{8,12},{10,14},{12,8},{14,10},{1,5},{3,7},... | collective-permute-start | bytes 860168 | tf_op jit(solution)/shard_map/ppermute | solution.py:118
  80.8 1.8 %copy-done = bf16[1,3584,512]{2,1,0:T(8,128)(2,1)S(1)} copy-done((bf16[1,3584,512]{2,1,0:T(8,128)(2,1)S(1)}, bf16[1,3584,512]{2,1,0:T(8,128)(2,1)}, u32[]{:S(2)}) %copy-start) | copy-done | bytes 3670040
  82.7 2.0 %copy-done.2 = bf16[1,512,3584]{2,1,0:T(8,128)(2,1)S(1)} copy-done((bf16[1,512,3584]{2,1,0:T(8,128)(2,1)S(1)}, bf16[1,512,3584]{2,1,0:T(8,128)(2,1)}, u32[]{:S(2)}) %copy-start.2) | copy-done | bytes 3670040
  84.7 17.3 %expert.2 = bf16[240,3712]{1,0:T(8,128)(2,1)S(1)} custom-call(bf16[240,3584]{1,0:T(8,128)(2,1)S(1)} %get-tuple-element.137.tokens_ref, bf16[240,3584]{1,0:T(8,128)(2,1)S(1)} %get-tuple-element.136.upstream_ref, bf16[1,3584,512]{2,1,0:T(8,128)(2,1)S(1)} %copy-done, bf16[1,3584,512]{2,1,0:T(8,128)(2,1)S(1)} %copy-done.1, bf16[1,512,3584]{2,1,0:T(8,128)(2,1)S(1)} %copy-done.2, ...), custom_call_target="tpu_custom_call" | custom-call | flops 1 | bytes 1 | tf_op jit(solution)/shard_map/expert/pallas_call | solution.py:87
  102.1 2.3 %collective-permute-done.10 = bf16[40,3584]{1,0:T(8,128)(2,1)S(1)} collective-permute-done((bf16[40,3584]{1,0:T(8,128)(2,1)S(1)}, bf16[40,3584]{1,0:T(8,128)(2,1)S(1)}, u32[]{:S(2)}, u32[]{:S(2)}) %collective-permute-start.10) | collective-permute-done | bytes 286752 | tf_op jit(solution)/shard_map/ppermute | solution.py:118
  104.4 2.1 %collective-permute-done.14 = bf16[40,3584]{1,0:T(8,128)(2,1)S(1)} collective-permute-done((bf16[40,3584]{1,0:T(8,128)(2,1)S(1)}, bf16[40,3584]{1,0:T(8,128)(2,1)S(1)}, u32[]{:S(2)}, u32[]{:S(2)}) %collective-permute-start.14) | collective-permute-done | bytes 286752 | tf_op jit(solution)/shard_map/ppermute | solution.py:118
  106.6 3.7 %collective-permute-start.16 = (bf16[40,3712]{1,0:T(8,128)(2,1)S(1)}, bf16[40,3712]{1,0:T(8,128)(2,1)S(1)}, u32[]{:S(2)}, u32[]{:S(2)}) collective-permute-start(bf16[40,3712]{1,0:T(8,128)(2,1)S(1)} %get-tuple-element.109), channel_id=1, source_target_pairs={{0,10},{2,8},{4,14},{6,12},{8,2},{10,0},{12,6},{14,4},{1,11},{3,9}... | collective-permute-start | bytes 890888 | tf_op jit(solution)/shard_map/ppermute | solution.py:118
  110.3 14.6 %expert.3 = bf16[80,3712]{1,0:T(8,128)(2,1)S(1)} custom-call(bf16[80,3584]{1,0:T(8,128)(2,1)S(1)} %pad_maximum_fusion.tokens_ref, bf16[80,3584]{1,0:T(8,128)(2,1)S(1)} %pad_maximum_fusion.1.upstream_ref, bf16[1,3584,512]{2,1,0:T(8,128)(2,1)S(1)} %copy-done, bf16[1,3584,512]{2,1,0:T(8,128)(2,1)S(1)} %copy-done.1, bf16[1,512,3584]{2,1,0:T(8,128)(2,1)S(1)} %copy-done.2, ...), custom_call_target="tpu_custom_call" | custom-call | flops 1 | bytes 1 | tf_op jit(solution)/shard_map/expert/pallas_call | solution.py:87
  125.0 0.8 collective-permute-start.19
  125.8 2.8 %collective-permute-start.21 = (bf16[40,3712]{1,0:T(8,128)(2,1)S(1)}, bf16[40,3712]{1,0:T(8,128)(2,1)S(1)}, u32[]{:S(2)}, u32[]{:S(2)}) collective-permute-start(bf16[40,3712]{1,0:T(8,128)(2,1)S(1)} %get-tuple-element.121), channel_id=1, source_target_pairs={{0,6},{2,4},{4,2},{6,0},{8,14},{10,12},{12,10},{14,8},{1,7},{3,5},... | collective-permute-start | bytes 890888 | tf_op jit(solution)/shard_map/ppermute | solution.py:118
  128.5 2.1 %collective-permute-done.16 = bf16[40,3712]{1,0:T(8,128)(2,1)S(1)} collective-permute-done((bf16[40,3712]{1,0:T(8,128)(2,1)S(1)}, bf16[40,3712]{1,0:T(8,128)(2,1)S(1)}, u32[]{:S(2)}, u32[]{:S(2)}) %collective-permute-start.16) | collective-permute-done | bytes 296992 | tf_op jit(solution)/shard_map/ppermute | solution.py:118
  131.3 1.5 collective-permute-start.17
  133.6 20.4 %collective-permute-done.17 = bf16[40,3712]{1,0:T(8,128)(2,1)S(1)} collective-permute-done((bf16[40,3712]{1,0:T(8,128)(2,1)S(1)}, bf16[40,3712]{1,0:T(8,128)(2,1)S(1)}, u32[]{:S(2)}, u32[]{:S(2)}) %collective-permute-start.17) | collective-permute-done | bytes 296992 | tf_op jit(solution)/shard_map/ppermute | solution.py:118
  154.1 5.2 %collective-permute-done.18 = bf16[40,3712]{1,0:T(8,128)(2,1)S(1)} collective-permute-done((bf16[40,3712]{1,0:T(8,128)(2,1)S(1)}, bf16[40,3712]{1,0:T(8,128)(2,1)S(1)}, u32[]{:S(2)}, u32[]{:S(2)}) %collective-permute-start.18) | collective-permute-done | bytes 296992 | tf_op jit(solution)/shard_map/ppermute | solution.py:118
  160.1 1.5 fusion.1
  (76 shorter events, 7.3 us)
Async XLA Ops:
  0.6 9.2 %collective-permute-start.2 = (bf16[1,3584,512]{2,1,0:T(8,128)(2,1)}, bf16[1,3584,512]{2,1,0:T(8,128)(2,1)}, u32[]{:S(2)}, u32[]{:S(2)}) collective-permute-start(bf16[1,3584,512]{2,1,0:T(8,128)(2,1)} %refs_0_.5), channel_id=1, source_target_pairs={{0,1},{1,0},{2,3},{3,2},{4,5},{5,4},{6,7},{7,6},{8,9},{9,8},{10,11... | collective-permute-start | bytes 11010056 | tf_op jit(solution)/shard_map/ppermute | solution.py:30
  0.7 12.0 %collective-permute-start.3 = (bf16[1,3584,512]{2,1,0:T(8,128)(2,1)}, bf16[1,3584,512]{2,1,0:T(8,128)(2,1)}, u32[]{:S(2)}, u32[]{:S(2)}) collective-permute-start(bf16[1,3584,512]{2,1,0:T(8,128)(2,1)} %refs_1_.3), channel_id=1, source_target_pairs={{0,1},{1,0},{2,3},{3,2},{4,5},{5,4},{6,7},{7,6},{8,9},{9,8},{10,11... | collective-permute-start | bytes 11010056 | tf_op jit(solution)/shard_map/ppermute | solution.py:30
  1.2 16.7 %collective-permute-start.4 = (bf16[1,512,3584]{2,1,0:T(8,128)(2,1)}, bf16[1,512,3584]{2,1,0:T(8,128)(2,1)}, u32[]{:S(2)}, u32[]{:S(2)}) collective-permute-start(bf16[1,512,3584]{2,1,0:T(8,128)(2,1)} %refs_2_.1), channel_id=1, source_target_pairs={{0,1},{1,0},{2,3},{3,2},{4,5},{5,4},{6,7},{7,6},{8,9},{9,8},{10,11... | collective-permute-start | bytes 11010056 | tf_op jit(solution)/shard_map/ppermute | solution.py:30
  1.3 42.7 %collective-permute-start = (bf16[128,3584]{1,0:T(8,128)(2,1)}, bf16[128,3584]{1,0:T(8,128)(2,1)S(1)}, u32[]{:S(2)}, u32[]{:S(2)}) collective-permute-start(bf16[128,3584]{1,0:T(8,128)(2,1)} %refs_0_.3), channel_id=1, source_target_pairs={{0,8},{2,10},{4,12},{6,14},{8,0},{10,2},{12,4},{14,6},{1,9},{3,11}... | collective-permute-start | bytes 2752520 | tf_op jit(solution)/shard_map/ppermute | solution.py:118
  5.7 1.2 copy-start.3
  6.9 1.2 copy-start.4
  9.2 34.8 %collective-permute-start.6 = (bf16[2,40,3584]{2,1,0:T(8,128)(2,1)S(1)}, bf16[2,40,3584]{2,1,0:T(8,128)(2,1)S(1)}, u32[]{:S(2)}, u32[]{:S(2)}) collective-permute-start(bf16[2,40,3584]{2,1,0:T(8,128)(2,1)S(1)} %get-tuple-element.68), channel_id=1, source_target_pairs={{0,4},{2,6},{4,0},{6,2},{8,12},{10,14},{12,8},{14,10},{1,5},{3,7},... | collective-permute-start | bytes 1720328 | tf_op jit(solution)/shard_map/ppermute | solution.py:118
  17.9 26.1 %collective-permute-start.7 = (bf16[2,40,3584]{2,1,0:T(8,128)(2,1)S(1)}, bf16[2,40,3584]{2,1,0:T(8,128)(2,1)S(1)}, u32[]{:S(2)}, u32[]{:S(2)}) collective-permute-start(bf16[2,40,3584]{2,1,0:T(8,128)(2,1)S(1)} %get-tuple-element.70), channel_id=1, source_target_pairs={{0,2},{2,0},{4,6},{6,4},{8,10},{10,8},{12,14},{14,12},{1,3},{3,1},... | collective-permute-start | bytes 1720328 | tf_op jit(solution)/shard_map/ppermute | solution.py:118
  19.5 24.5 %collective-permute-start.5 = (s32[2,128]{1,0:T(2,128)S(1)}, s32[2,128]{1,0:T(2,128)S(1)}, u32[]{:S(2)}, u32[]{:S(2)}) collective-permute-start(s32[2,128]{1,0:T(2,128)S(1)} %add_bitcast_fusion.1.index_ref), channel_id=1, source_target_pairs={{0,8},{2,10},{4,12},{6,14},{8,0},{10,2},{12,4},{14,6},{1,9},{3,11}... | collective-permute-start | bytes 3080 | tf_op jit(solution)/shard_map/ppermute | solution.py:118
  44.0 31.9 %collective-permute-start.12 = (bf16[2,40,3584]{2,1,0:T(8,128)(2,1)S(1)}, bf16[2,40,3584]{2,1,0:T(8,128)(2,1)S(1)}, u32[]{:S(2)}, u32[]{:S(2)}) collective-permute-start(bf16[2,40,3584]{2,1,0:T(8,128)(2,1)S(1)} %get-tuple-element.89), channel_id=1, source_target_pairs={{0,6},{2,4},{4,2},{6,0},{8,14},{10,12},{12,10},{14,8},{1,7},{3,5},... | collective-permute-start | bytes 1720328 | tf_op jit(solution)/shard_map/ppermute | solution.py:118
  46.3 21.1 %collective-permute-start.1 = (bf16[40,3584]{1,0:T(8,128)(2,1)S(1)}, bf16[40,3584]{1,0:T(8,128)(2,1)S(1)}, u32[]{:S(2)}, u32[]{:S(2)}) collective-permute-start(bf16[40,3584]{1,0:T(8,128)(2,1)S(1)} %bitcast.73), channel_id=1, source_target_pairs={{0,8},{2,10},{4,12},{6,14},{8,0},{10,2},{12,4},{14,6},{1,9},{3,11}... | collective-permute-start | bytes 860168 | tf_op jit(solution)/shard_map/ppermute | solution.py:118
  47.5 26.4 %collective-permute-start.8 = (bf16[40,3584]{1,0:T(8,128)(2,1)S(1)}, bf16[40,3584]{1,0:T(8,128)(2,1)S(1)}, u32[]{:S(2)}, u32[]{:S(2)}) collective-permute-start(bf16[40,3584]{1,0:T(8,128)(2,1)S(1)} %bitcast.72), channel_id=1, source_target_pairs={{0,10},{2,8},{4,14},{6,12},{8,2},{10,0},{12,6},{14,4},{1,11},{3,9}... | collective-permute-start | bytes 860168 | tf_op jit(solution)/shard_map/ppermute | solution.py:118
  49.2 31.6 %copy-start.1 = (bf16[1,3584,512]{2,1,0:T(8,128)(2,1)S(1)}, bf16[1,3584,512]{2,1,0:T(8,128)(2,1)}, u32[]{:S(2)}) copy-start(bf16[1,3584,512]{2,1,0:T(8,128)(2,1)} %refs_1_.3) | copy-start | bytes 11010052
  49.9 26.0 %collective-permute-start.11 = (bf16[40,3584]{1,0:T(8,128)(2,1)S(1)}, bf16[40,3584]{1,0:T(8,128)(2,1)S(1)}, u32[]{:S(2)}, u32[]{:S(2)}) collective-permute-start(bf16[40,3584]{1,0:T(8,128)(2,1)S(1)} %bitcast.74), channel_id=1, source_target_pairs={{0,2},{2,0},{4,6},{6,4},{8,10},{10,8},{12,14},{14,12},{1,3},{3,1},... | collective-permute-start | bytes 860168 | tf_op jit(solution)/shard_map/ppermute | solution.py:118
  73.9 28.2 %collective-permute-start.9 = (bf16[40,3584]{1,0:T(8,128)(2,1)S(1)}, bf16[40,3584]{1,0:T(8,128)(2,1)S(1)}, u32[]{:S(2)}, u32[]{:S(2)}) collective-permute-start(bf16[40,3584]{1,0:T(8,128)(2,1)S(1)} %bitcast.69), channel_id=1, source_target_pairs={{0,12},{2,14},{4,8},{6,10},{8,4},{10,6},{12,0},{14,2},{1,13},{3,15... | collective-permute-start | bytes 860168 | tf_op jit(solution)/shard_map/ppermute | solution.py:118
  73.9 30.5 %collective-permute-start.10 = (bf16[40,3584]{1,0:T(8,128)(2,1)S(1)}, bf16[40,3584]{1,0:T(8,128)(2,1)S(1)}, u32[]{:S(2)}, u32[]{:S(2)}) collective-permute-start(bf16[40,3584]{1,0:T(8,128)(2,1)S(1)} %bitcast.68), channel_id=1, source_target_pairs={{0,14},{2,12},{4,10},{6,8},{8,6},{10,4},{12,2},{14,0},{1,15},{3,13... | collective-permute-start | bytes 860168 | tf_op jit(solution)/shard_map/ppermute | solution.py:118
  75.9 28.5 %collective-permute-start.13 = (bf16[40,3584]{1,0:T(8,128)(2,1)S(1)}, bf16[40,3584]{1,0:T(8,128)(2,1)S(1)}, u32[]{:S(2)}, u32[]{:S(2)}) collective-permute-start(bf16[40,3584]{1,0:T(8,128)(2,1)S(1)} %bitcast.71), channel_id=1, source_target_pairs={{0,4},{2,6},{4,0},{6,2},{8,12},{10,14},{12,8},{14,10},{1,5},{3,7},... | collective-permute-start | bytes 860168 | tf_op jit(solution)/shard_map/ppermute | solution.py:118
  80.5 26.0 %collective-permute-start.14 = (bf16[40,3584]{1,0:T(8,128)(2,1)S(1)}, bf16[40,3584]{1,0:T(8,128)(2,1)S(1)}, u32[]{:S(2)}, u32[]{:S(2)}) collective-permute-start(bf16[40,3584]{1,0:T(8,128)(2,1)S(1)} %bitcast.70), channel_id=1, source_target_pairs={{0,6},{2,4},{4,2},{6,0},{8,14},{10,12},{12,10},{14,8},{1,7},{3,5},... | collective-permute-start | bytes 860168 | tf_op jit(solution)/shard_map/ppermute | solution.py:118
  80.6 2.0 %copy-start = (bf16[1,3584,512]{2,1,0:T(8,128)(2,1)S(1)}, bf16[1,3584,512]{2,1,0:T(8,128)(2,1)}, u32[]{:S(2)}) copy-start(bf16[1,3584,512]{2,1,0:T(8,128)(2,1)} %refs_0_.5) | copy-start | bytes 11010052
  82.7 2.0 %copy-start.2 = (bf16[1,512,3584]{2,1,0:T(8,128)(2,1)S(1)}, bf16[1,512,3584]{2,1,0:T(8,128)(2,1)}, u32[]{:S(2)}) copy-start(bf16[1,512,3584]{2,1,0:T(8,128)(2,1)} %refs_2_.1) | copy-start | bytes 11010052
  106.5 22.0 %collective-permute-start.15 = (bf16[40,3712]{1,0:T(8,128)(2,1)S(1)}, bf16[40,3712]{1,0:T(8,128)(2,1)S(1)}, u32[]{:S(2)}, u32[]{:S(2)}) collective-permute-start(bf16[40,3712]{1,0:T(8,128)(2,1)S(1)} %get-tuple-element.108), channel_id=1, source_target_pairs={{0,8},{2,10},{4,12},{6,14},{8,0},{10,2},{12,4},{14,6},{1,9},{3,11}... | collective-permute-start | bytes 890888 | tf_op jit(solution)/shard_map/ppermute | solution.py:118
  106.6 24.0 %collective-permute-start.16 = (bf16[40,3712]{1,0:T(8,128)(2,1)S(1)}, bf16[40,3712]{1,0:T(8,128)(2,1)S(1)}, u32[]{:S(2)}, u32[]{:S(2)}) collective-permute-start(bf16[40,3712]{1,0:T(8,128)(2,1)S(1)} %get-tuple-element.109), channel_id=1, source_target_pairs={{0,10},{2,8},{4,14},{6,12},{8,2},{10,0},{12,6},{14,4},{1,11},{3,9}... | collective-permute-start | bytes 890888 | tf_op jit(solution)/shard_map/ppermute | solution.py:118
  124.9 5.9 %copy-start.5 = (f32[128,2]{0,1:T(2,128)S(1)}, f32[128,2]{0,1:T(2,128)}, u32[]{:S(2)}) copy-start(f32[128,2]{0,1:T(2,128)} %param.10) | copy-start | bytes 3076
  125.0 34.3 %collective-permute-start.19 = (bf16[40,3712]{1,0:T(8,128)(2,1)S(1)}, bf16[40,3712]{1,0:T(8,128)(2,1)S(1)}, u32[]{:S(2)}, u32[]{:S(2)}) collective-permute-start(bf16[40,3712]{1,0:T(8,128)(2,1)S(1)} %get-tuple-element.119), channel_id=1, source_target_pairs={{0,2},{2,0},{4,6},{6,4},{8,10},{10,8},{12,14},{14,12},{1,3},{3,1},... | collective-permute-start | bytes 890888 | tf_op jit(solution)/shard_map/ppermute | solution.py:118
  125.8 33.6 %collective-permute-start.20 = (bf16[40,3712]{1,0:T(8,128)(2,1)S(1)}, bf16[40,3712]{1,0:T(8,128)(2,1)S(1)}, u32[]{:S(2)}, u32[]{:S(2)}) collective-permute-start(bf16[40,3712]{1,0:T(8,128)(2,1)S(1)} %get-tuple-element.120), channel_id=1, source_target_pairs={{0,4},{2,6},{4,0},{6,2},{8,12},{10,14},{12,8},{14,10},{1,5},{3,7},... | collective-permute-start | bytes 890888 | tf_op jit(solution)/shard_map/ppermute | solution.py:118
  125.8 33.6 %collective-permute-start.21 = (bf16[40,3712]{1,0:T(8,128)(2,1)S(1)}, bf16[40,3712]{1,0:T(8,128)(2,1)S(1)}, u32[]{:S(2)}, u32[]{:S(2)}) collective-permute-start(bf16[40,3712]{1,0:T(8,128)(2,1)S(1)} %get-tuple-element.121), channel_id=1, source_target_pairs={{0,6},{2,4},{4,2},{6,0},{8,14},{10,12},{12,10},{14,8},{1,7},{3,5},... | collective-permute-start | bytes 890888 | tf_op jit(solution)/shard_map/ppermute | solution.py:118
  131.3 22.8 %collective-permute-start.17 = (bf16[40,3712]{1,0:T(8,128)(2,1)S(1)}, bf16[40,3712]{1,0:T(8,128)(2,1)S(1)}, u32[]{:S(2)}, u32[]{:S(2)}) collective-permute-start(bf16[40,3712]{1,0:T(8,128)(2,1)S(1)} %get-tuple-element.116), channel_id=1, source_target_pairs={{0,12},{2,14},{4,8},{6,10},{8,4},{10,6},{12,0},{14,2},{1,13},{3,15... | collective-permute-start | bytes 890888 | tf_op jit(solution)/shard_map/ppermute | solution.py:118
  132.8 26.4 %collective-permute-start.18 = (bf16[40,3712]{1,0:T(8,128)(2,1)S(1)}, bf16[40,3712]{1,0:T(8,128)(2,1)S(1)}, u32[]{:S(2)}, u32[]{:S(2)}) collective-permute-start(bf16[40,3712]{1,0:T(8,128)(2,1)S(1)} %get-tuple-element.117), channel_id=1, source_target_pairs={{0,14},{2,12},{4,10},{6,8},{8,6},{10,4},{12,2},{14,0},{1,15},{3,13... | collective-permute-start | bytes 890888 | tf_op jit(solution)/shard_map/ppermute | solution.py:118

commit v4 on v3

--- a/solution.py
+++ b/solution.py
@@ -58,7 +58,7 @@
 
 
 def expert_kernel(tile, tokens_ref, upstream_ref, *refs):
-    pieces, (out_ref, total, part) = (refs[:3], refs[3:6]), refs[6:]
+    pieces, out_refs, (total, part) = (refs[:3], refs[3:6]), refs[6:-2], refs[-2:]
     width = tokens_ref.shape[1]
     total[...] = jnp.zeros_like(total)
     part[...] = jnp.zeros_like(part)
@@ -78,17 +78,20 @@
             d_gate = (projected * up_lin * slope).astype(BF16)
             d_up = (projected * activated).astype(BF16)
             total[...] += nt(d_gate, gate_piece) + nt(d_up, up_piece)
-    out_ref[:, :width] = total[...].astype(BF16)
-    out_ref[:, width:] = jnp.broadcast_to(part[...], (part.shape[0], LANES)).astype(BF16)
-
-
-def expert(tokens, upstream, own, other):
+    for place, out_ref in enumerate(out_refs):
+        count = out_ref.shape[0]
+        rows = slice(place * count, (place + 1) * count)
+        out_ref[:, :width] = total[rows, :].astype(BF16)
+        out_ref[:, width:] = jnp.broadcast_to(part[rows, :], (count, LANES)).astype(BF16)
+
+
+def expert(tokens, upstream, own, other, blocks):
     rows, width = tokens.shape
     return pl.pallas_call(
         functools.partial(expert_kernel, min(256, own[0].shape[2])),
-        out_shape=jax.ShapeDtypeStruct((rows, width + LANES), BF16),
+        out_shape=[jax.ShapeDtypeStruct((rows // blocks, width + LANES), BF16)] * blocks,
         in_specs=[VMEM] * 8,
-        out_specs=VMEM,
+        out_specs=[VMEM] * blocks,
         scratch_shapes=[pltpu.VMEM((rows, width), F32), pltpu.VMEM((rows, 1), F32)],
         compiler_params=pltpu.CompilerParams(vmem_limit_bytes=38 << 20),
         cost_estimate=SMALL,
@@ -120,8 +123,10 @@
         ]
 
     def work(got_tokens, got_upstream, weights):
-        out = expert(jnp.concatenate(got_tokens), jnp.concatenate(got_upstream), *weights)
-        return [out[i * capacity : (i + 1) * capacity] for i in range(len(got_tokens))]
+        blocks = len(got_tokens)
+        return expert(
+            jnp.concatenate(got_tokens), jnp.concatenate(got_upstream), *weights, blocks
+        )
 
     def combine(back, offsets):
         rows = jnp.arange(capacity, dtype=jnp.int32)
@@ -168,10 +173,8 @@
     got_cross += move(sent_last, cross[cut:])
     up_far1, sent_far = tie((up_far1, sent_far))
     up_far2 = move(sent_far, far2)
-    up_far1, pass_far1, got_side, got_cross, passed = tie(
-        (up_far1, pass_far1, got_side, got_cross, passed[len(far1) :])
-    )
-    pass_far2 = move(passed, cross)
+    pass_far2 = move(passed[len(far1) :], cross)
+    up_far1, pass_far1, got_side, got_cross = tie((up_far1, pass_far1, got_side, got_cross))
     got = got_side + got_cross
     first = work(
         pass_far1 + [rows[0] for rows in got], up_far1 + [rows[1] for rows in got], weights
@@ -180,10 +183,11 @@
     back_far1 = move(first[: len(far1)], far1)
     back_near = move(first[len(far1) :], near)
     second = work(pass_far2, up_far2, weights)
-    back_far1, second = tie((back_far1, second))
+    second, back_first = tie((second, back_far1[0]))
+    back_far1 = [back_first] + back_far1[1:]
     back_far2 = move(second, far2)
-    early, gate_early = combine(back_far1, far1)
-    late, gate_late = combine(back_far2 + back_near, far2 + near)
+    early, gate_early = combine(back_far1 + back_near, far1 + near)
+    late, gate_late = combine(back_far2, far2)
     return (early + late).astype(BF16), gate_early + gate_late
 
 

time: 162 us -> 157 us (0.969)
  starting transfers between devices: 30.5 us -> 25.4 us
    ppermute x19, starting transfers between devices: 29.8 us -> 24.8 us  [move(): lax.ppermute(rows, CHIPS, [(i, i ^ offset) for i in range(chips)])]
    unnamed x24 -> x26, local copies, waits for them, and re-layouts: 6.59 us -> 6.62 us
  transfers between devices with their start and end apart: 22 -> 22, of which waited for: 10 -> 10; matrix products, arithmetic and copies ran while one was open for 2% -> 2% of each run, Pallas kernels for 21% -> 22%
where the time goes in v4:
time: 157 us
  waiting for transfers between devices  83.7 us (53%)
  Pallas kernels  34 us (22%)
  starting transfers between devices  25.4 us (16%)
  local copies, waits for them, and re-layouts  6.86 us (4%)
  other arithmetic  3.21 us (2%)
  matrix products  2.78 us (2%)
    ppermute x19, waiting for transfers between devices, move(): lax.ppermute(rows, CHIPS, [(i, i ^ offset) for i in range(chips)])  75.6 us
    pallas_call x2, Pallas kernels, expert(): pl.pallas_call(functools.partial(expert_kernel, min(256, own[0].shape[2])...  31.7 us
    ppermute x19, starting transfers between devices, move(): lax.ppermute(rows, CHIPS, [(i, i ^ offset) for i in range(chips)])  24.8 us
    ppermute x3, waiting for transfers between devices, swap_cores(): return lax.ppermute(values, 'core', [(0, 1), (1, 0)])  8.08 us
    unnamed x26, local copies, waits for them, and re-layouts  6.62 us
  transfers between devices with their start and end apart: 22, of which 10 were waited for; matrix products, arithmetic and copies ran while one was open for 2% of the time, Pallas kernels for 22%

profile of v4, /device:TPU:8, one launch (start us, length us, event | category | flops | bytes accessed | tf_op | source)
XLA Modules:
  0.0 156.9 jit_solution(15057136246837454249)
XLA Ops:
  1.3 2.6 %collective-permute-start = (bf16[128,3584]{1,0:T(8,128)(2,1)}, bf16[128,3584]{1,0:T(8,128)(2,1)S(1)}, u32[]{:S(2)}, u32[]{:S(2)}) collective-permute-start(bf16[128,3584]{1,0:T(8,128)(2,1)} %refs_0_.3), channel_id=1, source_target_pairs={{0,8},{2,10},{4,12},{6,14},{8,0},{10,2},{12,4},{14,6},{1,9},{3,11}... | collective-permute-start | bytes 2752520 | tf_op jit(solution)/shard_map/ppermute | solution.py:121
  3.9 0.7 convert_reduce_fusion.2
  4.9 0.8 select_reduce_fusion.5
  5.7 1.2 copy-done.4
  6.9 1.2 copy-done.5
  8.1 1.1 dispatch.4
  9.9 2.8 %collective-permute-done.3.refs_4_ = bf16[1,3584,512]{2,1,0:T(8,128)(2,1)} collective-permute-done((bf16[1,3584,512]{2,1,0:T(8,128)(2,1)}, bf16[1,3584,512]{2,1,0:T(8,128)(2,1)}, u32[]{:S(2)}, u32[]{:S(2)}) %collective-permute-start.3) | collective-permute-done | bytes 3670048 | tf_op jit(solution)/shard_map/ppermute | solution.py:30
  12.7 5.2 %collective-permute-done.4.refs_5_ = bf16[1,512,3584]{2,1,0:T(8,128)(2,1)} collective-permute-done((bf16[1,512,3584]{2,1,0:T(8,128)(2,1)}, bf16[1,512,3584]{2,1,0:T(8,128)(2,1)}, u32[]{:S(2)}, u32[]{:S(2)}) %collective-permute-start.4) | collective-permute-done | bytes 3670048 | tf_op jit(solution)/shard_map/ppermute | solution.py:30
  17.9 1.5 collective-permute-start.7
  19.5 2.7 %collective-permute-start.5 = (s32[2,128]{1,0:T(2,128)S(1)}, s32[2,128]{1,0:T(2,128)S(1)}, u32[]{:S(2)}, u32[]{:S(2)}) collective-permute-start(s32[2,128]{1,0:T(2,128)S(1)} %add_bitcast_fusion.1.index_ref), channel_id=1, source_target_pairs={{0,8},{2,10},{4,12},{6,14},{8,0},{10,2},{12,4},{14,6},{1,9},{3,11}... | collective-permute-start | bytes 3080 | tf_op jit(solution)/shard_map/ppermute | solution.py:121
  22.8 21.2 %collective-permute-done.refs_0_ = bf16[128,3584]{1,0:T(8,128)(2,1)S(1)} collective-permute-done((bf16[128,3584]{1,0:T(8,128)(2,1)}, bf16[128,3584]{1,0:T(8,128)(2,1)S(1)}, u32[]{:S(2)}, u32[]{:S(2)}) %collective-permute-start) | collective-permute-done | bytes 917536 | tf_op jit(solution)/shard_map/ppermute | solution.py:121
  44.0 2.2 %collective-permute-start.14 = (bf16[2,40,3584]{2,1,0:T(8,128)(2,1)S(1)}, bf16[2,40,3584]{2,1,0:T(8,128)(2,1)S(1)}, u32[]{:S(2)}, u32[]{:S(2)}) collective-permute-start(bf16[2,40,3584]{2,1,0:T(8,128)(2,1)S(1)} %get-tuple-element.96), channel_id=1, source_target_pairs={{0,6},{2,4},{4,2},{6,0},{8,14},{10,12},{12,10},{14,8},{1,7},{3,5},... | collective-permute-start | bytes 1720328 | tf_op jit(solution)/shard_map/ppermute | solution.py:121
  46.3 1.2 collective-permute-start.1
  47.5 1.7 %collective-permute-start.8 = (bf16[40,3584]{1,0:T(8,128)(2,1)S(1)}, bf16[40,3584]{1,0:T(8,128)(2,1)S(1)}, u32[]{:S(2)}, u32[]{:S(2)}) collective-permute-start(bf16[40,3584]{1,0:T(8,128)(2,1)S(1)} %bitcast.72), channel_id=1, source_target_pairs={{0,10},{2,8},{4,14},{6,12},{8,2},{10,0},{12,6},{14,4},{1,11},{3,9}... | collective-permute-start | bytes 860168 | tf_op jit(solution)/shard_map/ppermute | solution.py:121
  49.2 0.6 dispatch.5
  49.9 1.6 %collective-permute-start.13 = (bf16[40,3584]{1,0:T(8,128)(2,1)S(1)}, bf16[40,3584]{1,0:T(8,128)(2,1)S(1)}, u32[]{:S(2)}, u32[]{:S(2)}) collective-permute-start(bf16[40,3584]{1,0:T(8,128)(2,1)S(1)} %bitcast.74), channel_id=1, source_target_pairs={{0,2},{2,0},{4,6},{6,4},{8,10},{10,8},{12,14},{14,12},{1,3},{3,1},... | collective-permute-start | bytes 860168 | tf_op jit(solution)/shard_map/ppermute | solution.py:121
  51.6 1.3 collective-permute-start.11
  52.8 14.6 %collective-permute-done.1 = bf16[40,3584]{1,0:T(8,128)(2,1)S(1)} collective-permute-done((bf16[40,3584]{1,0:T(8,128)(2,1)S(1)}, bf16[40,3584]{1,0:T(8,128)(2,1)S(1)}, u32[]{:S(2)}, u32[]{:S(2)}) %collective-permute-start.1) | collective-permute-done | bytes 286752 | tf_op jit(solution)/shard_map/ppermute | solution.py:121
  67.4 7.0 %collective-permute-done.8 = bf16[40,3584]{1,0:T(8,128)(2,1)S(1)} collective-permute-done((bf16[40,3584]{1,0:T(8,128)(2,1)S(1)}, bf16[40,3584]{1,0:T(8,128)(2,1)S(1)}, u32[]{:S(2)}, u32[]{:S(2)}) %collective-permute-start.8) | collective-permute-done | bytes 286752 | tf_op jit(solution)/shard_map/ppermute | solution.py:121
  74.7 1.7 %collective-permute-start.10 = (bf16[40,3584]{1,0:T(8,128)(2,1)S(1)}, bf16[40,3584]{1,0:T(8,128)(2,1)S(1)}, u32[]{:S(2)}, u32[]{:S(2)}) collective-permute-start(bf16[40,3584]{1,0:T(8,128)(2,1)S(1)} %bitcast.68), channel_id=1, source_target_pairs={{0,14},{2,12},{4,10},{6,8},{8,6},{10,4},{12,2},{14,0},{1,15},{3,13... | collective-permute-start | bytes 860168 | tf_op jit(solution)/shard_map/ppermute | solution.py:121
  76.8 1.8 %copy-done = bf16[1,3584,512]{2,1,0:T(8,128)(2,1)S(1)} copy-done((bf16[1,3584,512]{2,1,0:T(8,128)(2,1)S(1)}, bf16[1,3584,512]{2,1,0:T(8,128)(2,1)}, u32[]{:S(2)}) %copy-start) | copy-done | bytes 3670040
  78.6 2.0 %copy-done.2 = bf16[1,512,3584]{2,1,0:T(8,128)(2,1)S(1)} copy-done((bf16[1,512,3584]{2,1,0:T(8,128)(2,1)S(1)}, bf16[1,512,3584]{2,1,0:T(8,128)(2,1)}, u32[]{:S(2)}) %copy-start.2) | copy-done | bytes 3670040
  80.6 17.1 %expert.2 = (bf16[40,3712]{1,0:T(8,128)(2,1)S(1)}, bf16[40,3712]{1,0:T(8,128)(2,1)S(1)}, bf16[40,3712]{1,0:T(8,128)(2,1)S(1)}, bf16[40,3712]{1,0:T(8,128)(2,1)S(...) custom-call(bf16[240,3584]{1,0:T(8,128)(2,1)S(1)} %get-tuple-element.139.tokens_ref, ...), custom_call_target="tpu_custom_call" | custom-call | flops 1 | bytes 1 | tf_op jit(solution)/shard_map/expert/pallas_call | solution.py:90
  97.8 11.6 %collective-permute-done.10 = bf16[40,3584]{1,0:T(8,128)(2,1)S(1)} collective-permute-done((bf16[40,3584]{1,0:T(8,128)(2,1)S(1)}, bf16[40,3584]{1,0:T(8,128)(2,1)S(1)}, u32[]{:S(2)}, u32[]{:S(2)}) %collective-permute-start.10) | collective-permute-done | bytes 286752 | tf_op jit(solution)/shard_map/ppermute | solution.py:121
  109.3 3.9 %collective-permute-start.16 = (bf16[40,3712]{1,0:T(8,128)(2,1)S(1)}, bf16[40,3712]{1,0:T(8,128)(2,1)S(1)}, u32[]{:S(2)}, u32[]{:S(2)}) collective-permute-start(bf16[40,3712]{1,0:T(8,128)(2,1)S(1)} %get-tuple-element.125), channel_id=1, source_target_pairs={{0,10},{2,8},{4,14},{6,12},{8,2},{10,0},{12,6},{14,4},{1,11},{3,9}... | collective-permute-start | bytes 890888 | tf_op jit(solution)/shard_map/ppermute | solution.py:121
  113.8 3.0 %collective-permute-start.19 = (bf16[40,3712]{1,0:T(8,128)(2,1)S(1)}, bf16[40,3712]{1,0:T(8,128)(2,1)S(1)}, u32[]{:S(2)}, u32[]{:S(2)}) collective-permute-start(bf16[40,3712]{1,0:T(8,128)(2,1)S(1)} %get-tuple-element.129), channel_id=1, source_target_pairs={{0,6},{2,4},{4,2},{6,0},{8,14},{10,12},{12,10},{14,8},{1,7},{3,5},... | collective-permute-start | bytes 890888 | tf_op jit(solution)/shard_map/ppermute | solution.py:121
  116.8 14.6 %expert.3 = (bf16[40,3712]{1,0:T(8,128)(2,1)S(1)}, bf16[40,3712]{1,0:T(8,128)(2,1)S(1)}) custom-call(bf16[80,3584]{1,0:T(8,128)(2,1)S(1)} %pad_maximum_fusion.tokens_ref, bf16[80,3584]{1,0:T(8,128)(2,1)S(1)} %pad_maximum_fusion.1.upstream_ref, bf16[1,3584,512]{2,1,0:T(8,128)(2,1)S(1)} %copy-done, bf16[1,3584,512]{2,1,0:T(8,128)(2,1)S(1)} %copy-done.1, ...), custom_call_target="tpu_custom_call" | custom-call | flops 1 | bytes 1 | tf_op jit(solution)/shard_map/expert/pallas_call | solution.py:90
  131.5 7.6 %collective-permute-done.16 = bf16[40,3712]{1,0:T(8,128)(2,1)S(1)} collective-permute-done((bf16[40,3712]{1,0:T(8,128)(2,1)S(1)}, bf16[40,3712]{1,0:T(8,128)(2,1)S(1)}, u32[]{:S(2)}, u32[]{:S(2)}) %collective-permute-start.16) | collective-permute-done | bytes 296992 | tf_op jit(solution)/shard_map/ppermute | solution.py:121
  139.3 2.0 %collective-permute-done.19 = bf16[40,3712]{1,0:T(8,128)(2,1)S(1)} collective-permute-done((bf16[40,3712]{1,0:T(8,128)(2,1)S(1)}, bf16[40,3712]{1,0:T(8,128)(2,1)S(1)}, u32[]{:S(2)}, u32[]{:S(2)}) %collective-permute-start.19) | collective-permute-done | bytes 296992 | tf_op jit(solution)/shard_map/ppermute | solution.py:121
  141.9 3.6 %collective-permute-done.20 = bf16[40,3712]{1,0:T(8,128)(2,1)S(1)} collective-permute-done((bf16[40,3712]{1,0:T(8,128)(2,1)S(1)}, bf16[40,3712]{1,0:T(8,128)(2,1)S(1)}, u32[]{:S(2)}, u32[]{:S(2)}) %collective-permute-start.20) | collective-permute-done | bytes 296992 | tf_op jit(solution)/shard_map/ppermute | solution.py:121
  145.5 8.2 %collective-permute-done.21 = bf16[40,3712]{1,0:T(8,128)(2,1)S(1)} collective-permute-done((bf16[40,3712]{1,0:T(8,128)(2,1)S(1)}, bf16[40,3712]{1,0:T(8,128)(2,1)S(1)}, u32[]{:S(2)}, u32[]{:S(2)}) %collective-permute-start.21) | collective-permute-done | bytes 296992 | tf_op jit(solution)/shard_map/ppermute | solution.py:121
  154.8 1.5 fusion.1
  (76 shorter events, 6.3 us)
Async XLA Ops:
  0.6 9.2 %collective-permute-start.2 = (bf16[1,3584,512]{2,1,0:T(8,128)(2,1)}, bf16[1,3584,512]{2,1,0:T(8,128)(2,1)}, u32[]{:S(2)}, u32[]{:S(2)}) collective-permute-start(bf16[1,3584,512]{2,1,0:T(8,128)(2,1)} %refs_0_.5), channel_id=1, source_target_pairs={{0,1},{1,0},{2,3},{3,2},{4,5},{5,4},{6,7},{7,6},{8,9},{9,8},{10,11... | collective-permute-start | bytes 11010056 | tf_op jit(solution)/shard_map/ppermute | solution.py:30
  0.7 12.0 %collective-permute-start.3 = (bf16[1,3584,512]{2,1,0:T(8,128)(2,1)}, bf16[1,3584,512]{2,1,0:T(8,128)(2,1)}, u32[]{:S(2)}, u32[]{:S(2)}) collective-permute-start(bf16[1,3584,512]{2,1,0:T(8,128)(2,1)} %refs_1_.3), channel_id=1, source_target_pairs={{0,1},{1,0},{2,3},{3,2},{4,5},{5,4},{6,7},{7,6},{8,9},{9,8},{10,11... | collective-permute-start | bytes 11010056 | tf_op jit(solution)/shard_map/ppermute | solution.py:30
  1.2 16.7 %collective-permute-start.4 = (bf16[1,512,3584]{2,1,0:T(8,128)(2,1)}, bf16[1,512,3584]{2,1,0:T(8,128)(2,1)}, u32[]{:S(2)}, u32[]{:S(2)}) collective-permute-start(bf16[1,512,3584]{2,1,0:T(8,128)(2,1)} %refs_2_.1), channel_id=1, source_target_pairs={{0,1},{1,0},{2,3},{3,2},{4,5},{5,4},{6,7},{7,6},{8,9},{9,8},{10,11... | collective-permute-start | bytes 11010056 | tf_op jit(solution)/shard_map/ppermute | solution.py:30
  1.3 42.7 %collective-permute-start = (bf16[128,3584]{1,0:T(8,128)(2,1)}, bf16[128,3584]{1,0:T(8,128)(2,1)S(1)}, u32[]{:S(2)}, u32[]{:S(2)}) collective-permute-start(bf16[128,3584]{1,0:T(8,128)(2,1)} %refs_0_.3), channel_id=1, source_target_pairs={{0,8},{2,10},{4,12},{6,14},{8,0},{10,2},{12,4},{14,6},{1,9},{3,11}... | collective-permute-start | bytes 2752520 | tf_op jit(solution)/shard_map/ppermute | solution.py:121
  5.7 1.2 copy-start.4
  6.9 1.2 copy-start.5
  9.2 34.8 %collective-permute-start.6 = (bf16[2,40,3584]{2,1,0:T(8,128)(2,1)S(1)}, bf16[2,40,3584]{2,1,0:T(8,128)(2,1)S(1)}, u32[]{:S(2)}, u32[]{:S(2)}) collective-permute-start(bf16[2,40,3584]{2,1,0:T(8,128)(2,1)S(1)} %get-tuple-element.73), channel_id=1, source_target_pairs={{0,4},{2,6},{4,0},{6,2},{8,12},{10,14},{12,8},{14,10},{1,5},{3,7},... | collective-permute-start | bytes 1720328 | tf_op jit(solution)/shard_map/ppermute | solution.py:121
  17.9 26.1 %collective-permute-start.7 = (bf16[2,40,3584]{2,1,0:T(8,128)(2,1)S(1)}, bf16[2,40,3584]{2,1,0:T(8,128)(2,1)S(1)}, u32[]{:S(2)}, u32[]{:S(2)}) collective-permute-start(bf16[2,40,3584]{2,1,0:T(8,128)(2,1)S(1)} %get-tuple-element.75), channel_id=1, source_target_pairs={{0,2},{2,0},{4,6},{6,4},{8,10},{10,8},{12,14},{14,12},{1,3},{3,1},... | collective-permute-start | bytes 1720328 | tf_op jit(solution)/shard_map/ppermute | solution.py:121
  19.5 24.5 %collective-permute-start.5 = (s32[2,128]{1,0:T(2,128)S(1)}, s32[2,128]{1,0:T(2,128)S(1)}, u32[]{:S(2)}, u32[]{:S(2)}) collective-permute-start(s32[2,128]{1,0:T(2,128)S(1)} %add_bitcast_fusion.1.index_ref), channel_id=1, source_target_pairs={{0,8},{2,10},{4,12},{6,14},{8,0},{10,2},{12,4},{14,6},{1,9},{3,11}... | collective-permute-start | bytes 3080 | tf_op jit(solution)/shard_map/ppermute | solution.py:121
  44.0 32.4 %collective-permute-start.14 = (bf16[2,40,3584]{2,1,0:T(8,128)(2,1)S(1)}, bf16[2,40,3584]{2,1,0:T(8,128)(2,1)S(1)}, u32[]{:S(2)}, u32[]{:S(2)}) collective-permute-start(bf16[2,40,3584]{2,1,0:T(8,128)(2,1)S(1)} %get-tuple-element.96), channel_id=1, source_target_pairs={{0,6},{2,4},{4,2},{6,0},{8,14},{10,12},{12,10},{14,8},{1,7},{3,5},... | collective-permute-start | bytes 1720328 | tf_op jit(solution)/shard_map/ppermute | solution.py:121
  46.3 21.1 %collective-permute-start.1 = (bf16[40,3584]{1,0:T(8,128)(2,1)S(1)}, bf16[40,3584]{1,0:T(8,128)(2,1)S(1)}, u32[]{:S(2)}, u32[]{:S(2)}) collective-permute-start(bf16[40,3584]{1,0:T(8,128)(2,1)S(1)} %bitcast.73), channel_id=1, source_target_pairs={{0,8},{2,10},{4,12},{6,14},{8,0},{10,2},{12,4},{14,6},{1,9},{3,11}... | collective-permute-start | bytes 860168 | tf_op jit(solution)/shard_map/ppermute | solution.py:121
  47.5 26.9 %collective-permute-start.8 = (bf16[40,3584]{1,0:T(8,128)(2,1)S(1)}, bf16[40,3584]{1,0:T(8,128)(2,1)S(1)}, u32[]{:S(2)}, u32[]{:S(2)}) collective-permute-start(bf16[40,3584]{1,0:T(8,128)(2,1)S(1)} %bitcast.72), channel_id=1, source_target_pairs={{0,10},{2,8},{4,14},{6,12},{8,2},{10,0},{12,6},{14,4},{1,11},{3,9}... | collective-permute-start | bytes 860168 | tf_op jit(solution)/shard_map/ppermute | solution.py:121
  49.2 27.5 %copy-start.1 = (bf16[1,3584,512]{2,1,0:T(8,128)(2,1)S(1)}, bf16[1,3584,512]{2,1,0:T(8,128)(2,1)}, u32[]{:S(2)}) copy-start(bf16[1,3584,512]{2,1,0:T(8,128)(2,1)} %refs_1_.3) | copy-start | bytes 11010052
  49.9 24.8 %collective-permute-start.13 = (bf16[40,3584]{1,0:T(8,128)(2,1)S(1)}, bf16[40,3584]{1,0:T(8,128)(2,1)S(1)}, u32[]{:S(2)}, u32[]{:S(2)}) collective-permute-start(bf16[40,3584]{1,0:T(8,128)(2,1)S(1)} %bitcast.74), channel_id=1, source_target_pairs={{0,2},{2,0},{4,6},{6,4},{8,10},{10,8},{12,14},{14,12},{1,3},{3,1},... | collective-permute-start | bytes 860168 | tf_op jit(solution)/shard_map/ppermute | solution.py:121
  51.6 46.2 %collective-permute-start.11 = (bf16[40,3584]{1,0:T(8,128)(2,1)S(1)}, bf16[40,3584]{1,0:T(8,128)(2,1)S(1)}, u32[]{:S(2)}, u32[]{:S(2)}) collective-permute-start(bf16[40,3584]{1,0:T(8,128)(2,1)S(1)} %bitcast.71), channel_id=1, source_target_pairs={{0,4},{2,6},{4,0},{6,2},{8,12},{10,14},{12,8},{14,10},{1,5},{3,7},... | collective-permute-start | bytes 860168 | tf_op jit(solution)/shard_map/ppermute | solution.py:121
  67.4 30.3 %collective-permute-start.12 = (bf16[40,3584]{1,0:T(8,128)(2,1)S(1)}, bf16[40,3584]{1,0:T(8,128)(2,1)S(1)}, u32[]{:S(2)}, u32[]{:S(2)}) collective-permute-start(bf16[40,3584]{1,0:T(8,128)(2,1)S(1)} %bitcast.70), channel_id=1, source_target_pairs={{0,6},{2,4},{4,2},{6,0},{8,14},{10,12},{12,10},{14,8},{1,7},{3,5},... | collective-permute-start | bytes 860168 | tf_op jit(solution)/shard_map/ppermute | solution.py:121
  74.4 23.3 %collective-permute-start.9 = (bf16[40,3584]{1,0:T(8,128)(2,1)S(1)}, bf16[40,3584]{1,0:T(8,128)(2,1)S(1)}, u32[]{:S(2)}, u32[]{:S(2)}) collective-permute-start(bf16[40,3584]{1,0:T(8,128)(2,1)S(1)} %bitcast.69), channel_id=1, source_target_pairs={{0,12},{2,14},{4,8},{6,10},{8,4},{10,6},{12,0},{14,2},{1,13},{3,15... | collective-permute-start | bytes 860168 | tf_op jit(solution)/shard_map/ppermute | solution.py:121
  74.7 34.6 %collective-permute-start.10 = (bf16[40,3584]{1,0:T(8,128)(2,1)S(1)}, bf16[40,3584]{1,0:T(8,128)(2,1)S(1)}, u32[]{:S(2)}, u32[]{:S(2)}) collective-permute-start(bf16[40,3584]{1,0:T(8,128)(2,1)S(1)} %bitcast.68), channel_id=1, source_target_pairs={{0,14},{2,12},{4,10},{6,8},{8,6},{10,4},{12,2},{14,0},{1,15},{3,13... | collective-permute-start | bytes 860168 | tf_op jit(solution)/shard_map/ppermute | solution.py:121
  76.5 2.0 %copy-start = (bf16[1,3584,512]{2,1,0:T(8,128)(2,1)S(1)}, bf16[1,3584,512]{2,1,0:T(8,128)(2,1)}, u32[]{:S(2)}) copy-start(bf16[1,3584,512]{2,1,0:T(8,128)(2,1)} %refs_0_.5) | copy-start | bytes 11010052
  78.6 2.0 %copy-start.2 = (bf16[1,512,3584]{2,1,0:T(8,128)(2,1)S(1)}, bf16[1,512,3584]{2,1,0:T(8,128)(2,1)}, u32[]{:S(2)}) copy-start(bf16[1,512,3584]{2,1,0:T(8,128)(2,1)} %refs_2_.1) | copy-start | bytes 11010052
  80.6 36.2 %copy-start.3 = (bf16[1,512,3584]{2,1,0:T(8,128)(2,1)S(1)}, bf16[1,512,3584]{2,1,0:T(8,128)(2,1)}, u32[]{:S(2)}) copy-start(bf16[1,512,3584]{2,1,0:T(8,128)(2,1)} %refs_2_.1) | copy-start | bytes 11010052
  109.3 22.1 %collective-permute-start.15 = (bf16[40,3712]{1,0:T(8,128)(2,1)S(1)}, bf16[40,3712]{1,0:T(8,128)(2,1)S(1)}, u32[]{:S(2)}, u32[]{:S(2)}) collective-permute-start(bf16[40,3712]{1,0:T(8,128)(2,1)S(1)} %get-tuple-element.123), channel_id=1, source_target_pairs={{0,8},{2,10},{4,12},{6,14},{8,0},{10,2},{12,4},{14,6},{1,9},{3,11}... | collective-permute-start | bytes 890888 | tf_op jit(solution)/shard_map/ppermute | solution.py:121
  109.3 29.8 %collective-permute-start.16 = (bf16[40,3712]{1,0:T(8,128)(2,1)S(1)}, bf16[40,3712]{1,0:T(8,128)(2,1)S(1)}, u32[]{:S(2)}, u32[]{:S(2)}) collective-permute-start(bf16[40,3712]{1,0:T(8,128)(2,1)S(1)} %get-tuple-element.125), channel_id=1, source_target_pairs={{0,10},{2,8},{4,14},{6,12},{8,2},{10,0},{12,6},{14,4},{1,11},{3,9}... | collective-permute-start | bytes 890888 | tf_op jit(solution)/shard_map/ppermute | solution.py:121
  113.2 26.0 %collective-permute-start.17 = (bf16[40,3712]{1,0:T(8,128)(2,1)S(1)}, bf16[40,3712]{1,0:T(8,128)(2,1)S(1)}, u32[]{:S(2)}, u32[]{:S(2)}) collective-permute-start(bf16[40,3712]{1,0:T(8,128)(2,1)S(1)} %get-tuple-element.127), channel_id=1, source_target_pairs={{0,2},{2,0},{4,6},{6,4},{8,10},{10,8},{12,14},{14,12},{1,3},{3,1},... | collective-permute-start | bytes 890888 | tf_op jit(solution)/shard_map/ppermute | solution.py:121
  113.7 25.5 %collective-permute-start.18 = (bf16[40,3712]{1,0:T(8,128)(2,1)S(1)}, bf16[40,3712]{1,0:T(8,128)(2,1)S(1)}, u32[]{:S(2)}, u32[]{:S(2)}) collective-permute-start(bf16[40,3712]{1,0:T(8,128)(2,1)S(1)} %get-tuple-element.128), channel_id=1, source_target_pairs={{0,4},{2,6},{4,0},{6,2},{8,12},{10,14},{12,8},{14,10},{1,5},{3,7},... | collective-permute-start | bytes 890888 | tf_op jit(solution)/shard_map/ppermute | solution.py:121
  113.8 27.4 %collective-permute-start.19 = (bf16[40,3712]{1,0:T(8,128)(2,1)S(1)}, bf16[40,3712]{1,0:T(8,128)(2,1)S(1)}, u32[]{:S(2)}, u32[]{:S(2)}) collective-permute-start(bf16[40,3712]{1,0:T(8,128)(2,1)S(1)} %get-tuple-element.129), channel_id=1, source_target_pairs={{0,6},{2,4},{4,2},{6,0},{8,14},{10,12},{12,10},{14,8},{1,7},{3,5},... | collective-permute-start | bytes 890888 | tf_op jit(solution)/shard_map/ppermute | solution.py:121
  131.4 10.0 %copy-start.6 = (f32[128,2]{0,1:T(2,128)S(1)}, f32[128,2]{0,1:T(2,128)}, u32[]{:S(2)}) copy-start(f32[128,2]{0,1:T(2,128)} %param.10) | copy-start | bytes 3076
  131.4 14.1 %collective-permute-start.20 = (bf16[40,3712]{1,0:T(8,128)(2,1)S(1)}, bf16[40,3712]{1,0:T(8,128)(2,1)S(1)}, u32[]{:S(2)}, u32[]{:S(2)}) collective-permute-start(bf16[40,3712]{1,0:T(8,128)(2,1)S(1)} %get-tuple-element.130), channel_id=1, source_target_pairs={{0,12},{2,14},{4,8},{6,10},{8,4},{10,6},{12,0},{14,2},{1,13},{3,15... | collective-permute-start | bytes 890888 | tf_op jit(solution)/shard_map/ppermute | solution.py:121
  139.1 14.6 %collective-permute-start.21 = (bf16[40,3712]{1,0:T(8,128)(2,1)S(1)}, bf16[40,3712]{1,0:T(8,128)(2,1)S(1)}, u32[]{:S(2)}, u32[]{:S(2)}) collective-permute-start(bf16[40,3712]{1,0:T(8,128)(2,1)S(1)} %get-tuple-element.131), channel_id=1, source_target_pairs={{0,14},{2,12},{4,10},{6,8},{8,6},{10,4},{12,2},{14,0},{1,15},{3,13... | collective-permute-start | bytes 890888 | tf_op jit(solution)/shard_map/ppermute | solution.py:121

commit v5 on v4

--- a/solution.py
+++ b/solution.py
@@ -133,15 +133,12 @@
         hits = jnp.concatenate(
             [(rows + o * capacity)[:, None, None] == row_index[None] for o in offsets]
         )
-        weighted = jnp.sum(jnp.where(hits, gates.T[None], 0.0), axis=1).T
-        high = weighted.astype(BF16)
-        low = (weighted - high.astype(F32)).astype(BF16)
+        weighted = jnp.sum(jnp.where(hits, gates.T[None], 0.0), axis=1).T.astype(BF16)
         rows = jnp.concatenate(back)
         part = rows[:, width].astype(F32)
-        rows = rows[:, :width]
-        return nn(high, rows) + nn(low, rows), jnp.sum(
+        return nn(weighted, rows[:, :width]), jnp.sum(
             jnp.where(hits, part[:, None, None], 0.0), axis=0
-        ).T
+        )
 
     half = chips // 2
     near = list(range(half))
@@ -170,25 +167,30 @@
     sent_far = rest_up[len(far1) - cut :]
     passed = [rows[0] for rows in dispatch(mirror_index, [mirror_tokens], far1 + far2, capacity)]
     pass_far1 = move(passed[: len(far1)], side)
-    got_cross += move(sent_last, cross[cut:])
+    got_last = move(sent_last, cross[cut:])
+    got = got_side + got_cross
+    zero = work([rows[0] for rows in got], [rows[1] for rows in got], weights)
+    passed, zero = tie((passed[len(far1) :], zero))
+    pass_far2 = move(passed, cross)
+
     up_far1, sent_far = tie((up_far1, sent_far))
     up_far2 = move(sent_far, far2)
-    pass_far2 = move(passed[len(far1) :], cross)
-    up_far1, pass_far1, got_side, got_cross = tie((up_far1, pass_far1, got_side, got_cross))
-    got = got_side + got_cross
+    up_far1, pass_far1, got_last = tie((up_far1, pass_far1, got_last))
     first = work(
-        pass_far1 + [rows[0] for rows in got], up_far1 + [rows[1] for rows in got], weights
-    )
-    up_far2, pass_far2, first = tie((up_far2, pass_far2, first))
+        pass_far1 + [rows[0] for rows in got_last], up_far1 + [rows[1] for rows in got_last], weights
+    )
+    up_far2, pass_far2, later, zero = tie((up_far2, pass_far2, first, zero))
+    first = first[: len(far1)] + later[len(far1) :]
+
     back_far1 = move(first[: len(far1)], far1)
-    back_near = move(first[len(far1) :], near)
+    back_near = move(zero + first[len(far1) :], near)
     second = work(pass_far2, up_far2, weights)
     second, back_first = tie((second, back_far1[0]))
     back_far1 = [back_first] + back_far1[1:]
     back_far2 = move(second, far2)
     early, gate_early = combine(back_far1 + back_near, far1 + near)
     late, gate_late = combine(back_far2, far2)
-    return (early + late).astype(BF16), gate_early + gate_late
+    return (early + late).astype(BF16), (gate_early + gate_late).T
 
 
 def solution(mesh):

time: 157 us -> 155 us (0.987)
  waiting for transfers between devices: 83.7 us -> 64.2 us
  Pallas kernels: 34 us -> 46.1 us
  starting transfers between devices: 25.4 us -> 31.5 us
    ppermute x19, waiting for transfers between devices: 75.6 us -> 56.2 us  [move(): lax.ppermute(rows, CHIPS, [(i, i ^ offset) for i in range(chips)])]
    pallas_call x2 -> x3, Pallas kernels: 31.7 us -> 43.8 us  [expert(): pl.pallas_call(functools.partial(expert_kernel, min(256, own[0].shape[2])...]
    ppermute x19, starting transfers between devices: 24.8 us -> 30.9 us  [move(): lax.ppermute(rows, CHIPS, [(i, i ^ offset) for i in range(chips)])]
    unnamed x26 -> x20, local copies, waits for them, and re-layouts: 6.62 us -> 6.3 us
  transfers between devices with their start and end apart: 22 -> 22, of which waited for: 10 -> 8; matrix products, arithmetic and copies ran while one was open for 2% -> 2% of each run, Pallas kernels for 22% -> 30%
where the time goes in v5:
time: 155 us
  waiting for transfers between devices  64.2 us (41%)
  Pallas kernels  46.1 us (30%)
  starting transfers between devices  31.5 us (20%)
  local copies, waits for them, and re-layouts  6.72 us (4%)
  other arithmetic  3.48 us (2%)
  matrix products  1.79 us (1%)
    ppermute x19, waiting for transfers between devices, move(): lax.ppermute(rows, CHIPS, [(i, i ^ offset) for i in range(chips)])  56.2 us
    pallas_call x3, Pallas kernels, expert(): pl.pallas_call(functools.partial(expert_kernel, min(256, own[0].shape[2])...  43.8 us
    ppermute x19, starting transfers between devices, move(): lax.ppermute(rows, CHIPS, [(i, i ^ offset) for i in range(chips)])  30.9 us
    ppermute x3, waiting for transfers between devices, swap_cores(): return lax.ppermute(values, 'core', [(0, 1), (1, 0)])  7.97 us
    unnamed x20, local copies, waits for them, and re-layouts  6.3 us
  transfers between devices with their start and end apart: 22, of which 8 were waited for; matrix products, arithmetic and copies ran while one was open for 2% of the time, Pallas kernels for 30%

profile of v5, /device:TPU:8, one launch (start us, length us, event | category | flops | bytes accessed | tf_op | source)
XLA Modules:
  0.0 154.7 jit_solution(18364863867466457820)
XLA Ops:
  1.3 2.6 %collective-permute-start = (bf16[128,3584]{1,0:T(8,128)(2,1)}, bf16[128,3584]{1,0:T(8,128)(2,1)S(1)}, u32[]{:S(2)}, u32[]{:S(2)}) collective-permute-start(bf16[128,3584]{1,0:T(8,128)(2,1)} %refs_0_.3), channel_id=1, source_target_pairs={{0,8},{2,10},{4,12},{6,14},{8,0},{10,2},{12,4},{14,6},{1,9},{3,11}... | collective-permute-start | bytes 2752520 | tf_op jit(solution)/shard_map/ppermute | solution.py:121
  3.9 0.7 convert_reduce_fusion.2
  4.9 0.8 select_reduce_fusion.5
  5.7 1.2 copy-done.4
  6.9 1.2 copy-done.5
  8.1 1.1 dispatch.4
  10.0 2.7 %collective-permute-done.3.refs_4_ = bf16[1,3584,512]{2,1,0:T(8,128)(2,1)} collective-permute-done((bf16[1,3584,512]{2,1,0:T(8,128)(2,1)}, bf16[1,3584,512]{2,1,0:T(8,128)(2,1)}, u32[]{:S(2)}, u32[]{:S(2)}) %collective-permute-start.3) | collective-permute-done | bytes 3670048 | tf_op jit(solution)/shard_map/ppermute | solution.py:30
  12.7 5.2 %collective-permute-done.4.refs_5_ = bf16[1,512,3584]{2,1,0:T(8,128)(2,1)} collective-permute-done((bf16[1,512,3584]{2,1,0:T(8,128)(2,1)}, bf16[1,512,3584]{2,1,0:T(8,128)(2,1)}, u32[]{:S(2)}, u32[]{:S(2)}) %collective-permute-start.4) | collective-permute-done | bytes 3670048 | tf_op jit(solution)/shard_map/ppermute | solution.py:30
  17.9 1.5 collective-permute-start.7
  19.5 2.7 %collective-permute-start.5 = (s32[2,128]{1,0:T(2,128)S(1)}, s32[2,128]{1,0:T(2,128)S(1)}, u32[]{:S(2)}, u32[]{:S(2)}) collective-permute-start(s32[2,128]{1,0:T(2,128)S(1)} %add_bitcast_fusion.1.index_ref), channel_id=1, source_target_pairs={{0,8},{2,10},{4,12},{6,14},{8,0},{10,2},{12,4},{14,6},{1,9},{3,11}... | collective-permute-start | bytes 3080 | tf_op jit(solution)/shard_map/ppermute | solution.py:121
  22.9 21.1 %collective-permute-done.refs_0_ = bf16[128,3584]{1,0:T(8,128)(2,1)S(1)} collective-permute-done((bf16[128,3584]{1,0:T(8,128)(2,1)}, bf16[128,3584]{1,0:T(8,128)(2,1)S(1)}, u32[]{:S(2)}, u32[]{:S(2)}) %collective-permute-start) | collective-permute-done | bytes 917536 | tf_op jit(solution)/shard_map/ppermute | solution.py:121
  44.0 3.3 %collective-permute-start.1 = (bf16[40,3584]{1,0:T(8,128)(2,1)S(1)}, bf16[40,3584]{1,0:T(8,128)(2,1)S(1)}, u32[]{:S(2)}, u32[]{:S(2)}) collective-permute-start(bf16[40,3584]{1,0:T(8,128)(2,1)S(1)} %bitcast.37), channel_id=1, source_target_pairs={{0,8},{2,10},{4,12},{6,14},{8,0},{10,2},{12,4},{14,6},{1,9},{3,11}... | collective-permute-start | bytes 860168 | tf_op jit(solution)/shard_map/ppermute | solution.py:121
  47.3 1.0 collective-permute-start.8
  49.6 1.8 %collective-permute-start.14 = (bf16[2,40,3584]{2,1,0:T(8,128)(2,1)S(1)}, bf16[2,40,3584]{2,1,0:T(8,128)(2,1)S(1)}, u32[]{:S(2)}, u32[]{:S(2)}) collective-permute-start(bf16[2,40,3584]{2,1,0:T(8,128)(2,1)S(1)} %get-tuple-element.107), channel_id=1, source_target_pairs={{0,6},{2,4},{4,2},{6,0},{8,14},{10,12},{12,10},{14,8},{1,7},{3,5},... | collective-permute-start | bytes 1720328 | tf_op jit(solution)/shard_map/ppermute | solution.py:121
  51.7 1.7 %copy-done = bf16[1,3584,512]{2,1,0:T(8,128)(2,1)S(1)} copy-done((bf16[1,3584,512]{2,1,0:T(8,128)(2,1)S(1)}, bf16[1,3584,512]{2,1,0:T(8,128)(2,1)}, u32[]{:S(2)}) %copy-start) | copy-done | bytes 3670040
  53.4 2.0 %copy-done.2 = bf16[1,512,3584]{2,1,0:T(8,128)(2,1)S(1)} copy-done((bf16[1,512,3584]{2,1,0:T(8,128)(2,1)S(1)}, bf16[1,512,3584]{2,1,0:T(8,128)(2,1)}, u32[]{:S(2)}) %copy-start.2) | copy-done | bytes 3670040
  55.4 14.5 %expert.3 = (bf16[40,3712]{1,0:T(8,128)(2,1)S(1)}, bf16[40,3712]{1,0:T(8,128)(2,1)S(1)}, bf16[40,3712]{1,0:T(8,128)(2,1)S(1)}) custom-call(bf16[120,3584]{1,0:T(8,128)(2,1)S(1)} %pad_maximum_fusion.tokens_ref, bf16[120,3584]{1,0:T(8,128)(2,1)S(1)} %pad_maximum_fusion.1.upstream_ref, bf16[1,3584,512]{2,1,0:T(8,128)(2,1)S(1)} %copy-done, ...), custom_call_target="tpu_custom_call" | custom-call | flops 1 | bytes 1 | tf_op jit(solution)/shard_map/expert/pallas_call | solution.py:90
  69.9 1.2 collective-permute-start.11
  71.1 0.8 collective-permute-start.12
  71.9 2.7 %collective-permute-start.9 = (bf16[40,3584]{1,0:T(8,128)(2,1)S(1)}, bf16[40,3584]{1,0:T(8,128)(2,1)S(1)}, u32[]{:S(2)}, u32[]{:S(2)}) collective-permute-start(bf16[40,3584]{1,0:T(8,128)(2,1)S(1)} %bitcast.33), channel_id=1, source_target_pairs={{0,12},{2,14},{4,8},{6,10},{8,4},{10,6},{12,0},{14,2},{1,13},{3,15... | collective-permute-start | bytes 860168 | tf_op jit(solution)/shard_map/ppermute | solution.py:121
  74.6 1.4 collective-permute-done.13
  76.2 14.8 %expert.4 = (bf16[40,3712]{1,0:T(8,128)(2,1)S(1)}, bf16[40,3712]{1,0:T(8,128)(2,1)S(1)}, bf16[40,3712]{1,0:T(8,128)(2,1)S(1)}) custom-call(bf16[120,3584]{1,0:T(8,128)(2,1)S(1)} %get-tuple-element.151.tokens_ref, bf16[120,3584]{1,0:T(8,128)(2,1)S(1)} %get-tuple-element.152.upstream_ref, bf16[1,3584,512]{2,1,0:T(8,128)(2,1)S(1)} %copy-done, ...), custom_call_target="tpu_custom_call" | custom-call | flops 1 | bytes 1 | tf_op jit(solution)/shard_map/expert/pallas_call | solution.py:90
  90.9 5.6 %collective-permute-start.15 = (bf16[40,3712]{1,0:T(8,128)(2,1)S(1)}, bf16[40,3712]{1,0:T(8,128)(2,1)S(1)}, u32[]{:S(2)}, u32[]{:S(2)}) collective-permute-start(bf16[40,3712]{1,0:T(8,128)(2,1)S(1)} %get-tuple-element.113), channel_id=1, source_target_pairs={{0,8},{2,10},{4,12},{6,14},{8,0},{10,2},{12,4},{14,6},{1,9},{3,11}... | collective-permute-start | bytes 890888 | tf_op jit(solution)/shard_map/ppermute | solution.py:121
  96.5 1.0 collective-permute-start.16
  97.5 16.0 %collective-permute-done.10 = bf16[40,3584]{1,0:T(8,128)(2,1)S(1)} collective-permute-done((bf16[40,3584]{1,0:T(8,128)(2,1)S(1)}, bf16[40,3584]{1,0:T(8,128)(2,1)S(1)}, u32[]{:S(2)}, u32[]{:S(2)}) %collective-permute-start.10) | collective-permute-done | bytes 286752 | tf_op jit(solution)/shard_map/ppermute | solution.py:121
  113.5 3.5 %collective-permute-start.19 = (bf16[40,3712]{1,0:T(8,128)(2,1)S(1)}, bf16[40,3712]{1,0:T(8,128)(2,1)S(1)}, u32[]{:S(2)}, u32[]{:S(2)}) collective-permute-start(bf16[40,3712]{1,0:T(8,128)(2,1)S(1)} %get-tuple-element.129), channel_id=1, source_target_pairs={{0,6},{2,4},{4,2},{6,0},{8,14},{10,12},{12,10},{14,8},{1,7},{3,5},... | collective-permute-start | bytes 890888 | tf_op jit(solution)/shard_map/ppermute | solution.py:121
  117.1 14.6 %expert.5 = (bf16[40,3712]{1,0:T(8,128)(2,1)S(1)}, bf16[40,3712]{1,0:T(8,128)(2,1)S(1)}) custom-call(bf16[80,3584]{1,0:T(8,128)(2,1)S(1)} %pad_maximum_fusion.4.tokens_ref, bf16[80,3584]{1,0:T(8,128)(2,1)S(1)} %pad_maximum_fusion.5.upstream_ref, bf16[1,3584,512]{2,1,0:T(8,128)(2,1)S(1)} %copy-done, bf16[1,3584,512]{2,1,0:T(8,128)(2,1)S(1)} %copy-done.1, ...), custom_call_target="tpu_custom_call" | custom-call | flops 1 | bytes 1 | tf_op jit(solution)/shard_map/expert/pallas_call | solution.py:90
  131.7 2.1 %collective-permute-start.20 = (bf16[40,3712]{1,0:T(8,128)(2,1)S(1)}, bf16[40,3712]{1,0:T(8,128)(2,1)S(1)}, u32[]{:S(2)}, u32[]{:S(2)}) collective-permute-start(bf16[40,3712]{1,0:T(8,128)(2,1)S(1)} %get-tuple-element.130), channel_id=1, source_target_pairs={{0,12},{2,14},{4,8},{6,10},{8,4},{10,6},{12,0},{14,2},{1,13},{3,15... | collective-permute-start | bytes 890888 | tf_op jit(solution)/shard_map/ppermute | solution.py:121
  134.1 8.6 %collective-permute-done.19 = bf16[40,3712]{1,0:T(8,128)(2,1)S(1)} collective-permute-done((bf16[40,3712]{1,0:T(8,128)(2,1)S(1)}, bf16[40,3712]{1,0:T(8,128)(2,1)S(1)}, u32[]{:S(2)}, u32[]{:S(2)}) %collective-permute-start.19) | collective-permute-done | bytes 296992 | tf_op jit(solution)/shard_map/ppermute | solution.py:121
  143.0 4.3 %collective-permute-done.20 = bf16[40,3712]{1,0:T(8,128)(2,1)S(1)} collective-permute-done((bf16[40,3712]{1,0:T(8,128)(2,1)S(1)}, bf16[40,3712]{1,0:T(8,128)(2,1)S(1)}, u32[]{:S(2)}, u32[]{:S(2)}) %collective-permute-start.20) | collective-permute-done | bytes 296992 | tf_op jit(solution)/shard_map/ppermute | solution.py:121
  147.3 4.8 %collective-permute-done.21 = bf16[40,3712]{1,0:T(8,128)(2,1)S(1)} collective-permute-done((bf16[40,3712]{1,0:T(8,128)(2,1)S(1)}, bf16[40,3712]{1,0:T(8,128)(2,1)S(1)}, u32[]{:S(2)}, u32[]{:S(2)}) %collective-permute-start.21) | collective-permute-done | bytes 296992 | tf_op jit(solution)/shard_map/ppermute | solution.py:121
  152.8 1.4 fusion
  (74 shorter events, 6.2 us)
Async XLA Ops:
  0.6 9.3 %collective-permute-start.2 = (bf16[1,3584,512]{2,1,0:T(8,128)(2,1)}, bf16[1,3584,512]{2,1,0:T(8,128)(2,1)}, u32[]{:S(2)}, u32[]{:S(2)}) collective-permute-start(bf16[1,3584,512]{2,1,0:T(8,128)(2,1)} %refs_0_.6), channel_id=1, source_target_pairs={{0,1},{1,0},{2,3},{3,2},{4,5},{5,4},{6,7},{7,6},{8,9},{9,8},{10,11... | collective-permute-start | bytes 11010056 | tf_op jit(solution)/shard_map/ppermute | solution.py:30
  0.7 12.0 %collective-permute-start.3 = (bf16[1,3584,512]{2,1,0:T(8,128)(2,1)}, bf16[1,3584,512]{2,1,0:T(8,128)(2,1)}, u32[]{:S(2)}, u32[]{:S(2)}) collective-permute-start(bf16[1,3584,512]{2,1,0:T(8,128)(2,1)} %refs_1_.4), channel_id=1, source_target_pairs={{0,1},{1,0},{2,3},{3,2},{4,5},{5,4},{6,7},{7,6},{8,9},{9,8},{10,11... | collective-permute-start | bytes 11010056 | tf_op jit(solution)/shard_map/ppermute | solution.py:30
  1.2 16.7 %collective-permute-start.4 = (bf16[1,512,3584]{2,1,0:T(8,128)(2,1)}, bf16[1,512,3584]{2,1,0:T(8,128)(2,1)}, u32[]{:S(2)}, u32[]{:S(2)}) collective-permute-start(bf16[1,512,3584]{2,1,0:T(8,128)(2,1)} %refs_2_.2), channel_id=1, source_target_pairs={{0,1},{1,0},{2,3},{3,2},{4,5},{5,4},{6,7},{7,6},{8,9},{9,8},{10,11... | collective-permute-start | bytes 11010056 | tf_op jit(solution)/shard_map/ppermute | solution.py:30
  1.3 42.7 %collective-permute-start = (bf16[128,3584]{1,0:T(8,128)(2,1)}, bf16[128,3584]{1,0:T(8,128)(2,1)S(1)}, u32[]{:S(2)}, u32[]{:S(2)}) collective-permute-start(bf16[128,3584]{1,0:T(8,128)(2,1)} %refs_0_.3), channel_id=1, source_target_pairs={{0,8},{2,10},{4,12},{6,14},{8,0},{10,2},{12,4},{14,6},{1,9},{3,11}... | collective-permute-start | bytes 2752520 | tf_op jit(solution)/shard_map/ppermute | solution.py:121
  5.7 1.2 copy-start.4
  6.9 1.2 copy-start.5
  9.2 38.1 %collective-permute-start.6 = (bf16[2,40,3584]{2,1,0:T(8,128)(2,1)S(1)}, bf16[2,40,3584]{2,1,0:T(8,128)(2,1)S(1)}, u32[]{:S(2)}, u32[]{:S(2)}) collective-permute-start(bf16[2,40,3584]{2,1,0:T(8,128)(2,1)S(1)} %get-tuple-element.73), channel_id=1, source_target_pairs={{0,4},{2,6},{4,0},{6,2},{8,12},{10,14},{12,8},{14,10},{1,5},{3,7},... | collective-permute-start | bytes 1720328 | tf_op jit(solution)/shard_map/ppermute | solution.py:121
  17.9 29.3 %collective-permute-start.7 = (bf16[2,40,3584]{2,1,0:T(8,128)(2,1)S(1)}, bf16[2,40,3584]{2,1,0:T(8,128)(2,1)S(1)}, u32[]{:S(2)}, u32[]{:S(2)}) collective-permute-start(bf16[2,40,3584]{2,1,0:T(8,128)(2,1)S(1)} %get-tuple-element.75), channel_id=1, source_target_pairs={{0,2},{2,0},{4,6},{6,4},{8,10},{10,8},{12,14},{14,12},{1,3},{3,1},... | collective-permute-start | bytes 1720328 | tf_op jit(solution)/shard_map/ppermute | solution.py:121
  19.5 27.7 %collective-permute-start.5 = (s32[2,128]{1,0:T(2,128)S(1)}, s32[2,128]{1,0:T(2,128)S(1)}, u32[]{:S(2)}, u32[]{:S(2)}) collective-permute-start(s32[2,128]{1,0:T(2,128)S(1)} %add_bitcast_fusion.1.index_ref), channel_id=1, source_target_pairs={{0,8},{2,10},{4,12},{6,14},{8,0},{10,2},{12,4},{14,6},{1,9},{3,11}... | collective-permute-start | bytes 3080 | tf_op jit(solution)/shard_map/ppermute | solution.py:121
  44.0 27.1 %collective-permute-start.1 = (bf16[40,3584]{1,0:T(8,128)(2,1)S(1)}, bf16[40,3584]{1,0:T(8,128)(2,1)S(1)}, u32[]{:S(2)}, u32[]{:S(2)}) collective-permute-start(bf16[40,3584]{1,0:T(8,128)(2,1)S(1)} %bitcast.37), channel_id=1, source_target_pairs={{0,8},{2,10},{4,12},{6,14},{8,0},{10,2},{12,4},{14,6},{1,9},{3,11}... | collective-permute-start | bytes 860168 | tf_op jit(solution)/shard_map/ppermute | solution.py:121
  47.3 24.6 %collective-permute-start.8 = (bf16[40,3584]{1,0:T(8,128)(2,1)S(1)}, bf16[40,3584]{1,0:T(8,128)(2,1)S(1)}, u32[]{:S(2)}, u32[]{:S(2)}) collective-permute-start(bf16[40,3584]{1,0:T(8,128)(2,1)S(1)} %bitcast.36), channel_id=1, source_target_pairs={{0,10},{2,8},{4,14},{6,12},{8,2},{10,0},{12,6},{14,4},{1,11},{3,9}... | collective-permute-start | bytes 860168 | tf_op jit(solution)/shard_map/ppermute | solution.py:121
  48.3 3.4 %copy-start.1 = (bf16[1,3584,512]{2,1,0:T(8,128)(2,1)S(1)}, bf16[1,3584,512]{2,1,0:T(8,128)(2,1)}, u32[]{:S(2)}) copy-start(bf16[1,3584,512]{2,1,0:T(8,128)(2,1)} %refs_1_.4) | copy-start | bytes 11010052
  48.9 27.0 %collective-permute-start.13 = (bf16[40,3584]{1,0:T(8,128)(2,1)S(1)}, bf16[40,3584]{1,0:T(8,128)(2,1)S(1)}, u32[]{:S(2)}, u32[]{:S(2)}) collective-permute-start(bf16[40,3584]{1,0:T(8,128)(2,1)S(1)} %bitcast.38), channel_id=1, source_target_pairs={{0,2},{2,0},{4,6},{6,4},{8,10},{10,8},{12,14},{14,12},{1,3},{3,1},... | collective-permute-start | bytes 860168 | tf_op jit(solution)/shard_map/ppermute | solution.py:121
  49.6 26.4 %collective-permute-start.14 = (bf16[2,40,3584]{2,1,0:T(8,128)(2,1)S(1)}, bf16[2,40,3584]{2,1,0:T(8,128)(2,1)S(1)}, u32[]{:S(2)}, u32[]{:S(2)}) collective-permute-start(bf16[2,40,3584]{2,1,0:T(8,128)(2,1)S(1)} %get-tuple-element.107), channel_id=1, source_target_pairs={{0,6},{2,4},{4,2},{6,0},{8,14},{10,12},{12,10},{14,8},{1,7},{3,5},... | collective-permute-start | bytes 1720328 | tf_op jit(solution)/shard_map/ppermute | solution.py:121
  51.4 2.0 %copy-start = (bf16[1,3584,512]{2,1,0:T(8,128)(2,1)S(1)}, bf16[1,3584,512]{2,1,0:T(8,128)(2,1)}, u32[]{:S(2)}) copy-start(bf16[1,3584,512]{2,1,0:T(8,128)(2,1)} %refs_0_.6) | copy-start | bytes 11010052
  53.4 2.0 %copy-start.2 = (bf16[1,512,3584]{2,1,0:T(8,128)(2,1)S(1)}, bf16[1,512,3584]{2,1,0:T(8,128)(2,1)}, u32[]{:S(2)}) copy-start(bf16[1,512,3584]{2,1,0:T(8,128)(2,1)} %refs_2_.2) | copy-start | bytes 11010052
  69.9 26.6 %collective-permute-start.11 = (bf16[40,3584]{1,0:T(8,128)(2,1)S(1)}, bf16[40,3584]{1,0:T(8,128)(2,1)S(1)}, u32[]{:S(2)}, u32[]{:S(2)}) collective-permute-start(bf16[40,3584]{1,0:T(8,128)(2,1)S(1)} %bitcast.35), channel_id=1, source_target_pairs={{0,4},{2,6},{4,0},{6,2},{8,12},{10,14},{12,8},{14,10},{1,5},{3,7},... | collective-permute-start | bytes 860168 | tf_op jit(solution)/shard_map/ppermute | solution.py:121
  71.1 26.3 %collective-permute-start.12 = (bf16[40,3584]{1,0:T(8,128)(2,1)S(1)}, bf16[40,3584]{1,0:T(8,128)(2,1)S(1)}, u32[]{:S(2)}, u32[]{:S(2)}) collective-permute-start(bf16[40,3584]{1,0:T(8,128)(2,1)S(1)} %bitcast.34), channel_id=1, source_target_pairs={{0,6},{2,4},{4,2},{6,0},{8,14},{10,12},{12,10},{14,8},{1,7},{3,5},... | collective-permute-start | bytes 860168 | tf_op jit(solution)/shard_map/ppermute | solution.py:121
  71.9 25.6 %collective-permute-start.9 = (bf16[40,3584]{1,0:T(8,128)(2,1)S(1)}, bf16[40,3584]{1,0:T(8,128)(2,1)S(1)}, u32[]{:S(2)}, u32[]{:S(2)}) collective-permute-start(bf16[40,3584]{1,0:T(8,128)(2,1)S(1)} %bitcast.33), channel_id=1, source_target_pairs={{0,12},{2,14},{4,8},{6,10},{8,4},{10,6},{12,0},{14,2},{1,13},{3,15... | collective-permute-start | bytes 860168 | tf_op jit(solution)/shard_map/ppermute | solution.py:121
  76.0 37.5 %collective-permute-start.10 = (bf16[40,3584]{1,0:T(8,128)(2,1)S(1)}, bf16[40,3584]{1,0:T(8,128)(2,1)S(1)}, u32[]{:S(2)}, u32[]{:S(2)}) collective-permute-start(bf16[40,3584]{1,0:T(8,128)(2,1)S(1)} %bitcast.32), channel_id=1, source_target_pairs={{0,14},{2,12},{4,10},{6,8},{8,6},{10,4},{12,2},{14,0},{1,15},{3,13... | collective-permute-start | bytes 860168 | tf_op jit(solution)/shard_map/ppermute | solution.py:121
  76.1 40.9 %copy-start.3 = (bf16[1,512,3584]{2,1,0:T(8,128)(2,1)S(1)}, bf16[1,512,3584]{2,1,0:T(8,128)(2,1)}, u32[]{:S(2)}) copy-start(bf16[1,512,3584]{2,1,0:T(8,128)(2,1)} %refs_2_.2) | copy-start | bytes 11010052
  90.9 40.7 %collective-permute-start.15 = (bf16[40,3712]{1,0:T(8,128)(2,1)S(1)}, bf16[40,3712]{1,0:T(8,128)(2,1)S(1)}, u32[]{:S(2)}, u32[]{:S(2)}) collective-permute-start(bf16[40,3712]{1,0:T(8,128)(2,1)S(1)} %get-tuple-element.113), channel_id=1, source_target_pairs={{0,8},{2,10},{4,12},{6,14},{8,0},{10,2},{12,4},{14,6},{1,9},{3,11}... | collective-permute-start | bytes 890888 | tf_op jit(solution)/shard_map/ppermute | solution.py:121
  96.5 37.3 %collective-permute-start.16 = (bf16[40,3712]{1,0:T(8,128)(2,1)S(1)}, bf16[40,3712]{1,0:T(8,128)(2,1)S(1)}, u32[]{:S(2)}, u32[]{:S(2)}) collective-permute-start(bf16[40,3712]{1,0:T(8,128)(2,1)S(1)} %get-tuple-element.114), channel_id=1, source_target_pairs={{0,10},{2,8},{4,14},{6,12},{8,2},{10,0},{12,6},{14,4},{1,11},{3,9}... | collective-permute-start | bytes 890888 | tf_op jit(solution)/shard_map/ppermute | solution.py:121
  113.4 20.6 %collective-permute-start.17 = (bf16[40,3712]{1,0:T(8,128)(2,1)S(1)}, bf16[40,3712]{1,0:T(8,128)(2,1)S(1)}, u32[]{:S(2)}, u32[]{:S(2)}) collective-permute-start(bf16[40,3712]{1,0:T(8,128)(2,1)S(1)} %get-tuple-element.127), channel_id=1, source_target_pairs={{0,2},{2,0},{4,6},{6,4},{8,10},{10,8},{12,14},{14,12},{1,3},{3,1},... | collective-permute-start | bytes 890888 | tf_op jit(solution)/shard_map/ppermute | solution.py:121
  113.4 20.6 %collective-permute-start.18 = (bf16[40,3712]{1,0:T(8,128)(2,1)S(1)}, bf16[40,3712]{1,0:T(8,128)(2,1)S(1)}, u32[]{:S(2)}, u32[]{:S(2)}) collective-permute-start(bf16[40,3712]{1,0:T(8,128)(2,1)S(1)} %get-tuple-element.128), channel_id=1, source_target_pairs={{0,4},{2,6},{4,0},{6,2},{8,12},{10,14},{12,8},{14,10},{1,5},{3,7},... | collective-permute-start | bytes 890888 | tf_op jit(solution)/shard_map/ppermute | solution.py:121
  113.5 29.2 %collective-permute-start.19 = (bf16[40,3712]{1,0:T(8,128)(2,1)S(1)}, bf16[40,3712]{1,0:T(8,128)(2,1)S(1)}, u32[]{:S(2)}, u32[]{:S(2)}) collective-permute-start(bf16[40,3712]{1,0:T(8,128)(2,1)S(1)} %get-tuple-element.129), channel_id=1, source_target_pairs={{0,6},{2,4},{4,2},{6,0},{8,14},{10,12},{12,10},{14,8},{1,7},{3,5},... | collective-permute-start | bytes 890888 | tf_op jit(solution)/shard_map/ppermute | solution.py:121
  131.7 11.2 %copy-start.6 = (f32[128,2]{0,1:T(2,128)S(1)}, f32[128,2]{0,1:T(2,128)}, u32[]{:S(2)}) copy-start(f32[128,2]{0,1:T(2,128)} %param.10) | copy-start | bytes 3076
  131.7 15.6 %collective-permute-start.20 = (bf16[40,3712]{1,0:T(8,128)(2,1)S(1)}, bf16[40,3712]{1,0:T(8,128)(2,1)S(1)}, u32[]{:S(2)}, u32[]{:S(2)}) collective-permute-start(bf16[40,3712]{1,0:T(8,128)(2,1)S(1)} %get-tuple-element.130), channel_id=1, source_target_pairs={{0,12},{2,14},{4,8},{6,10},{8,4},{10,6},{12,0},{14,2},{1,13},{3,15... | collective-permute-start | bytes 890888 | tf_op jit(solution)/shard_map/ppermute | solution.py:121
  133.8 18.3 %collective-permute-start.21 = (bf16[40,3712]{1,0:T(8,128)(2,1)S(1)}, bf16[40,3712]{1,0:T(8,128)(2,1)S(1)}, u32[]{:S(2)}, u32[]{:S(2)}) collective-permute-start(bf16[40,3712]{1,0:T(8,128)(2,1)S(1)} %get-tuple-element.131), channel_id=1, source_target_pairs={{0,14},{2,12},{4,10},{6,8},{8,6},{10,4},{12,2},{14,0},{1,15},{3,13... | collective-permute-start | bytes 890888 | tf_op jit(solution)/shard_map/ppermute | solution.py:121

commit v6 on v5

--- a/solution.py
+++ b/solution.py
@@ -99,6 +99,28 @@
     )(tokens, upstream, *own, *other)
 
 
+def finish_kernel(early_ref, gate_early_ref, weighted_ref, rows_ref, gate_ref, out_ref, sums_ref):
+    width = out_ref.shape[1]
+    total = early_ref[...] + nn(weighted_ref[...], rows_ref[:, :width])
+    out_ref[...] = total.astype(BF16)
+    sums_ref[...] = gate_early_ref[...] + gate_ref[...]
+
+
+def finish(early, gate_early, weighted, rows, gate_late):
+    return pl.pallas_call(
+        finish_kernel,
+        out_shape=[
+            jax.ShapeDtypeStruct(early.shape, BF16),
+            jax.ShapeDtypeStruct(gate_early.shape, F32),
+        ],
+        in_specs=[VMEM] * 5,
+        out_specs=[VMEM] * 2,
+        compiler_params=pltpu.CompilerParams(vmem_limit_bytes=24 << 20),
+        cost_estimate=SMALL,
+        name="finish",
+    )(early, gate_early, weighted, rows, gate_late)
+
+
 def per_device(tokens, routes, gates, placement, upstream, w_gate, w_up, w_down):
     tok_dev, width = tokens.shape
     top_count = routes.shape[1]
@@ -136,9 +158,7 @@
         weighted = jnp.sum(jnp.where(hits, gates.T[None], 0.0), axis=1).T.astype(BF16)
         rows = jnp.concatenate(back)
         part = rows[:, width].astype(F32)
-        return nn(weighted, rows[:, :width]), jnp.sum(
-            jnp.where(hits, part[:, None, None], 0.0), axis=0
-        )
+        return weighted, rows, jnp.sum(jnp.where(hits, part[:, None, None], 0.0), axis=0)
 
     half = chips // 2
     near = list(range(half))
@@ -188,9 +208,13 @@
     second, back_first = tie((second, back_far1[0]))
     back_far1 = [back_first] + back_far1[1:]
     back_far2 = move(second, far2)
-    early, gate_early = combine(back_far1 + back_near, far1 + near)
-    late, gate_late = combine(back_far2, far2)
-    return (early + late).astype(BF16), (gate_early + gate_late).T
+    back_far1, back_near, ahead = tie((back_far1, back_near, back_far2[:1]))
+    back_far2 = ahead + back_far2[1:]
+    weighted, rows, gate_early = combine(back_far1 + back_near, far1 + near)
+    early = nn(weighted, rows[:, :width])
+    weighted, rows, gate_late = combine(back_far2, far2)
+    grad_tokens, grad_gates = finish(early, gate_early, weighted, rows, gate_late)
+    return grad_tokens, grad_gates.T
 
 
 def solution(mesh):

time: 155 us -> 154 us (level)
  waiting for transfers between devices: 64.2 us -> 61.8 us
  local copies, waits for them, and re-layouts: 6.72 us -> 9.03 us
    ppermute x19, waiting for transfers between devices: 56.2 us -> 53.7 us  [move(): lax.ppermute(rows, CHIPS, [(i, i ^ offset) for i in range(chips)])]
    unnamed x20 -> x22, local copies, waits for them, and re-layouts: 6.3 us -> 8.55 us
where the time goes in v6:
time: 154 us
  waiting for transfers between devices  61.8 us (40%)
  Pallas kernels  47.2 us (31%)
  starting transfers between devices  31.5 us (20%)
  local copies, waits for them, and re-layouts  9.03 us (6%)
  other arithmetic  2.94 us (2%)
    ppermute x19, waiting for transfers between devices, move(): lax.ppermute(rows, CHIPS, [(i, i ^ offset) for i in range(chips)])  53.7 us
    pallas_call x3, Pallas kernels, expert(): pl.pallas_call(functools.partial(expert_kernel, min(256, own[0].shape[2])...  43.6 us
    ppermute x19, starting transfers between devices, move(): lax.ppermute(rows, CHIPS, [(i, i ^ offset) for i in range(chips)])  30.9 us
    unnamed x22, local copies, waits for them, and re-layouts  8.55 us
    ppermute x3, waiting for transfers between devices, swap_cores(): return lax.ppermute(values, 'core', [(0, 1), (1, 0)])  8.05 us
  transfers between devices with their start and end apart: 22, of which 8 were waited for; matrix products, arithmetic and copies ran while one was open for 2% of the time, Pallas kernels for 30%

profile of v6, /device:TPU:8, one launch (start us, length us, event | category | flops | bytes accessed | tf_op | source)
XLA Modules:
  0.0 153.8 jit_solution(12807643284746302507)
XLA Ops:
  1.3 2.6 %collective-permute-start = (bf16[128,3584]{1,0:T(8,128)(2,1)}, bf16[128,3584]{1,0:T(8,128)(2,1)S(1)}, u32[]{:S(2)}, u32[]{:S(2)}) collective-permute-start(bf16[128,3584]{1,0:T(8,128)(2,1)} %refs_0_.3), channel_id=1, source_target_pairs={{0,8},{2,10},{4,12},{6,14},{8,0},{10,2},{12,4},{14,6},{1,9},{3,11}... | collective-permute-start | bytes 2752520 | tf_op jit(solution)/shard_map/ppermute | solution.py:143
  4.9 0.8 select_reduce_fusion.5
  5.7 1.2 copy-done.4
  6.9 1.2 copy-done.6
  8.1 1.1 dispatch.4
  9.9 2.8 %collective-permute-done.3.refs_4_ = bf16[1,3584,512]{2,1,0:T(8,128)(2,1)} collective-permute-done((bf16[1,3584,512]{2,1,0:T(8,128)(2,1)}, bf16[1,3584,512]{2,1,0:T(8,128)(2,1)}, u32[]{:S(2)}, u32[]{:S(2)}) %collective-permute-start.3) | collective-permute-done | bytes 3670048 | tf_op jit(solution)/shard_map/ppermute | solution.py:30
  12.7 5.2 %collective-permute-done.4.refs_5_ = bf16[1,512,3584]{2,1,0:T(8,128)(2,1)} collective-permute-done((bf16[1,512,3584]{2,1,0:T(8,128)(2,1)}, bf16[1,512,3584]{2,1,0:T(8,128)(2,1)}, u32[]{:S(2)}, u32[]{:S(2)}) %collective-permute-start.4) | collective-permute-done | bytes 3670048 | tf_op jit(solution)/shard_map/ppermute | solution.py:30
  17.9 1.5 collective-permute-start.7
  19.5 2.7 %collective-permute-start.5 = (s32[2,128]{1,0:T(2,128)S(1)}, s32[2,128]{1,0:T(2,128)S(1)}, u32[]{:S(2)}, u32[]{:S(2)}) collective-permute-start(s32[2,128]{1,0:T(2,128)S(1)} %add_bitcast_fusion.index_ref), channel_id=1, source_target_pairs={{0,8},{2,10},{4,12},{6,14},{8,0},{10,2},{12,4},{14,6},{1,9},{3,11}... | collective-permute-start | bytes 3080 | tf_op jit(solution)/shard_map/ppermute | solution.py:143
  22.9 21.1 %collective-permute-done.refs_0_ = bf16[128,3584]{1,0:T(8,128)(2,1)S(1)} collective-permute-done((bf16[128,3584]{1,0:T(8,128)(2,1)}, bf16[128,3584]{1,0:T(8,128)(2,1)S(1)}, u32[]{:S(2)}, u32[]{:S(2)}) %collective-permute-start) | collective-permute-done | bytes 917536 | tf_op jit(solution)/shard_map/ppermute | solution.py:143
  44.0 3.3 %collective-permute-start.1 = (bf16[40,3584]{1,0:T(8,128)(2,1)S(1)}, bf16[40,3584]{1,0:T(8,128)(2,1)S(1)}, u32[]{:S(2)}, u32[]{:S(2)}) collective-permute-start(bf16[40,3584]{1,0:T(8,128)(2,1)S(1)} %bitcast.37), channel_id=1, source_target_pairs={{0,8},{2,10},{4,12},{6,14},{8,0},{10,2},{12,4},{14,6},{1,9},{3,11}... | collective-permute-start | bytes 860168 | tf_op jit(solution)/shard_map/ppermute | solution.py:143
  47.3 1.0 collective-permute-start.8
  49.6 1.8 %collective-permute-start.14 = (bf16[2,40,3584]{2,1,0:T(8,128)(2,1)S(1)}, bf16[2,40,3584]{2,1,0:T(8,128)(2,1)S(1)}, u32[]{:S(2)}, u32[]{:S(2)}) collective-permute-start(bf16[2,40,3584]{2,1,0:T(8,128)(2,1)S(1)} %get-tuple-element.116), channel_id=1, source_target_pairs={{0,6},{2,4},{4,2},{6,0},{8,14},{10,12},{12,10},{14,8},{1,7},{3,5},... | collective-permute-start | bytes 1720328 | tf_op jit(solution)/shard_map/ppermute | solution.py:143
  51.6 1.8 %copy-done = bf16[1,3584,512]{2,1,0:T(8,128)(2,1)S(1)} copy-done((bf16[1,3584,512]{2,1,0:T(8,128)(2,1)S(1)}, bf16[1,3584,512]{2,1,0:T(8,128)(2,1)}, u32[]{:S(2)}) %copy-start) | copy-done | bytes 3670040
  53.4 2.0 %copy-done.2 = bf16[1,512,3584]{2,1,0:T(8,128)(2,1)S(1)} copy-done((bf16[1,512,3584]{2,1,0:T(8,128)(2,1)S(1)}, bf16[1,512,3584]{2,1,0:T(8,128)(2,1)}, u32[]{:S(2)}) %copy-start.2) | copy-done | bytes 3670040
  55.4 14.5 %expert.3 = (bf16[40,3712]{1,0:T(8,128)(2,1)S(1)}, bf16[40,3712]{1,0:T(8,128)(2,1)S(1)}, bf16[40,3712]{1,0:T(8,128)(2,1)S(1)}) custom-call(bf16[120,3584]{1,0:T(8,128)(2,1)S(1)} %pad_maximum_fusion.tokens_ref, bf16[120,3584]{1,0:T(8,128)(2,1)S(1)} %pad_maximum_fusion.1.upstream_ref, bf16[1,3584,512]{2,1,0:T(8,128)(2,1)S(1)} %copy-done, ...), custom_call_target="tpu_custom_call" | custom-call | flops 1 | bytes 1 | tf_op jit(solution)/shard_map/expert/pallas_call | solution.py:90
  69.9 1.2 collective-permute-start.11
  71.1 0.8 collective-permute-start.12
  71.9 2.7 %collective-permute-start.9 = (bf16[40,3584]{1,0:T(8,128)(2,1)S(1)}, bf16[40,3584]{1,0:T(8,128)(2,1)S(1)}, u32[]{:S(2)}, u32[]{:S(2)}) collective-permute-start(bf16[40,3584]{1,0:T(8,128)(2,1)S(1)} %bitcast.33), channel_id=1, source_target_pairs={{0,12},{2,14},{4,8},{6,10},{8,4},{10,6},{12,0},{14,2},{1,13},{3,15... | collective-permute-start | bytes 860168 | tf_op jit(solution)/shard_map/ppermute | solution.py:143
  74.6 1.4 collective-permute-done.13
  76.2 1.8 %copy-done.3 = bf16[1,512,3584]{2,1,0:T(8,128)(2,1)S(1)} copy-done((bf16[1,512,3584]{2,1,0:T(8,128)(2,1)S(1)}, bf16[1,512,3584]{2,1,0:T(8,128)(2,1)}, u32[]{:S(2)}) %copy-start.3) | copy-done | bytes 3670040
  78.0 14.6 %expert.4 = (bf16[40,3712]{1,0:T(8,128)(2,1)S(1)}, bf16[40,3712]{1,0:T(8,128)(2,1)S(1)}, bf16[40,3712]{1,0:T(8,128)(2,1)S(1)}) custom-call(bf16[120,3584]{1,0:T(8,128)(2,1)S(1)} %get-tuple-element.169.tokens_ref, bf16[120,3584]{1,0:T(8,128)(2,1)S(1)} %get-tuple-element.170.upstream_ref, bf16[1,3584,512]{2,1,0:T(8,128)(2,1)S(1)} %copy-done, ...), custom_call_target="tpu_custom_call" | custom-call | flops 1 | bytes 1 | tf_op jit(solution)/shard_map/expert/pallas_call | solution.py:90
  92.6 5.6 %collective-permute-start.15 = (bf16[40,3712]{1,0:T(8,128)(2,1)S(1)}, bf16[40,3712]{1,0:T(8,128)(2,1)S(1)}, u32[]{:S(2)}, u32[]{:S(2)}) collective-permute-start(bf16[40,3712]{1,0:T(8,128)(2,1)S(1)} %get-tuple-element.122), channel_id=1, source_target_pairs={{0,8},{2,10},{4,12},{6,14},{8,0},{10,2},{12,4},{14,6},{1,9},{3,11}... | collective-permute-start | bytes 890888 | tf_op jit(solution)/shard_map/ppermute | solution.py:143
  98.1 1.0 collective-permute-start.16
  99.1 14.3 %collective-permute-done.10 = bf16[40,3584]{1,0:T(8,128)(2,1)S(1)} collective-permute-done((bf16[40,3584]{1,0:T(8,128)(2,1)S(1)}, bf16[40,3584]{1,0:T(8,128)(2,1)S(1)}, u32[]{:S(2)}, u32[]{:S(2)}) %collective-permute-start.10) | collective-permute-done | bytes 286752 | tf_op jit(solution)/shard_map/ppermute | solution.py:143
  113.5 3.5 %collective-permute-start.19 = (bf16[40,3712]{1,0:T(8,128)(2,1)S(1)}, bf16[40,3712]{1,0:T(8,128)(2,1)S(1)}, u32[]{:S(2)}, u32[]{:S(2)}) collective-permute-start(bf16[40,3712]{1,0:T(8,128)(2,1)S(1)} %get-tuple-element.138), channel_id=1, source_target_pairs={{0,6},{2,4},{4,2},{6,0},{8,14},{10,12},{12,10},{14,8},{1,7},{3,5},... | collective-permute-start | bytes 890888 | tf_op jit(solution)/shard_map/ppermute | solution.py:143
  117.1 14.6 %expert.5 = (bf16[40,3712]{1,0:T(8,128)(2,1)S(1)}, bf16[40,3712]{1,0:T(8,128)(2,1)S(1)}) custom-call(bf16[80,3584]{1,0:T(8,128)(2,1)S(1)} %pad_maximum_fusion.4.tokens_ref, bf16[80,3584]{1,0:T(8,128)(2,1)S(1)} %pad_maximum_fusion.5.upstream_ref, bf16[1,3584,512]{2,1,0:T(8,128)(2,1)S(1)} %copy-done, bf16[1,3584,512]{2,1,0:T(8,128)(2,1)S(1)} %copy-done.1, ...), custom_call_target="tpu_custom_call" | custom-call | flops 1 | bytes 1 | tf_op jit(solution)/shard_map/expert/pallas_call | solution.py:90
  131.7 2.1 %collective-permute-start.20 = (bf16[40,3712]{1,0:T(8,128)(2,1)S(1)}, bf16[40,3712]{1,0:T(8,128)(2,1)S(1)}, u32[]{:S(2)}, u32[]{:S(2)}) collective-permute-start(bf16[40,3712]{1,0:T(8,128)(2,1)S(1)} %get-tuple-element.139), channel_id=1, source_target_pairs={{0,12},{2,14},{4,8},{6,10},{8,4},{10,6},{12,0},{14,2},{1,13},{3,15... | collective-permute-start | bytes 890888 | tf_op jit(solution)/shard_map/ppermute | solution.py:143
  134.0 8.7 %collective-permute-done.19 = bf16[40,3712]{1,0:T(8,128)(2,1)S(1)} collective-permute-done((bf16[40,3712]{1,0:T(8,128)(2,1)S(1)}, bf16[40,3712]{1,0:T(8,128)(2,1)S(1)}, u32[]{:S(2)}, u32[]{:S(2)}) %collective-permute-start.19) | collective-permute-done | bytes 296992 | tf_op jit(solution)/shard_map/ppermute | solution.py:143
  142.7 4.6 %collective-permute-done.20 = bf16[40,3712]{1,0:T(8,128)(2,1)S(1)} collective-permute-done((bf16[40,3712]{1,0:T(8,128)(2,1)S(1)}, bf16[40,3712]{1,0:T(8,128)(2,1)S(1)}, u32[]{:S(2)}, u32[]{:S(2)}) %collective-permute-start.20) | collective-permute-done | bytes 296992 | tf_op jit(solution)/shard_map/ppermute | solution.py:143
  148.6 3.6 %collective-permute-done.21 = bf16[40,3712]{1,0:T(8,128)(2,1)S(1)} collective-permute-done((bf16[40,3712]{1,0:T(8,128)(2,1)S(1)}, bf16[40,3712]{1,0:T(8,128)(2,1)S(1)}, u32[]{:S(2)}, u32[]{:S(2)}) %collective-permute-start.21) | collective-permute-done | bytes 296992 | tf_op jit(solution)/shard_map/ppermute | solution.py:143
  152.5 1.3 finish.1
  (76 shorter events, 6.8 us)
Async XLA Ops:
  0.6 9.3 %collective-permute-start.2 = (bf16[1,3584,512]{2,1,0:T(8,128)(2,1)}, bf16[1,3584,512]{2,1,0:T(8,128)(2,1)}, u32[]{:S(2)}, u32[]{:S(2)}) collective-permute-start(bf16[1,3584,512]{2,1,0:T(8,128)(2,1)} %refs_0_.6), channel_id=1, source_target_pairs={{0,1},{1,0},{2,3},{3,2},{4,5},{5,4},{6,7},{7,6},{8,9},{9,8},{10,11... | collective-permute-start | bytes 11010056 | tf_op jit(solution)/shard_map/ppermute | solution.py:30
  0.7 12.0 %collective-permute-start.3 = (bf16[1,3584,512]{2,1,0:T(8,128)(2,1)}, bf16[1,3584,512]{2,1,0:T(8,128)(2,1)}, u32[]{:S(2)}, u32[]{:S(2)}) collective-permute-start(bf16[1,3584,512]{2,1,0:T(8,128)(2,1)} %refs_1_.4), channel_id=1, source_target_pairs={{0,1},{1,0},{2,3},{3,2},{4,5},{5,4},{6,7},{7,6},{8,9},{9,8},{10,11... | collective-permute-start | bytes 11010056 | tf_op jit(solution)/shard_map/ppermute | solution.py:30
  1.2 16.7 %collective-permute-start.4 = (bf16[1,512,3584]{2,1,0:T(8,128)(2,1)}, bf16[1,512,3584]{2,1,0:T(8,128)(2,1)}, u32[]{:S(2)}, u32[]{:S(2)}) collective-permute-start(bf16[1,512,3584]{2,1,0:T(8,128)(2,1)} %refs_2_.2), channel_id=1, source_target_pairs={{0,1},{1,0},{2,3},{3,2},{4,5},{5,4},{6,7},{7,6},{8,9},{9,8},{10,11... | collective-permute-start | bytes 11010056 | tf_op jit(solution)/shard_map/ppermute | solution.py:30
  1.3 42.7 %collective-permute-start = (bf16[128,3584]{1,0:T(8,128)(2,1)}, bf16[128,3584]{1,0:T(8,128)(2,1)S(1)}, u32[]{:S(2)}, u32[]{:S(2)}) collective-permute-start(bf16[128,3584]{1,0:T(8,128)(2,1)} %refs_0_.3), channel_id=1, source_target_pairs={{0,8},{2,10},{4,12},{6,14},{8,0},{10,2},{12,4},{14,6},{1,9},{3,11}... | collective-permute-start | bytes 2752520 | tf_op jit(solution)/shard_map/ppermute | solution.py:143
  5.7 1.2 copy-start.4
  6.9 1.2 copy-start.6
  8.1 14.2 %copy-start.5 = (bf16[128,3584]{1,0:T(8,128)(2,1)S(1)}, bf16[128,3584]{1,0:T(8,128)(2,1)}, u32[]{:S(2)}) copy-start(bf16[128,3584]{1,0:T(8,128)(2,1)} %refs_1_.1) | copy-start | bytes 2752516
  9.2 38.1 %collective-permute-start.6 = (bf16[2,40,3584]{2,1,0:T(8,128)(2,1)S(1)}, bf16[2,40,3584]{2,1,0:T(8,128)(2,1)S(1)}, u32[]{:S(2)}, u32[]{:S(2)}) collective-permute-start(bf16[2,40,3584]{2,1,0:T(8,128)(2,1)S(1)} %get-tuple-element.82), channel_id=1, source_target_pairs={{0,4},{2,6},{4,0},{6,2},{8,12},{10,14},{12,8},{14,10},{1,5},{3,7},... | collective-permute-start | bytes 1720328 | tf_op jit(solution)/shard_map/ppermute | solution.py:143
  17.9 29.3 %collective-permute-start.7 = (bf16[2,40,3584]{2,1,0:T(8,128)(2,1)S(1)}, bf16[2,40,3584]{2,1,0:T(8,128)(2,1)S(1)}, u32[]{:S(2)}, u32[]{:S(2)}) collective-permute-start(bf16[2,40,3584]{2,1,0:T(8,128)(2,1)S(1)} %get-tuple-element.84), channel_id=1, source_target_pairs={{0,2},{2,0},{4,6},{6,4},{8,10},{10,8},{12,14},{14,12},{1,3},{3,1},... | collective-permute-start | bytes 1720328 | tf_op jit(solution)/shard_map/ppermute | solution.py:143
  19.5 27.7 %collective-permute-start.5 = (s32[2,128]{1,0:T(2,128)S(1)}, s32[2,128]{1,0:T(2,128)S(1)}, u32[]{:S(2)}, u32[]{:S(2)}) collective-permute-start(s32[2,128]{1,0:T(2,128)S(1)} %add_bitcast_fusion.index_ref), channel_id=1, source_target_pairs={{0,8},{2,10},{4,12},{6,14},{8,0},{10,2},{12,4},{14,6},{1,9},{3,11}... | collective-permute-start | bytes 3080 | tf_op jit(solution)/shard_map/ppermute | solution.py:143
  44.0 27.1 %collective-permute-start.1 = (bf16[40,3584]{1,0:T(8,128)(2,1)S(1)}, bf16[40,3584]{1,0:T(8,128)(2,1)S(1)}, u32[]{:S(2)}, u32[]{:S(2)}) collective-permute-start(bf16[40,3584]{1,0:T(8,128)(2,1)S(1)} %bitcast.37), channel_id=1, source_target_pairs={{0,8},{2,10},{4,12},{6,14},{8,0},{10,2},{12,4},{14,6},{1,9},{3,11}... | collective-permute-start | bytes 860168 | tf_op jit(solution)/shard_map/ppermute | solution.py:143
  47.3 24.6 %collective-permute-start.8 = (bf16[40,3584]{1,0:T(8,128)(2,1)S(1)}, bf16[40,3584]{1,0:T(8,128)(2,1)S(1)}, u32[]{:S(2)}, u32[]{:S(2)}) collective-permute-start(bf16[40,3584]{1,0:T(8,128)(2,1)S(1)} %bitcast.36), channel_id=1, source_target_pairs={{0,10},{2,8},{4,14},{6,12},{8,2},{10,0},{12,6},{14,4},{1,11},{3,9}... | collective-permute-start | bytes 860168 | tf_op jit(solution)/shard_map/ppermute | solution.py:143
  48.3 3.3 %copy-start.1 = (bf16[1,3584,512]{2,1,0:T(8,128)(2,1)S(1)}, bf16[1,3584,512]{2,1,0:T(8,128)(2,1)}, u32[]{:S(2)}) copy-start(bf16[1,3584,512]{2,1,0:T(8,128)(2,1)} %refs_1_.4) | copy-start | bytes 11010052
  48.9 27.0 %collective-permute-start.13 = (bf16[40,3584]{1,0:T(8,128)(2,1)S(1)}, bf16[40,3584]{1,0:T(8,128)(2,1)S(1)}, u32[]{:S(2)}, u32[]{:S(2)}) collective-permute-start(bf16[40,3584]{1,0:T(8,128)(2,1)S(1)} %bitcast.38), channel_id=1, source_target_pairs={{0,2},{2,0},{4,6},{6,4},{8,10},{10,8},{12,14},{14,12},{1,3},{3,1},... | collective-permute-start | bytes 860168 | tf_op jit(solution)/shard_map/ppermute | solution.py:143
  49.6 26.4 %collective-permute-start.14 = (bf16[2,40,3584]{2,1,0:T(8,128)(2,1)S(1)}, bf16[2,40,3584]{2,1,0:T(8,128)(2,1)S(1)}, u32[]{:S(2)}, u32[]{:S(2)}) collective-permute-start(bf16[2,40,3584]{2,1,0:T(8,128)(2,1)S(1)} %get-tuple-element.116), channel_id=1, source_target_pairs={{0,6},{2,4},{4,2},{6,0},{8,14},{10,12},{12,10},{14,8},{1,7},{3,5},... | collective-permute-start | bytes 1720328 | tf_op jit(solution)/shard_map/ppermute | solution.py:143
  51.4 2.0 %copy-start = (bf16[1,3584,512]{2,1,0:T(8,128)(2,1)S(1)}, bf16[1,3584,512]{2,1,0:T(8,128)(2,1)}, u32[]{:S(2)}) copy-start(bf16[1,3584,512]{2,1,0:T(8,128)(2,1)} %refs_0_.6) | copy-start | bytes 11010052
  53.4 2.0 %copy-start.2 = (bf16[1,512,3584]{2,1,0:T(8,128)(2,1)S(1)}, bf16[1,512,3584]{2,1,0:T(8,128)(2,1)}, u32[]{:S(2)}) copy-start(bf16[1,512,3584]{2,1,0:T(8,128)(2,1)} %refs_2_.2) | copy-start | bytes 11010052
  69.9 28.2 %collective-permute-start.11 = (bf16[40,3584]{1,0:T(8,128)(2,1)S(1)}, bf16[40,3584]{1,0:T(8,128)(2,1)S(1)}, u32[]{:S(2)}, u32[]{:S(2)}) collective-permute-start(bf16[40,3584]{1,0:T(8,128)(2,1)S(1)} %bitcast.35), channel_id=1, source_target_pairs={{0,4},{2,6},{4,0},{6,2},{8,12},{10,14},{12,8},{14,10},{1,5},{3,7},... | collective-permute-start | bytes 860168 | tf_op jit(solution)/shard_map/ppermute | solution.py:143
  71.1 28.0 %collective-permute-start.12 = (bf16[40,3584]{1,0:T(8,128)(2,1)S(1)}, bf16[40,3584]{1,0:T(8,128)(2,1)S(1)}, u32[]{:S(2)}, u32[]{:S(2)}) collective-permute-start(bf16[40,3584]{1,0:T(8,128)(2,1)S(1)} %bitcast.34), channel_id=1, source_target_pairs={{0,6},{2,4},{4,2},{6,0},{8,14},{10,12},{12,10},{14,8},{1,7},{3,5},... | collective-permute-start | bytes 860168 | tf_op jit(solution)/shard_map/ppermute | solution.py:143
  71.9 27.2 %collective-permute-start.9 = (bf16[40,3584]{1,0:T(8,128)(2,1)S(1)}, bf16[40,3584]{1,0:T(8,128)(2,1)S(1)}, u32[]{:S(2)}, u32[]{:S(2)}) collective-permute-start(bf16[40,3584]{1,0:T(8,128)(2,1)S(1)} %bitcast.33), channel_id=1, source_target_pairs={{0,12},{2,14},{4,8},{6,10},{8,4},{10,6},{12,0},{14,2},{1,13},{3,15... | collective-permute-start | bytes 860168 | tf_op jit(solution)/shard_map/ppermute | solution.py:143
  76.0 37.5 %collective-permute-start.10 = (bf16[40,3584]{1,0:T(8,128)(2,1)S(1)}, bf16[40,3584]{1,0:T(8,128)(2,1)S(1)}, u32[]{:S(2)}, u32[]{:S(2)}) collective-permute-start(bf16[40,3584]{1,0:T(8,128)(2,1)S(1)} %bitcast.32), channel_id=1, source_target_pairs={{0,14},{2,12},{4,10},{6,8},{8,6},{10,4},{12,2},{14,0},{1,15},{3,13... | collective-permute-start | bytes 860168 | tf_op jit(solution)/shard_map/ppermute | solution.py:143
  76.0 2.0 %copy-start.3 = (bf16[1,512,3584]{2,1,0:T(8,128)(2,1)S(1)}, bf16[1,512,3584]{2,1,0:T(8,128)(2,1)}, u32[]{:S(2)}) copy-start(bf16[1,512,3584]{2,1,0:T(8,128)(2,1)} %refs_2_.2) | copy-start | bytes 11010052
  92.6 39.1 %collective-permute-start.15 = (bf16[40,3712]{1,0:T(8,128)(2,1)S(1)}, bf16[40,3712]{1,0:T(8,128)(2,1)S(1)}, u32[]{:S(2)}, u32[]{:S(2)}) collective-permute-start(bf16[40,3712]{1,0:T(8,128)(2,1)S(1)} %get-tuple-element.122), channel_id=1, source_target_pairs={{0,8},{2,10},{4,12},{6,14},{8,0},{10,2},{12,4},{14,6},{1,9},{3,11}... | collective-permute-start | bytes 890888 | tf_op jit(solution)/shard_map/ppermute | solution.py:143
  98.1 35.7 %collective-permute-start.16 = (bf16[40,3712]{1,0:T(8,128)(2,1)S(1)}, bf16[40,3712]{1,0:T(8,128)(2,1)S(1)}, u32[]{:S(2)}, u32[]{:S(2)}) collective-permute-start(bf16[40,3712]{1,0:T(8,128)(2,1)S(1)} %get-tuple-element.123), channel_id=1, source_target_pairs={{0,10},{2,8},{4,14},{6,12},{8,2},{10,0},{12,6},{14,4},{1,11},{3,9}... | collective-permute-start | bytes 890888 | tf_op jit(solution)/shard_map/ppermute | solution.py:143
  113.4 20.5 %collective-permute-start.17 = (bf16[40,3712]{1,0:T(8,128)(2,1)S(1)}, bf16[40,3712]{1,0:T(8,128)(2,1)S(1)}, u32[]{:S(2)}, u32[]{:S(2)}) collective-permute-start(bf16[40,3712]{1,0:T(8,128)(2,1)S(1)} %get-tuple-element.136), channel_id=1, source_target_pairs={{0,2},{2,0},{4,6},{6,4},{8,10},{10,8},{12,14},{14,12},{1,3},{3,1},... | collective-permute-start | bytes 890888 | tf_op jit(solution)/shard_map/ppermute | solution.py:143
  113.4 20.5 %collective-permute-start.18 = (bf16[40,3712]{1,0:T(8,128)(2,1)S(1)}, bf16[40,3712]{1,0:T(8,128)(2,1)S(1)}, u32[]{:S(2)}, u32[]{:S(2)}) collective-permute-start(bf16[40,3712]{1,0:T(8,128)(2,1)S(1)} %get-tuple-element.137), channel_id=1, source_target_pairs={{0,4},{2,6},{4,0},{6,2},{8,12},{10,14},{12,8},{14,10},{1,5},{3,7},... | collective-permute-start | bytes 890888 | tf_op jit(solution)/shard_map/ppermute | solution.py:143
  113.5 29.2 %collective-permute-start.19 = (bf16[40,3712]{1,0:T(8,128)(2,1)S(1)}, bf16[40,3712]{1,0:T(8,128)(2,1)S(1)}, u32[]{:S(2)}, u32[]{:S(2)}) collective-permute-start(bf16[40,3712]{1,0:T(8,128)(2,1)S(1)} %get-tuple-element.138), channel_id=1, source_target_pairs={{0,6},{2,4},{4,2},{6,0},{8,14},{10,12},{12,10},{14,8},{1,7},{3,5},... | collective-permute-start | bytes 890888 | tf_op jit(solution)/shard_map/ppermute | solution.py:143
  131.7 15.6 %collective-permute-start.20 = (bf16[40,3712]{1,0:T(8,128)(2,1)S(1)}, bf16[40,3712]{1,0:T(8,128)(2,1)S(1)}, u32[]{:S(2)}, u32[]{:S(2)}) collective-permute-start(bf16[40,3712]{1,0:T(8,128)(2,1)S(1)} %get-tuple-element.139), channel_id=1, source_target_pairs={{0,12},{2,14},{4,8},{6,10},{8,4},{10,6},{12,0},{14,2},{1,13},{3,15... | collective-permute-start | bytes 890888 | tf_op jit(solution)/shard_map/ppermute | solution.py:143
  133.9 18.3 %collective-permute-start.21 = (bf16[40,3712]{1,0:T(8,128)(2,1)S(1)}, bf16[40,3712]{1,0:T(8,128)(2,1)S(1)}, u32[]{:S(2)}, u32[]{:S(2)}) collective-permute-start(bf16[40,3712]{1,0:T(8,128)(2,1)S(1)} %get-tuple-element.147), channel_id=1, source_target_pairs={{0,14},{2,12},{4,10},{6,8},{8,6},{10,4},{12,2},{14,0},{1,15},{3,13... | collective-permute-start | bytes 890888 | tf_op jit(solution)/shard_map/ppermute | solution.py:143
  147.3 0.7 copy-start.7

commit v7 on v6

--- a/solution.py
+++ b/solution.py
@@ -88,7 +88,7 @@
 def expert(tokens, upstream, own, other, blocks):
     rows, width = tokens.shape
     return pl.pallas_call(
-        functools.partial(expert_kernel, min(256, own[0].shape[2])),
+        functools.partial(expert_kernel, min(512, own[0].shape[2])),
         out_shape=[jax.ShapeDtypeStruct((rows // blocks, width + LANES), BF16)] * blocks,
         in_specs=[VMEM] * 8,
         out_specs=[VMEM] * blocks,
@@ -191,9 +191,10 @@
     got = got_side + got_cross
     zero = work([rows[0] for rows in got], [rows[1] for rows in got], weights)
     passed, zero = tie((passed[len(far1) :], zero))
-    pass_far2 = move(passed, cross)
-
-    up_far1, sent_far = tie((up_far1, sent_far))
+    pass_far2 = move(passed[:cut], cross[:cut])
+
+    up_far1, sent_far, passed = tie((up_far1, sent_far, passed[cut:]))
+    pass_far2 = pass_far2 + move(passed, cross[cut:])
     up_far2 = move(sent_far, far2)
     up_far1, pass_far1, got_last = tie((up_far1, pass_far1, got_last))
     first = work(

time: 154 us -> 153 us (level)
  Pallas kernels: 47.2 us -> 44.4 us
  starting transfers between devices: 31.5 us -> 33.7 us
    pallas_call x3, Pallas kernels: 43.6 us -> 40.8 us  [expert(): pl.pallas_call(functools.partial(expert_kernel, min(512, own[0].shape[2])...]
    ppermute x19, starting transfers between devices: 30.9 us -> 33 us  [move(): lax.ppermute(rows, CHIPS, [(i, i ^ offset) for i in range(chips)])]
  transfers between devices with their start and end apart: 22 -> 22, of which waited for: 8 -> 7; matrix products, arithmetic and copies ran while one was open for 2% -> 2% of each run, Pallas kernels for 30% -> 28%
where the time goes in v7:
time: 153 us; the launch traced here: 152 us
  waiting for transfers between devices  61.6 us (40%)
  Pallas kernels  44.4 us (29%)
  starting transfers between devices  33.7 us (22%)
  local copies, waits for them, and re-layouts  8.59 us (6%)
  other arithmetic  2.92 us (2%)
    ppermute x19, waiting for transfers between devices, move(): lax.ppermute(rows, CHIPS, [(i, i ^ offset) for i in range(chips)])  53.5 us
    pallas_call x3, Pallas kernels, expert(): pl.pallas_call(functools.partial(expert_kernel, min(512, own[0].shape[2])...  40.8 us
    ppermute x19, starting transfers between devices, move(): lax.ppermute(rows, CHIPS, [(i, i ^ offset) for i in range(chips)])  33 us
    unnamed x22, local copies, waits for them, and re-layouts  8.12 us
    ppermute x3, waiting for transfers between devices, swap_cores(): return lax.ppermute(values, 'core', [(0, 1), (1, 0)])  8.07 us
  transfers between devices with their start and end apart: 22, of which 7 were waited for; matrix products, arithmetic and copies ran while one was open for 2% of the time, Pallas kernels for 28%

profile of v7, /device:TPU:8, one launch (start us, length us, event | category | flops | bytes accessed | tf_op | source)
XLA Modules:
  0.0 152.4 jit_solution(17544290198552918678)
XLA Ops:
  1.3 2.6 %collective-permute-start = (bf16[128,3584]{1,0:T(8,128)(2,1)}, bf16[128,3584]{1,0:T(8,128)(2,1)S(1)}, u32[]{:S(2)}, u32[]{:S(2)}) collective-permute-start(bf16[128,3584]{1,0:T(8,128)(2,1)} %refs_0_.3), channel_id=1, source_target_pairs={{0,8},{2,10},{4,12},{6,14},{8,0},{10,2},{12,4},{14,6},{1,9},{3,11}... | collective-permute-start | bytes 2752520 | tf_op jit(solution)/shard_map/ppermute | solution.py:143
  3.9 0.7 convert_reduce_fusion.2
  4.9 0.8 select_reduce_fusion.5
  5.7 1.2 copy-done.4
  6.9 1.2 copy-done.6
  8.1 1.1 dispatch.4
  9.9 2.8 %collective-permute-done.3.refs_4_ = bf16[1,3584,512]{2,1,0:T(8,128)(2,1)} collective-permute-done((bf16[1,3584,512]{2,1,0:T(8,128)(2,1)}, bf16[1,3584,512]{2,1,0:T(8,128)(2,1)}, u32[]{:S(2)}, u32[]{:S(2)}) %collective-permute-start.3) | collective-permute-done | bytes 3670048 | tf_op jit(solution)/shard_map/ppermute | solution.py:30
  12.7 5.2 %collective-permute-done.4.refs_5_ = bf16[1,512,3584]{2,1,0:T(8,128)(2,1)} collective-permute-done((bf16[1,512,3584]{2,1,0:T(8,128)(2,1)}, bf16[1,512,3584]{2,1,0:T(8,128)(2,1)}, u32[]{:S(2)}, u32[]{:S(2)}) %collective-permute-start.4) | collective-permute-done | bytes 3670048 | tf_op jit(solution)/shard_map/ppermute | solution.py:30
  17.9 1.5 collective-permute-start.7
  19.5 2.7 %collective-permute-start.5 = (s32[2,128]{1,0:T(2,128)S(1)}, s32[2,128]{1,0:T(2,128)S(1)}, u32[]{:S(2)}, u32[]{:S(2)}) collective-permute-start(s32[2,128]{1,0:T(2,128)S(1)} %add_bitcast_fusion.index_ref), channel_id=1, source_target_pairs={{0,8},{2,10},{4,12},{6,14},{8,0},{10,2},{12,4},{14,6},{1,9},{3,11}... | collective-permute-start | bytes 3080 | tf_op jit(solution)/shard_map/ppermute | solution.py:143
  22.8 21.2 %collective-permute-done.refs_0_ = bf16[128,3584]{1,0:T(8,128)(2,1)S(1)} collective-permute-done((bf16[128,3584]{1,0:T(8,128)(2,1)}, bf16[128,3584]{1,0:T(8,128)(2,1)S(1)}, u32[]{:S(2)}, u32[]{:S(2)}) %collective-permute-start) | collective-permute-done | bytes 917536 | tf_op jit(solution)/shard_map/ppermute | solution.py:143
  44.0 3.3 %collective-permute-start.1 = (bf16[40,3584]{1,0:T(8,128)(2,1)S(1)}, bf16[40,3584]{1,0:T(8,128)(2,1)S(1)}, u32[]{:S(2)}, u32[]{:S(2)}) collective-permute-start(bf16[40,3584]{1,0:T(8,128)(2,1)S(1)} %bitcast.37), channel_id=1, source_target_pairs={{0,8},{2,10},{4,12},{6,14},{8,0},{10,2},{12,4},{14,6},{1,9},{3,11}... | collective-permute-start | bytes 860168 | tf_op jit(solution)/shard_map/ppermute | solution.py:143
  47.3 1.0 collective-permute-start.8
  49.6 1.8 %collective-permute-start.14 = (bf16[2,40,3584]{2,1,0:T(8,128)(2,1)S(1)}, bf16[2,40,3584]{2,1,0:T(8,128)(2,1)S(1)}, u32[]{:S(2)}, u32[]{:S(2)}) collective-permute-start(bf16[2,40,3584]{2,1,0:T(8,128)(2,1)S(1)} %get-tuple-element.118), channel_id=1, source_target_pairs={{0,6},{2,4},{4,2},{6,0},{8,14},{10,12},{12,10},{14,8},{1,7},{3,5},... | collective-permute-start | bytes 1720328 | tf_op jit(solution)/shard_map/ppermute | solution.py:143
  51.6 1.8 %copy-done = bf16[1,3584,512]{2,1,0:T(8,128)(2,1)S(1)} copy-done((bf16[1,3584,512]{2,1,0:T(8,128)(2,1)S(1)}, bf16[1,3584,512]{2,1,0:T(8,128)(2,1)}, u32[]{:S(2)}) %copy-start) | copy-done | bytes 3670040
  53.4 2.0 %copy-done.2 = bf16[1,512,3584]{2,1,0:T(8,128)(2,1)S(1)} copy-done((bf16[1,512,3584]{2,1,0:T(8,128)(2,1)S(1)}, bf16[1,512,3584]{2,1,0:T(8,128)(2,1)}, u32[]{:S(2)}) %copy-start.2) | copy-done | bytes 3670040
  55.5 13.5 %expert.3 = (bf16[40,3712]{1,0:T(8,128)(2,1)S(1)}, bf16[40,3712]{1,0:T(8,128)(2,1)S(1)}, bf16[40,3712]{1,0:T(8,128)(2,1)S(1)}) custom-call(bf16[120,3584]{1,0:T(8,128)(2,1)S(1)} %pad_maximum_fusion.tokens_ref, bf16[120,3584]{1,0:T(8,128)(2,1)S(1)} %pad_maximum_fusion.1.upstream_ref, bf16[1,3584,512]{2,1,0:T(8,128)(2,1)S(1)} %copy-done, ...), custom_call_target="tpu_custom_call" | custom-call | flops 1 | bytes 1 | tf_op jit(solution)/shard_map/expert/pallas_call | solution.py:90
  69.0 1.2 collective-permute-start.11
  70.2 1.8 %collective-permute-start.10 = (bf16[40,3584]{1,0:T(8,128)(2,1)S(1)}, bf16[40,3584]{1,0:T(8,128)(2,1)S(1)}, u32[]{:S(2)}, u32[]{:S(2)}) collective-permute-start(bf16[40,3584]{1,0:T(8,128)(2,1)S(1)} %bitcast.33), channel_id=1, source_target_pairs={{0,14},{2,12},{4,10},{6,8},{8,6},{10,4},{12,2},{14,0},{1,15},{3,13... | collective-permute-start | bytes 860168 | tf_op jit(solution)/shard_map/ppermute | solution.py:143
  72.0 4.1 %collective-permute-start.12 = (bf16[40,3584]{1,0:T(8,128)(2,1)S(1)}, bf16[40,3584]{1,0:T(8,128)(2,1)S(1)}, u32[]{:S(2)}, u32[]{:S(2)}) collective-permute-start(bf16[40,3584]{1,0:T(8,128)(2,1)S(1)} %bitcast.34), channel_id=1, source_target_pairs={{0,6},{2,4},{4,2},{6,0},{8,14},{10,12},{12,10},{14,8},{1,7},{3,5},... | collective-permute-start | bytes 860168 | tf_op jit(solution)/shard_map/ppermute | solution.py:143
  76.1 6.1 %collective-permute-done.13 = bf16[40,3584]{1,0:T(8,128)(2,1)S(1)} collective-permute-done((bf16[40,3584]{1,0:T(8,128)(2,1)S(1)}, bf16[40,3584]{1,0:T(8,128)(2,1)S(1)}, u32[]{:S(2)}, u32[]{:S(2)}) %collective-permute-start.13) | collective-permute-done | bytes 286752 | tf_op jit(solution)/shard_map/ppermute | solution.py:143
  82.4 1.8 %copy-done.3 = bf16[1,512,3584]{2,1,0:T(8,128)(2,1)S(1)} copy-done((bf16[1,512,3584]{2,1,0:T(8,128)(2,1)S(1)}, bf16[1,512,3584]{2,1,0:T(8,128)(2,1)}, u32[]{:S(2)}) %copy-start.3) | copy-done | bytes 3670040
  84.2 13.7 %expert.4 = (bf16[40,3712]{1,0:T(8,128)(2,1)S(1)}, bf16[40,3712]{1,0:T(8,128)(2,1)S(1)}, bf16[40,3712]{1,0:T(8,128)(2,1)S(1)}) custom-call(bf16[120,3584]{1,0:T(8,128)(2,1)S(1)} %pad_maximum_fusion.2.tokens_ref, bf16[120,3584]{1,0:T(8,128)(2,1)S(1)} %pad_maximum_fusion.3.upstream_ref, bf16[1,3584,512]{2,1,0:T(8,128)(2,1)S(1)} %copy-done, ...), custom_call_target="tpu_custom_call" | custom-call | flops 1 | bytes 1 | tf_op jit(solution)/shard_map/expert/pallas_call | solution.py:90
  97.9 4.2 %collective-permute-start.16 = (bf16[40,3712]{1,0:T(8,128)(2,1)S(1)}, bf16[40,3712]{1,0:T(8,128)(2,1)S(1)}, u32[]{:S(2)}, u32[]{:S(2)}) collective-permute-start(bf16[40,3712]{1,0:T(8,128)(2,1)S(1)} %get-tuple-element.125), channel_id=1, source_target_pairs={{0,10},{2,8},{4,14},{6,12},{8,2},{10,0},{12,6},{14,4},{1,11},{3,9}... | collective-permute-start | bytes 890888 | tf_op jit(solution)/shard_map/ppermute | solution.py:143
  103.1 2.7 %collective-permute-start.19 = (bf16[40,3712]{1,0:T(8,128)(2,1)S(1)}, bf16[40,3712]{1,0:T(8,128)(2,1)S(1)}, u32[]{:S(2)}, u32[]{:S(2)}) collective-permute-start(bf16[40,3712]{1,0:T(8,128)(2,1)S(1)} %get-tuple-element.140), channel_id=1, source_target_pairs={{0,6},{2,4},{4,2},{6,0},{8,14},{10,12},{12,10},{14,8},{1,7},{3,5},... | collective-permute-start | bytes 890888 | tf_op jit(solution)/shard_map/ppermute | solution.py:143
  105.8 13.6 %expert.5 = (bf16[40,3712]{1,0:T(8,128)(2,1)S(1)}, bf16[40,3712]{1,0:T(8,128)(2,1)S(1)}) custom-call(bf16[80,3584]{1,0:T(8,128)(2,1)S(1)} %pad_maximum_fusion.4.tokens_ref, bf16[80,3584]{1,0:T(8,128)(2,1)S(1)} %pad_maximum_fusion.5.upstream_ref, bf16[1,3584,512]{2,1,0:T(8,128)(2,1)S(1)} %copy-done, bf16[1,3584,512]{2,1,0:T(8,128)(2,1)S(1)} %copy-done.1, ...), custom_call_target="tpu_custom_call" | custom-call | flops 1 | bytes 1 | tf_op jit(solution)/shard_map/expert/pallas_call | solution.py:90
  119.4 3.2 %collective-permute-start.20 = (bf16[40,3712]{1,0:T(8,128)(2,1)S(1)}, bf16[40,3712]{1,0:T(8,128)(2,1)S(1)}, u32[]{:S(2)}, u32[]{:S(2)}) collective-permute-start(bf16[40,3712]{1,0:T(8,128)(2,1)S(1)} %get-tuple-element.141), channel_id=1, source_target_pairs={{0,12},{2,14},{4,8},{6,10},{8,4},{10,6},{12,0},{14,2},{1,13},{3,15... | collective-permute-start | bytes 890888 | tf_op jit(solution)/shard_map/ppermute | solution.py:143
  122.7 1.0 collective-permute-start.21
  123.7 14.7 %collective-permute-done.19 = bf16[40,3712]{1,0:T(8,128)(2,1)S(1)} collective-permute-done((bf16[40,3712]{1,0:T(8,128)(2,1)S(1)}, bf16[40,3712]{1,0:T(8,128)(2,1)S(1)}, u32[]{:S(2)}, u32[]{:S(2)}) %collective-permute-start.19) | collective-permute-done | bytes 296992 | tf_op jit(solution)/shard_map/ppermute | solution.py:143
  138.4 6.7 %collective-permute-done.20 = bf16[40,3712]{1,0:T(8,128)(2,1)S(1)} collective-permute-done((bf16[40,3712]{1,0:T(8,128)(2,1)S(1)}, bf16[40,3712]{1,0:T(8,128)(2,1)S(1)}, u32[]{:S(2)}, u32[]{:S(2)}) %collective-permute-start.20) | collective-permute-done | bytes 296992 | tf_op jit(solution)/shard_map/ppermute | solution.py:143
  145.1 4.9 %collective-permute-done.21 = bf16[40,3712]{1,0:T(8,128)(2,1)S(1)} collective-permute-done((bf16[40,3712]{1,0:T(8,128)(2,1)S(1)}, bf16[40,3712]{1,0:T(8,128)(2,1)S(1)}, u32[]{:S(2)}, u32[]{:S(2)}) %collective-permute-start.21) | collective-permute-done | bytes 296992 | tf_op jit(solution)/shard_map/ppermute | solution.py:143
  151.1 1.3 finish.1
  (77 shorter events, 6.6 us)
Async XLA Ops:
  0.6 9.2 %collective-permute-start.2 = (bf16[1,3584,512]{2,1,0:T(8,128)(2,1)}, bf16[1,3584,512]{2,1,0:T(8,128)(2,1)}, u32[]{:S(2)}, u32[]{:S(2)}) collective-permute-start(bf16[1,3584,512]{2,1,0:T(8,128)(2,1)} %refs_0_.6), channel_id=1, source_target_pairs={{0,1},{1,0},{2,3},{3,2},{4,5},{5,4},{6,7},{7,6},{8,9},{9,8},{10,11... | collective-permute-start | bytes 11010056 | tf_op jit(solution)/shard_map/ppermute | solution.py:30
  0.7 12.0 %collective-permute-start.3 = (bf16[1,3584,512]{2,1,0:T(8,128)(2,1)}, bf16[1,3584,512]{2,1,0:T(8,128)(2,1)}, u32[]{:S(2)}, u32[]{:S(2)}) collective-permute-start(bf16[1,3584,512]{2,1,0:T(8,128)(2,1)} %refs_1_.4), channel_id=1, source_target_pairs={{0,1},{1,0},{2,3},{3,2},{4,5},{5,4},{6,7},{7,6},{8,9},{9,8},{10,11... | collective-permute-start | bytes 11010056 | tf_op jit(solution)/shard_map/ppermute | solution.py:30
  1.2 16.7 %collective-permute-start.4 = (bf16[1,512,3584]{2,1,0:T(8,128)(2,1)}, bf16[1,512,3584]{2,1,0:T(8,128)(2,1)}, u32[]{:S(2)}, u32[]{:S(2)}) collective-permute-start(bf16[1,512,3584]{2,1,0:T(8,128)(2,1)} %refs_2_.2), channel_id=1, source_target_pairs={{0,1},{1,0},{2,3},{3,2},{4,5},{5,4},{6,7},{7,6},{8,9},{9,8},{10,11... | collective-permute-start | bytes 11010056 | tf_op jit(solution)/shard_map/ppermute | solution.py:30
  1.3 42.7 %collective-permute-start = (bf16[128,3584]{1,0:T(8,128)(2,1)}, bf16[128,3584]{1,0:T(8,128)(2,1)S(1)}, u32[]{:S(2)}, u32[]{:S(2)}) collective-permute-start(bf16[128,3584]{1,0:T(8,128)(2,1)} %refs_0_.3), channel_id=1, source_target_pairs={{0,8},{2,10},{4,12},{6,14},{8,0},{10,2},{12,4},{14,6},{1,9},{3,11}... | collective-permute-start | bytes 2752520 | tf_op jit(solution)/shard_map/ppermute | solution.py:143
  5.7 1.2 copy-start.4
  6.9 1.2 copy-start.6
  8.1 14.1 %copy-start.5 = (bf16[128,3584]{1,0:T(8,128)(2,1)S(1)}, bf16[128,3584]{1,0:T(8,128)(2,1)}, u32[]{:S(2)}) copy-start(bf16[128,3584]{1,0:T(8,128)(2,1)} %refs_1_.1) | copy-start | bytes 2752516
  9.2 38.1 %collective-permute-start.6 = (bf16[2,40,3584]{2,1,0:T(8,128)(2,1)S(1)}, bf16[2,40,3584]{2,1,0:T(8,128)(2,1)S(1)}, u32[]{:S(2)}, u32[]{:S(2)}) collective-permute-start(bf16[2,40,3584]{2,1,0:T(8,128)(2,1)S(1)} %get-tuple-element.83), channel_id=1, source_target_pairs={{0,4},{2,6},{4,0},{6,2},{8,12},{10,14},{12,8},{14,10},{1,5},{3,7},... | collective-permute-start | bytes 1720328 | tf_op jit(solution)/shard_map/ppermute | solution.py:143
  17.9 29.3 %collective-permute-start.7 = (bf16[2,40,3584]{2,1,0:T(8,128)(2,1)S(1)}, bf16[2,40,3584]{2,1,0:T(8,128)(2,1)S(1)}, u32[]{:S(2)}, u32[]{:S(2)}) collective-permute-start(bf16[2,40,3584]{2,1,0:T(8,128)(2,1)S(1)} %get-tuple-element.85), channel_id=1, source_target_pairs={{0,2},{2,0},{4,6},{6,4},{8,10},{10,8},{12,14},{14,12},{1,3},{3,1},... | collective-permute-start | bytes 1720328 | tf_op jit(solution)/shard_map/ppermute | solution.py:143
  19.5 27.7 %collective-permute-start.5 = (s32[2,128]{1,0:T(2,128)S(1)}, s32[2,128]{1,0:T(2,128)S(1)}, u32[]{:S(2)}, u32[]{:S(2)}) collective-permute-start(s32[2,128]{1,0:T(2,128)S(1)} %add_bitcast_fusion.index_ref), channel_id=1, source_target_pairs={{0,8},{2,10},{4,12},{6,14},{8,0},{10,2},{12,4},{14,6},{1,9},{3,11}... | collective-permute-start | bytes 3080 | tf_op jit(solution)/shard_map/ppermute | solution.py:143
  44.0 26.2 %collective-permute-start.1 = (bf16[40,3584]{1,0:T(8,128)(2,1)S(1)}, bf16[40,3584]{1,0:T(8,128)(2,1)S(1)}, u32[]{:S(2)}, u32[]{:S(2)}) collective-permute-start(bf16[40,3584]{1,0:T(8,128)(2,1)S(1)} %bitcast.37), channel_id=1, source_target_pairs={{0,8},{2,10},{4,12},{6,14},{8,0},{10,2},{12,4},{14,6},{1,9},{3,11}... | collective-permute-start | bytes 860168 | tf_op jit(solution)/shard_map/ppermute | solution.py:143
  47.3 4.4 %copy-start.1 = (bf16[1,3584,512]{2,1,0:T(8,128)(2,1)S(1)}, bf16[1,3584,512]{2,1,0:T(8,128)(2,1)}, u32[]{:S(2)}) copy-start(bf16[1,3584,512]{2,1,0:T(8,128)(2,1)} %refs_1_.4) | copy-start | bytes 11010052
  47.3 22.9 %collective-permute-start.8 = (bf16[40,3584]{1,0:T(8,128)(2,1)S(1)}, bf16[40,3584]{1,0:T(8,128)(2,1)S(1)}, u32[]{:S(2)}, u32[]{:S(2)}) collective-permute-start(bf16[40,3584]{1,0:T(8,128)(2,1)S(1)} %bitcast.36), channel_id=1, source_target_pairs={{0,10},{2,8},{4,14},{6,12},{8,2},{10,0},{12,6},{14,4},{1,11},{3,9}... | collective-permute-start | bytes 860168 | tf_op jit(solution)/shard_map/ppermute | solution.py:143
  49.0 33.1 %collective-permute-start.13 = (bf16[40,3584]{1,0:T(8,128)(2,1)S(1)}, bf16[40,3584]{1,0:T(8,128)(2,1)S(1)}, u32[]{:S(2)}, u32[]{:S(2)}) collective-permute-start(bf16[40,3584]{1,0:T(8,128)(2,1)S(1)} %bitcast.38), channel_id=1, source_target_pairs={{0,2},{2,0},{4,6},{6,4},{8,10},{10,8},{12,14},{14,12},{1,3},{3,1},... | collective-permute-start | bytes 860168 | tf_op jit(solution)/shard_map/ppermute | solution.py:143
  49.6 32.5 %collective-permute-start.14 = (bf16[2,40,3584]{2,1,0:T(8,128)(2,1)S(1)}, bf16[2,40,3584]{2,1,0:T(8,128)(2,1)S(1)}, u32[]{:S(2)}, u32[]{:S(2)}) collective-permute-start(bf16[2,40,3584]{2,1,0:T(8,128)(2,1)S(1)} %get-tuple-element.118), channel_id=1, source_target_pairs={{0,6},{2,4},{4,2},{6,0},{8,14},{10,12},{12,10},{14,8},{1,7},{3,5},... | collective-permute-start | bytes 1720328 | tf_op jit(solution)/shard_map/ppermute | solution.py:143
  51.4 2.0 %copy-start = (bf16[1,3584,512]{2,1,0:T(8,128)(2,1)S(1)}, bf16[1,3584,512]{2,1,0:T(8,128)(2,1)}, u32[]{:S(2)}) copy-start(bf16[1,3584,512]{2,1,0:T(8,128)(2,1)} %refs_0_.6) | copy-start | bytes 11010052
  53.4 2.0 %copy-start.2 = (bf16[1,512,3584]{2,1,0:T(8,128)(2,1)S(1)}, bf16[1,512,3584]{2,1,0:T(8,128)(2,1)}, u32[]{:S(2)}) copy-start(bf16[1,512,3584]{2,1,0:T(8,128)(2,1)} %refs_2_.2) | copy-start | bytes 11010052
  69.0 28.9 %collective-permute-start.11 = (bf16[40,3584]{1,0:T(8,128)(2,1)S(1)}, bf16[40,3584]{1,0:T(8,128)(2,1)S(1)}, u32[]{:S(2)}, u32[]{:S(2)}) collective-permute-start(bf16[40,3584]{1,0:T(8,128)(2,1)S(1)} %bitcast.35), channel_id=1, source_target_pairs={{0,4},{2,6},{4,0},{6,2},{8,12},{10,14},{12,8},{14,10},{1,5},{3,7},... | collective-permute-start | bytes 860168 | tf_op jit(solution)/shard_map/ppermute | solution.py:143
  70.2 31.9 %collective-permute-start.10 = (bf16[40,3584]{1,0:T(8,128)(2,1)S(1)}, bf16[40,3584]{1,0:T(8,128)(2,1)S(1)}, u32[]{:S(2)}, u32[]{:S(2)}) collective-permute-start(bf16[40,3584]{1,0:T(8,128)(2,1)S(1)} %bitcast.33), channel_id=1, source_target_pairs={{0,14},{2,12},{4,10},{6,8},{8,6},{10,4},{12,2},{14,0},{1,15},{3,13... | collective-permute-start | bytes 860168 | tf_op jit(solution)/shard_map/ppermute | solution.py:143
  72.0 30.1 %collective-permute-start.12 = (bf16[40,3584]{1,0:T(8,128)(2,1)S(1)}, bf16[40,3584]{1,0:T(8,128)(2,1)S(1)}, u32[]{:S(2)}, u32[]{:S(2)}) collective-permute-start(bf16[40,3584]{1,0:T(8,128)(2,1)S(1)} %bitcast.34), channel_id=1, source_target_pairs={{0,6},{2,4},{4,2},{6,0},{8,14},{10,12},{12,10},{14,8},{1,7},{3,5},... | collective-permute-start | bytes 860168 | tf_op jit(solution)/shard_map/ppermute | solution.py:143
  82.1 20.0 %collective-permute-start.9 = (bf16[40,3584]{1,0:T(8,128)(2,1)S(1)}, bf16[40,3584]{1,0:T(8,128)(2,1)S(1)}, u32[]{:S(2)}, u32[]{:S(2)}) collective-permute-start(bf16[40,3584]{1,0:T(8,128)(2,1)S(1)} %bitcast.32), channel_id=1, source_target_pairs={{0,12},{2,14},{4,8},{6,10},{8,4},{10,6},{12,0},{14,2},{1,13},{3,15... | collective-permute-start | bytes 860168 | tf_op jit(solution)/shard_map/ppermute | solution.py:143
  82.1 2.0 %copy-start.3 = (bf16[1,512,3584]{2,1,0:T(8,128)(2,1)S(1)}, bf16[1,512,3584]{2,1,0:T(8,128)(2,1)}, u32[]{:S(2)}) copy-start(bf16[1,512,3584]{2,1,0:T(8,128)(2,1)} %refs_2_.2) | copy-start | bytes 11010052
  97.8 21.6 %collective-permute-start.15 = (bf16[40,3712]{1,0:T(8,128)(2,1)S(1)}, bf16[40,3712]{1,0:T(8,128)(2,1)S(1)}, u32[]{:S(2)}, u32[]{:S(2)}) collective-permute-start(bf16[40,3712]{1,0:T(8,128)(2,1)S(1)} %get-tuple-element.124), channel_id=1, source_target_pairs={{0,8},{2,10},{4,12},{6,14},{8,0},{10,2},{12,4},{14,6},{1,9},{3,11}... | collective-permute-start | bytes 890888 | tf_op jit(solution)/shard_map/ppermute | solution.py:143
  97.9 40.4 %collective-permute-start.16 = (bf16[40,3712]{1,0:T(8,128)(2,1)S(1)}, bf16[40,3712]{1,0:T(8,128)(2,1)S(1)}, u32[]{:S(2)}, u32[]{:S(2)}) collective-permute-start(bf16[40,3712]{1,0:T(8,128)(2,1)S(1)} %get-tuple-element.125), channel_id=1, source_target_pairs={{0,10},{2,8},{4,14},{6,12},{8,2},{10,0},{12,6},{14,4},{1,11},{3,9}... | collective-permute-start | bytes 890888 | tf_op jit(solution)/shard_map/ppermute | solution.py:143
  102.1 20.6 %collective-permute-start.17 = (bf16[40,3712]{1,0:T(8,128)(2,1)S(1)}, bf16[40,3712]{1,0:T(8,128)(2,1)S(1)}, u32[]{:S(2)}, u32[]{:S(2)}) collective-permute-start(bf16[40,3712]{1,0:T(8,128)(2,1)S(1)} %get-tuple-element.138), channel_id=1, source_target_pairs={{0,2},{2,0},{4,6},{6,4},{8,10},{10,8},{12,14},{14,12},{1,3},{3,1},... | collective-permute-start | bytes 890888 | tf_op jit(solution)/shard_map/ppermute | solution.py:143
  102.7 21.0 %collective-permute-start.18 = (bf16[40,3712]{1,0:T(8,128)(2,1)S(1)}, bf16[40,3712]{1,0:T(8,128)(2,1)S(1)}, u32[]{:S(2)}, u32[]{:S(2)}) collective-permute-start(bf16[40,3712]{1,0:T(8,128)(2,1)S(1)} %get-tuple-element.139), channel_id=1, source_target_pairs={{0,4},{2,6},{4,0},{6,2},{8,12},{10,14},{12,8},{14,10},{1,5},{3,7},... | collective-permute-start | bytes 890888 | tf_op jit(solution)/shard_map/ppermute | solution.py:143
  103.1 46.9 %copy-start.7 = (f32[128,2]{0,1:T(2,128)S(1)}, f32[128,2]{0,1:T(2,128)}, u32[]{:S(2)}) copy-start(f32[128,2]{0,1:T(2,128)} %param.10) | copy-start | bytes 3076
  103.1 35.2 %collective-permute-start.19 = (bf16[40,3712]{1,0:T(8,128)(2,1)S(1)}, bf16[40,3712]{1,0:T(8,128)(2,1)S(1)}, u32[]{:S(2)}, u32[]{:S(2)}) collective-permute-start(bf16[40,3712]{1,0:T(8,128)(2,1)S(1)} %get-tuple-element.140), channel_id=1, source_target_pairs={{0,6},{2,4},{4,2},{6,0},{8,14},{10,12},{12,10},{14,8},{1,7},{3,5},... | collective-permute-start | bytes 890888 | tf_op jit(solution)/shard_map/ppermute | solution.py:143
  119.4 25.6 %collective-permute-start.20 = (bf16[40,3712]{1,0:T(8,128)(2,1)S(1)}, bf16[40,3712]{1,0:T(8,128)(2,1)S(1)}, u32[]{:S(2)}, u32[]{:S(2)}) collective-permute-start(bf16[40,3712]{1,0:T(8,128)(2,1)S(1)} %get-tuple-element.141), channel_id=1, source_target_pairs={{0,12},{2,14},{4,8},{6,10},{8,4},{10,6},{12,0},{14,2},{1,13},{3,15... | collective-permute-start | bytes 890888 | tf_op jit(solution)/shard_map/ppermute | solution.py:143
  122.7 27.2 %collective-permute-start.21 = (bf16[40,3712]{1,0:T(8,128)(2,1)S(1)}, bf16[40,3712]{1,0:T(8,128)(2,1)S(1)}, u32[]{:S(2)}, u32[]{:S(2)}) collective-permute-start(bf16[40,3712]{1,0:T(8,128)(2,1)S(1)} %get-tuple-element.149), channel_id=1, source_target_pairs={{0,14},{2,12},{4,10},{6,8},{8,6},{10,4},{12,2},{14,0},{1,15},{3,13... | collective-permute-start | bytes 890888 | tf_op jit(solution)/shard_map/ppermute | solution.py:143

commit v8 on v6

--- a/solution.py
+++ b/solution.py
@@ -88,7 +88,7 @@
 def expert(tokens, upstream, own, other, blocks):
     rows, width = tokens.shape
     return pl.pallas_call(
-        functools.partial(expert_kernel, min(256, own[0].shape[2])),
+        functools.partial(expert_kernel, min(512, own[0].shape[2])),
         out_shape=[jax.ShapeDtypeStruct((rows // blocks, width + LANES), BF16)] * blocks,
         in_specs=[VMEM] * 8,
         out_specs=[VMEM] * blocks,
@@ -190,10 +190,10 @@
     got_last = move(sent_last, cross[cut:])
     got = got_side + got_cross
     zero = work([rows[0] for rows in got], [rows[1] for rows in got], weights)
-    passed, zero = tie((passed[len(far1) :], zero))
+    sent_far, zero = tie((sent_far, zero))
+    passed = passed[len(far1) :]
+    up_far1, sent_far, passed = tie((up_far1, sent_far, passed))
     pass_far2 = move(passed, cross)
-
-    up_far1, sent_far = tie((up_far1, sent_far))
     up_far2 = move(sent_far, far2)
     up_far1, pass_far1, got_last = tie((up_far1, pass_far1, got_last))
     first = work(

time: 154 us -> 153 us (level)
  starting transfers between devices: 31.5 us -> 45.4 us
  waiting for transfers between devices: 61.8 us -> 49.4 us
  Pallas kernels: 47.2 us -> 44.4 us
    ppermute x19, starting transfers between devices: 30.9 us -> 44.7 us  [move(): lax.ppermute(rows, CHIPS, [(i, i ^ offset) for i in range(chips)])]
    ppermute x19, waiting for transfers between devices: 53.7 us -> 41.3 us  [move(): lax.ppermute(rows, CHIPS, [(i, i ^ offset) for i in range(chips)])]
    pallas_call x3, Pallas kernels: 43.6 us -> 40.8 us  [expert(): pl.pallas_call(functools.partial(expert_kernel, min(512, own[0].shape[2])...]
  transfers between devices with their start and end apart: 22 -> 22, of which waited for: 8 -> 7; matrix products, arithmetic and copies ran while one was open for 2% -> 2% of each run, Pallas kernels for 30% -> 28%
where the time goes in v8:
time: 153 us; the launch traced here: 152 us
  waiting for transfers between devices  49.4 us (32%)
  starting transfers between devices  45.4 us (30%)
  Pallas kernels  44.4 us (29%)
  local copies, waits for them, and re-layouts  8.96 us (6%)
  other arithmetic  2.93 us (2%)
    ppermute x19, starting transfers between devices, move(): lax.ppermute(rows, CHIPS, [(i, i ^ offset) for i in range(chips)])  44.7 us
    ppermute x19, waiting for transfers between devices, move(): lax.ppermute(rows, CHIPS, [(i, i ^ offset) for i in range(chips)])  41.3 us
    pallas_call x3, Pallas kernels, expert(): pl.pallas_call(functools.partial(expert_kernel, min(512, own[0].shape[2])...  40.8 us
    unnamed x22, local copies, waits for them, and re-layouts  8.48 us
    ppermute x3, waiting for transfers between devices, swap_cores(): return lax.ppermute(values, 'core', [(0, 1), (1, 0)])  8.07 us
  transfers between devices with their start and end apart: 22, of which 7 were waited for; matrix products, arithmetic and copies ran while one was open for 2% of the time, Pallas kernels for 28%

profile of v8, /device:TPU:8, one launch (start us, length us, event | category | flops | bytes accessed | tf_op | source)
XLA Modules:
  0.0 152.4 jit_solution(11172551088894701778)
XLA Ops:
  1.3 2.6 %collective-permute-start = (bf16[128,3584]{1,0:T(8,128)(2,1)}, bf16[128,3584]{1,0:T(8,128)(2,1)S(1)}, u32[]{:S(2)}, u32[]{:S(2)}) collective-permute-start(bf16[128,3584]{1,0:T(8,128)(2,1)} %refs_0_.3), channel_id=1, source_target_pairs={{0,8},{2,10},{4,12},{6,14},{8,0},{10,2},{12,4},{14,6},{1,9},{3,11}... | collective-permute-start | bytes 2752520 | tf_op jit(solution)/shard_map/ppermute | solution.py:143
  3.9 0.7 convert_reduce_fusion.2
  4.9 0.8 select_reduce_fusion.5
  5.7 1.2 copy-done.4
  6.9 1.2 copy-done.6
  8.1 1.1 dispatch.4
  9.9 2.8 %collective-permute-done.3.refs_4_ = bf16[1,3584,512]{2,1,0:T(8,128)(2,1)} collective-permute-done((bf16[1,3584,512]{2,1,0:T(8,128)(2,1)}, bf16[1,3584,512]{2,1,0:T(8,128)(2,1)}, u32[]{:S(2)}, u32[]{:S(2)}) %collective-permute-start.3) | collective-permute-done | bytes 3670048 | tf_op jit(solution)/shard_map/ppermute | solution.py:30
  12.7 5.2 %collective-permute-done.4.refs_5_ = bf16[1,512,3584]{2,1,0:T(8,128)(2,1)} collective-permute-done((bf16[1,512,3584]{2,1,0:T(8,128)(2,1)}, bf16[1,512,3584]{2,1,0:T(8,128)(2,1)}, u32[]{:S(2)}, u32[]{:S(2)}) %collective-permute-start.4) | collective-permute-done | bytes 3670048 | tf_op jit(solution)/shard_map/ppermute | solution.py:30
  17.9 1.5 collective-permute-start.7
  19.5 2.7 %collective-permute-start.5 = (s32[2,128]{1,0:T(2,128)S(1)}, s32[2,128]{1,0:T(2,128)S(1)}, u32[]{:S(2)}, u32[]{:S(2)}) collective-permute-start(s32[2,128]{1,0:T(2,128)S(1)} %add_bitcast_fusion.index_ref), channel_id=1, source_target_pairs={{0,8},{2,10},{4,12},{6,14},{8,0},{10,2},{12,4},{14,6},{1,9},{3,11}... | collective-permute-start | bytes 3080 | tf_op jit(solution)/shard_map/ppermute | solution.py:143
  22.8 21.2 %collective-permute-done.refs_0_ = bf16[128,3584]{1,0:T(8,128)(2,1)S(1)} collective-permute-done((bf16[128,3584]{1,0:T(8,128)(2,1)}, bf16[128,3584]{1,0:T(8,128)(2,1)S(1)}, u32[]{:S(2)}, u32[]{:S(2)}) %collective-permute-start) | collective-permute-done | bytes 917536 | tf_op jit(solution)/shard_map/ppermute | solution.py:143
  44.0 3.3 %collective-permute-start.1 = (bf16[40,3584]{1,0:T(8,128)(2,1)S(1)}, bf16[40,3584]{1,0:T(8,128)(2,1)S(1)}, u32[]{:S(2)}, u32[]{:S(2)}) collective-permute-start(bf16[40,3584]{1,0:T(8,128)(2,1)S(1)} %bitcast.37), channel_id=1, source_target_pairs={{0,8},{2,10},{4,12},{6,14},{8,0},{10,2},{12,4},{14,6},{1,9},{3,11}... | collective-permute-start | bytes 860168 | tf_op jit(solution)/shard_map/ppermute | solution.py:143
  47.3 1.0 collective-permute-start.8
  48.9 0.6 collective-permute-start.13
  49.6 1.8 %collective-permute-start.14 = (bf16[2,40,3584]{2,1,0:T(8,128)(2,1)S(1)}, bf16[2,40,3584]{2,1,0:T(8,128)(2,1)S(1)}, u32[]{:S(2)}, u32[]{:S(2)}) collective-permute-start(bf16[2,40,3584]{2,1,0:T(8,128)(2,1)S(1)} %get-tuple-element.120), channel_id=1, source_target_pairs={{0,6},{2,4},{4,2},{6,0},{8,14},{10,12},{12,10},{14,8},{1,7},{3,5},... | collective-permute-start | bytes 1720328 | tf_op jit(solution)/shard_map/ppermute | solution.py:143
  51.6 1.8 %copy-done = bf16[1,3584,512]{2,1,0:T(8,128)(2,1)S(1)} copy-done((bf16[1,3584,512]{2,1,0:T(8,128)(2,1)S(1)}, bf16[1,3584,512]{2,1,0:T(8,128)(2,1)}, u32[]{:S(2)}) %copy-start) | copy-done | bytes 3670040
  53.4 2.0 %copy-done.2 = bf16[1,512,3584]{2,1,0:T(8,128)(2,1)S(1)} copy-done((bf16[1,512,3584]{2,1,0:T(8,128)(2,1)S(1)}, bf16[1,512,3584]{2,1,0:T(8,128)(2,1)}, u32[]{:S(2)}) %copy-start.2) | copy-done | bytes 3670040
  55.4 13.5 %expert.3 = (bf16[40,3712]{1,0:T(8,128)(2,1)S(1)}, bf16[40,3712]{1,0:T(8,128)(2,1)S(1)}, bf16[40,3712]{1,0:T(8,128)(2,1)S(1)}) custom-call(bf16[120,3584]{1,0:T(8,128)(2,1)S(1)} %pad_maximum_fusion.tokens_ref, bf16[120,3584]{1,0:T(8,128)(2,1)S(1)} %pad_maximum_fusion.1.upstream_ref, bf16[1,3584,512]{2,1,0:T(8,128)(2,1)S(1)} %copy-done, ...), custom_call_target="tpu_custom_call" | custom-call | flops 1 | bytes 1 | tf_op jit(solution)/shard_map/expert/pallas_call | solution.py:90
  69.5 2.2 %collective-permute-start.9 = (bf16[40,3584]{1,0:T(8,128)(2,1)S(1)}, bf16[40,3584]{1,0:T(8,128)(2,1)S(1)}, u32[]{:S(2)}, u32[]{:S(2)}) collective-permute-start(bf16[40,3584]{1,0:T(8,128)(2,1)S(1)} %bitcast.33), channel_id=1, source_target_pairs={{0,12},{2,14},{4,8},{6,10},{8,4},{10,6},{12,0},{14,2},{1,13},{3,15... | collective-permute-start | bytes 860168 | tf_op jit(solution)/shard_map/ppermute | solution.py:143
  72.3 5.5 %collective-permute-start.11 = (bf16[40,3584]{1,0:T(8,128)(2,1)S(1)}, bf16[40,3584]{1,0:T(8,128)(2,1)S(1)}, u32[]{:S(2)}, u32[]{:S(2)}) collective-permute-start(bf16[40,3584]{1,0:T(8,128)(2,1)S(1)} %bitcast.35), channel_id=1, source_target_pairs={{0,4},{2,6},{4,0},{6,2},{8,12},{10,14},{12,8},{14,10},{1,5},{3,7},... | collective-permute-start | bytes 860168 | tf_op jit(solution)/shard_map/ppermute | solution.py:143
  77.8 0.8 collective-permute-start.12
  78.9 1.8 %copy-done.3 = bf16[1,512,3584]{2,1,0:T(8,128)(2,1)S(1)} copy-done((bf16[1,512,3584]{2,1,0:T(8,128)(2,1)S(1)}, bf16[1,512,3584]{2,1,0:T(8,128)(2,1)}, u32[]{:S(2)}) %copy-start.3) | copy-done | bytes 3670040
  80.7 13.7 %expert.4 = (bf16[40,3712]{1,0:T(8,128)(2,1)S(1)}, bf16[40,3712]{1,0:T(8,128)(2,1)S(1)}, bf16[40,3712]{1,0:T(8,128)(2,1)S(1)}) custom-call(bf16[120,3584]{1,0:T(8,128)(2,1)S(1)} %pad_maximum_fusion.2.tokens_ref, bf16[120,3584]{1,0:T(8,128)(2,1)S(1)} %pad_maximum_fusion.3.upstream_ref, bf16[1,3584,512]{2,1,0:T(8,128)(2,1)S(1)} %copy-done, ...), custom_call_target="tpu_custom_call" | custom-call | flops 1 | bytes 1 | tf_op jit(solution)/shard_map/expert/pallas_call | solution.py:90
  94.4 14.8 %collective-permute-start.15 = (bf16[40,3712]{1,0:T(8,128)(2,1)S(1)}, bf16[40,3712]{1,0:T(8,128)(2,1)S(1)}, u32[]{:S(2)}, u32[]{:S(2)}) collective-permute-start(bf16[40,3712]{1,0:T(8,128)(2,1)S(1)} %get-tuple-element.126), channel_id=1, source_target_pairs={{0,8},{2,10},{4,12},{6,14},{8,0},{10,2},{12,4},{14,6},{1,9},{3,11}... | collective-permute-start | bytes 890888 | tf_op jit(solution)/shard_map/ppermute | solution.py:143
  109.1 1.1 collective-permute-start.16
  111.0 3.1 %collective-permute-start.19 = (bf16[40,3712]{1,0:T(8,128)(2,1)S(1)}, bf16[40,3712]{1,0:T(8,128)(2,1)S(1)}, u32[]{:S(2)}, u32[]{:S(2)}) collective-permute-start(bf16[40,3712]{1,0:T(8,128)(2,1)S(1)} %get-tuple-element.142), channel_id=1, source_target_pairs={{0,6},{2,4},{4,2},{6,0},{8,14},{10,12},{12,10},{14,8},{1,7},{3,5},... | collective-permute-start | bytes 890888 | tf_op jit(solution)/shard_map/ppermute | solution.py:143
  114.0 13.6 %expert.5 = (bf16[40,3712]{1,0:T(8,128)(2,1)S(1)}, bf16[40,3712]{1,0:T(8,128)(2,1)S(1)}) custom-call(bf16[80,3584]{1,0:T(8,128)(2,1)S(1)} %pad_maximum_fusion.4.tokens_ref, bf16[80,3584]{1,0:T(8,128)(2,1)S(1)} %pad_maximum_fusion.5.upstream_ref, bf16[1,3584,512]{2,1,0:T(8,128)(2,1)S(1)} %copy-done, bf16[1,3584,512]{2,1,0:T(8,128)(2,1)S(1)} %copy-done.1, ...), custom_call_target="tpu_custom_call" | custom-call | flops 1 | bytes 1 | tf_op jit(solution)/shard_map/expert/pallas_call | solution.py:90
  127.6 1.4 collective-permute-start.20
  129.8 1.2 collective-permute-done.19
  131.0 16.5 %collective-permute-done.20 = bf16[40,3712]{1,0:T(8,128)(2,1)S(1)} collective-permute-done((bf16[40,3712]{1,0:T(8,128)(2,1)S(1)}, bf16[40,3712]{1,0:T(8,128)(2,1)S(1)}, u32[]{:S(2)}, u32[]{:S(2)}) %collective-permute-start.20) | collective-permute-done | bytes 296992 | tf_op jit(solution)/shard_map/ppermute | solution.py:143
  148.7 2.0 %collective-permute-done.21 = bf16[40,3712]{1,0:T(8,128)(2,1)S(1)} collective-permute-done((bf16[40,3712]{1,0:T(8,128)(2,1)S(1)}, bf16[40,3712]{1,0:T(8,128)(2,1)S(1)}, u32[]{:S(2)}, u32[]{:S(2)}) %collective-permute-start.21) | collective-permute-done | bytes 296992 | tf_op jit(solution)/shard_map/ppermute | solution.py:143
  151.0 1.3 finish.1
  (77 shorter events, 7.6 us)
Async XLA Ops:
  0.6 9.2 %collective-permute-start.2 = (bf16[1,3584,512]{2,1,0:T(8,128)(2,1)}, bf16[1,3584,512]{2,1,0:T(8,128)(2,1)}, u32[]{:S(2)}, u32[]{:S(2)}) collective-permute-start(bf16[1,3584,512]{2,1,0:T(8,128)(2,1)} %refs_0_.6), channel_id=1, source_target_pairs={{0,1},{1,0},{2,3},{3,2},{4,5},{5,4},{6,7},{7,6},{8,9},{9,8},{10,11... | collective-permute-start | bytes 11010056 | tf_op jit(solution)/shard_map/ppermute | solution.py:30
  0.7 12.0 %collective-permute-start.3 = (bf16[1,3584,512]{2,1,0:T(8,128)(2,1)}, bf16[1,3584,512]{2,1,0:T(8,128)(2,1)}, u32[]{:S(2)}, u32[]{:S(2)}) collective-permute-start(bf16[1,3584,512]{2,1,0:T(8,128)(2,1)} %refs_1_.4), channel_id=1, source_target_pairs={{0,1},{1,0},{2,3},{3,2},{4,5},{5,4},{6,7},{7,6},{8,9},{9,8},{10,11... | collective-permute-start | bytes 11010056 | tf_op jit(solution)/shard_map/ppermute | solution.py:30
  1.2 16.7 %collective-permute-start.4 = (bf16[1,512,3584]{2,1,0:T(8,128)(2,1)}, bf16[1,512,3584]{2,1,0:T(8,128)(2,1)}, u32[]{:S(2)}, u32[]{:S(2)}) collective-permute-start(bf16[1,512,3584]{2,1,0:T(8,128)(2,1)} %refs_2_.2), channel_id=1, source_target_pairs={{0,1},{1,0},{2,3},{3,2},{4,5},{5,4},{6,7},{7,6},{8,9},{9,8},{10,11... | collective-permute-start | bytes 11010056 | tf_op jit(solution)/shard_map/ppermute | solution.py:30
  1.3 42.7 %collective-permute-start = (bf16[128,3584]{1,0:T(8,128)(2,1)}, bf16[128,3584]{1,0:T(8,128)(2,1)S(1)}, u32[]{:S(2)}, u32[]{:S(2)}) collective-permute-start(bf16[128,3584]{1,0:T(8,128)(2,1)} %refs_0_.3), channel_id=1, source_target_pairs={{0,8},{2,10},{4,12},{6,14},{8,0},{10,2},{12,4},{14,6},{1,9},{3,11}... | collective-permute-start | bytes 2752520 | tf_op jit(solution)/shard_map/ppermute | solution.py:143
  5.7 1.2 copy-start.4
  6.9 1.2 copy-start.6
  8.1 14.1 %copy-start.5 = (bf16[128,3584]{1,0:T(8,128)(2,1)S(1)}, bf16[128,3584]{1,0:T(8,128)(2,1)}, u32[]{:S(2)}) copy-start(bf16[128,3584]{1,0:T(8,128)(2,1)} %refs_1_.1) | copy-start | bytes 2752516
  9.2 38.1 %collective-permute-start.6 = (bf16[2,40,3584]{2,1,0:T(8,128)(2,1)S(1)}, bf16[2,40,3584]{2,1,0:T(8,128)(2,1)S(1)}, u32[]{:S(2)}, u32[]{:S(2)}) collective-permute-start(bf16[2,40,3584]{2,1,0:T(8,128)(2,1)S(1)} %get-tuple-element.84), channel_id=1, source_target_pairs={{0,4},{2,6},{4,0},{6,2},{8,12},{10,14},{12,8},{14,10},{1,5},{3,7},... | collective-permute-start | bytes 1720328 | tf_op jit(solution)/shard_map/ppermute | solution.py:143
  17.9 29.3 %collective-permute-start.7 = (bf16[2,40,3584]{2,1,0:T(8,128)(2,1)S(1)}, bf16[2,40,3584]{2,1,0:T(8,128)(2,1)S(1)}, u32[]{:S(2)}, u32[]{:S(2)}) collective-permute-start(bf16[2,40,3584]{2,1,0:T(8,128)(2,1)S(1)} %get-tuple-element.86), channel_id=1, source_target_pairs={{0,2},{2,0},{4,6},{6,4},{8,10},{10,8},{12,14},{14,12},{1,3},{3,1},... | collective-permute-start | bytes 1720328 | tf_op jit(solution)/shard_map/ppermute | solution.py:143
  19.5 27.7 %collective-permute-start.5 = (s32[2,128]{1,0:T(2,128)S(1)}, s32[2,128]{1,0:T(2,128)S(1)}, u32[]{:S(2)}, u32[]{:S(2)}) collective-permute-start(s32[2,128]{1,0:T(2,128)S(1)} %add_bitcast_fusion.index_ref), channel_id=1, source_target_pairs={{0,8},{2,10},{4,12},{6,14},{8,0},{10,2},{12,4},{14,6},{1,9},{3,11}... | collective-permute-start | bytes 3080 | tf_op jit(solution)/shard_map/ppermute | solution.py:143
  44.0 25.0 %collective-permute-start.1 = (bf16[40,3584]{1,0:T(8,128)(2,1)S(1)}, bf16[40,3584]{1,0:T(8,128)(2,1)S(1)}, u32[]{:S(2)}, u32[]{:S(2)}) collective-permute-start(bf16[40,3584]{1,0:T(8,128)(2,1)S(1)} %bitcast.37), channel_id=1, source_target_pairs={{0,8},{2,10},{4,12},{6,14},{8,0},{10,2},{12,4},{14,6},{1,9},{3,11}... | collective-permute-start | bytes 860168 | tf_op jit(solution)/shard_map/ppermute | solution.py:143
  47.3 22.2 %collective-permute-start.8 = (bf16[40,3584]{1,0:T(8,128)(2,1)S(1)}, bf16[40,3584]{1,0:T(8,128)(2,1)S(1)}, u32[]{:S(2)}, u32[]{:S(2)}) collective-permute-start(bf16[40,3584]{1,0:T(8,128)(2,1)S(1)} %bitcast.36), channel_id=1, source_target_pairs={{0,10},{2,8},{4,14},{6,12},{8,2},{10,0},{12,6},{14,4},{1,11},{3,9}... | collective-permute-start | bytes 860168 | tf_op jit(solution)/shard_map/ppermute | solution.py:143
  48.3 3.3 %copy-start.1 = (bf16[1,3584,512]{2,1,0:T(8,128)(2,1)S(1)}, bf16[1,3584,512]{2,1,0:T(8,128)(2,1)}, u32[]{:S(2)}) copy-start(bf16[1,3584,512]{2,1,0:T(8,128)(2,1)} %refs_1_.4) | copy-start | bytes 11010052
  48.9 28.9 %collective-permute-start.13 = (bf16[40,3584]{1,0:T(8,128)(2,1)S(1)}, bf16[40,3584]{1,0:T(8,128)(2,1)S(1)}, u32[]{:S(2)}, u32[]{:S(2)}) collective-permute-start(bf16[40,3584]{1,0:T(8,128)(2,1)S(1)} %bitcast.38), channel_id=1, source_target_pairs={{0,2},{2,0},{4,6},{6,4},{8,10},{10,8},{12,14},{14,12},{1,3},{3,1},... | collective-permute-start | bytes 860168 | tf_op jit(solution)/shard_map/ppermute | solution.py:143
  49.6 29.0 %collective-permute-start.14 = (bf16[2,40,3584]{2,1,0:T(8,128)(2,1)S(1)}, bf16[2,40,3584]{2,1,0:T(8,128)(2,1)S(1)}, u32[]{:S(2)}, u32[]{:S(2)}) collective-permute-start(bf16[2,40,3584]{2,1,0:T(8,128)(2,1)S(1)} %get-tuple-element.120), channel_id=1, source_target_pairs={{0,6},{2,4},{4,2},{6,0},{8,14},{10,12},{12,10},{14,8},{1,7},{3,5},... | collective-permute-start | bytes 1720328 | tf_op jit(solution)/shard_map/ppermute | solution.py:143
  51.4 2.0 %copy-start = (bf16[1,3584,512]{2,1,0:T(8,128)(2,1)S(1)}, bf16[1,3584,512]{2,1,0:T(8,128)(2,1)}, u32[]{:S(2)}) copy-start(bf16[1,3584,512]{2,1,0:T(8,128)(2,1)} %refs_0_.6) | copy-start | bytes 11010052
  53.4 2.0 %copy-start.2 = (bf16[1,512,3584]{2,1,0:T(8,128)(2,1)S(1)}, bf16[1,512,3584]{2,1,0:T(8,128)(2,1)}, u32[]{:S(2)}) copy-start(bf16[1,512,3584]{2,1,0:T(8,128)(2,1)} %refs_2_.2) | copy-start | bytes 11010052
  69.5 39.7 %collective-permute-start.9 = (bf16[40,3584]{1,0:T(8,128)(2,1)S(1)}, bf16[40,3584]{1,0:T(8,128)(2,1)S(1)}, u32[]{:S(2)}, u32[]{:S(2)}) collective-permute-start(bf16[40,3584]{1,0:T(8,128)(2,1)S(1)} %bitcast.33), channel_id=1, source_target_pairs={{0,12},{2,14},{4,8},{6,10},{8,4},{10,6},{12,0},{14,2},{1,13},{3,15... | collective-permute-start | bytes 860168 | tf_op jit(solution)/shard_map/ppermute | solution.py:143
  71.7 38.6 %collective-permute-start.10 = (bf16[40,3584]{1,0:T(8,128)(2,1)S(1)}, bf16[40,3584]{1,0:T(8,128)(2,1)S(1)}, u32[]{:S(2)}, u32[]{:S(2)}) collective-permute-start(bf16[40,3584]{1,0:T(8,128)(2,1)S(1)} %bitcast.32), channel_id=1, source_target_pairs={{0,14},{2,12},{4,10},{6,8},{8,6},{10,4},{12,2},{14,0},{1,15},{3,13... | collective-permute-start | bytes 860168 | tf_op jit(solution)/shard_map/ppermute | solution.py:143
  72.3 38.0 %collective-permute-start.11 = (bf16[40,3584]{1,0:T(8,128)(2,1)S(1)}, bf16[40,3584]{1,0:T(8,128)(2,1)S(1)}, u32[]{:S(2)}, u32[]{:S(2)}) collective-permute-start(bf16[40,3584]{1,0:T(8,128)(2,1)S(1)} %bitcast.35), channel_id=1, source_target_pairs={{0,4},{2,6},{4,0},{6,2},{8,12},{10,14},{12,8},{14,10},{1,5},{3,7},... | collective-permute-start | bytes 860168 | tf_op jit(solution)/shard_map/ppermute | solution.py:143
  77.8 32.5 %collective-permute-start.12 = (bf16[40,3584]{1,0:T(8,128)(2,1)S(1)}, bf16[40,3584]{1,0:T(8,128)(2,1)S(1)}, u32[]{:S(2)}, u32[]{:S(2)}) collective-permute-start(bf16[40,3584]{1,0:T(8,128)(2,1)S(1)} %bitcast.34), channel_id=1, source_target_pairs={{0,6},{2,4},{4,2},{6,0},{8,14},{10,12},{12,10},{14,8},{1,7},{3,5},... | collective-permute-start | bytes 860168 | tf_op jit(solution)/shard_map/ppermute | solution.py:143
  78.6 2.0 %copy-start.3 = (bf16[1,512,3584]{2,1,0:T(8,128)(2,1)S(1)}, bf16[1,512,3584]{2,1,0:T(8,128)(2,1)}, u32[]{:S(2)}) copy-start(bf16[1,512,3584]{2,1,0:T(8,128)(2,1)} %refs_2_.2) | copy-start | bytes 11010052
  94.4 33.2 %collective-permute-start.15 = (bf16[40,3712]{1,0:T(8,128)(2,1)S(1)}, bf16[40,3712]{1,0:T(8,128)(2,1)S(1)}, u32[]{:S(2)}, u32[]{:S(2)}) collective-permute-start(bf16[40,3712]{1,0:T(8,128)(2,1)S(1)} %get-tuple-element.126), channel_id=1, source_target_pairs={{0,8},{2,10},{4,12},{6,14},{8,0},{10,2},{12,4},{14,6},{1,9},{3,11}... | collective-permute-start | bytes 890888 | tf_op jit(solution)/shard_map/ppermute | solution.py:143
  109.1 20.0 %collective-permute-start.16 = (bf16[40,3712]{1,0:T(8,128)(2,1)S(1)}, bf16[40,3712]{1,0:T(8,128)(2,1)S(1)}, u32[]{:S(2)}, u32[]{:S(2)}) collective-permute-start(bf16[40,3712]{1,0:T(8,128)(2,1)S(1)} %get-tuple-element.127), channel_id=1, source_target_pairs={{0,10},{2,8},{4,14},{6,12},{8,2},{10,0},{12,6},{14,4},{1,11},{3,9}... | collective-permute-start | bytes 890888 | tf_op jit(solution)/shard_map/ppermute | solution.py:143
  110.3 19.5 %collective-permute-start.17 = (bf16[40,3712]{1,0:T(8,128)(2,1)S(1)}, bf16[40,3712]{1,0:T(8,128)(2,1)S(1)}, u32[]{:S(2)}, u32[]{:S(2)}) collective-permute-start(bf16[40,3712]{1,0:T(8,128)(2,1)S(1)} %get-tuple-element.140), channel_id=1, source_target_pairs={{0,2},{2,0},{4,6},{6,4},{8,10},{10,8},{12,14},{14,12},{1,3},{3,1},... | collective-permute-start | bytes 890888 | tf_op jit(solution)/shard_map/ppermute | solution.py:143
  110.9 18.9 %collective-permute-start.18 = (bf16[40,3712]{1,0:T(8,128)(2,1)S(1)}, bf16[40,3712]{1,0:T(8,128)(2,1)S(1)}, u32[]{:S(2)}, u32[]{:S(2)}) collective-permute-start(bf16[40,3712]{1,0:T(8,128)(2,1)S(1)} %get-tuple-element.141), channel_id=1, source_target_pairs={{0,4},{2,6},{4,0},{6,2},{8,12},{10,14},{12,8},{14,10},{1,5},{3,7},... | collective-permute-start | bytes 890888 | tf_op jit(solution)/shard_map/ppermute | solution.py:143
  111.0 20.0 %collective-permute-start.19 = (bf16[40,3712]{1,0:T(8,128)(2,1)S(1)}, bf16[40,3712]{1,0:T(8,128)(2,1)S(1)}, u32[]{:S(2)}, u32[]{:S(2)}) collective-permute-start(bf16[40,3712]{1,0:T(8,128)(2,1)S(1)} %get-tuple-element.142), channel_id=1, source_target_pairs={{0,6},{2,4},{4,2},{6,0},{8,14},{10,12},{12,10},{14,8},{1,7},{3,5},... | collective-permute-start | bytes 890888 | tf_op jit(solution)/shard_map/ppermute | solution.py:143
  127.6 19.9 %collective-permute-start.20 = (bf16[40,3712]{1,0:T(8,128)(2,1)S(1)}, bf16[40,3712]{1,0:T(8,128)(2,1)S(1)}, u32[]{:S(2)}, u32[]{:S(2)}) collective-permute-start(bf16[40,3712]{1,0:T(8,128)(2,1)S(1)} %get-tuple-element.143), channel_id=1, source_target_pairs={{0,12},{2,14},{4,8},{6,10},{8,4},{10,6},{12,0},{14,2},{1,13},{3,15... | collective-permute-start | bytes 890888 | tf_op jit(solution)/shard_map/ppermute | solution.py:143
  129.1 21.5 %collective-permute-start.21 = (bf16[40,3712]{1,0:T(8,128)(2,1)S(1)}, bf16[40,3712]{1,0:T(8,128)(2,1)S(1)}, u32[]{:S(2)}, u32[]{:S(2)}) collective-permute-start(bf16[40,3712]{1,0:T(8,128)(2,1)S(1)} %get-tuple-element.151), channel_id=1, source_target_pairs={{0,14},{2,12},{4,10},{6,8},{8,6},{10,4},{12,2},{14,0},{1,15},{3,13... | collective-permute-start | bytes 890888 | tf_op jit(solution)/shard_map/ppermute | solution.py:143
  147.5 0.7 copy-start.7

commit v9 on v8

--- a/solution.py
+++ b/solution.py
@@ -60,8 +60,6 @@
 def expert_kernel(tile, tokens_ref, upstream_ref, *refs):
     pieces, out_refs, (total, part) = (refs[:3], refs[3:6]), refs[6:-2], refs[-2:]
     width = tokens_ref.shape[1]
-    total[...] = jnp.zeros_like(total)
-    part[...] = jnp.zeros_like(part)
     for gate_ref, up_ref, down_ref in pieces:
         for start in range(0, gate_ref.shape[2], tile):
             units = slice(start, start + tile)
@@ -73,11 +71,16 @@
             sigmoid_g = jax.nn.sigmoid(gate_lin)
             activated = gate_lin * sigmoid_g
             hidden = (activated * up_lin).astype(BF16).astype(F32)
-            part[...] += jnp.sum(projected * hidden, axis=1, keepdims=True)
+            parts = jnp.sum(projected * hidden, axis=1, keepdims=True)
             slope = sigmoid_g * (1.0 + gate_lin * (1.0 - sigmoid_g))
             d_gate = (projected * up_lin * slope).astype(BF16)
             d_up = (projected * activated).astype(BF16)
-            total[...] += nt(d_gate, gate_piece) + nt(d_up, up_piece)
+            sums = nt(d_gate, gate_piece) + nt(d_up, up_piece)
+            if start == 0 and gate_ref is pieces[0][0]:
+                part[...], total[...] = parts, sums
+            else:
+                part[...] += parts
+                total[...] += sums
     for place, out_ref in enumerate(out_refs):
         count = out_ref.shape[0]
         rows = slice(place * count, (place + 1) * count)

time: 153 us -> 153 us (level)
  no operation moved by 1% of the time
where the time goes in v9:
time: 153 us; the launch traced here: 152 us
  waiting for transfers between devices  49.4 us (32%)
  starting transfers between devices  45.4 us (30%)
  Pallas kernels  44.4 us (29%)
  local copies, waits for them, and re-layouts  8.96 us (6%)
  other arithmetic  2.93 us (2%)
    ppermute x19, starting transfers between devices, move(): lax.ppermute(rows, CHIPS, [(i, i ^ offset) for i in range(chips)])  44.7 us
    ppermute x19, waiting for transfers between devices, move(): lax.ppermute(rows, CHIPS, [(i, i ^ offset) for i in range(chips)])  41.3 us
    pallas_call x3, Pallas kernels, expert(): pl.pallas_call(functools.partial(expert_kernel, min(512, own[0].shape[2])...  40.8 us
    unnamed x22, local copies, waits for them, and re-layouts  8.48 us
    ppermute x3, waiting for transfers between devices, swap_cores(): return lax.ppermute(values, 'core', [(0, 1), (1, 0)])  8.07 us
  transfers between devices with their start and end apart: 22, of which 7 were waited for; matrix products, arithmetic and copies ran while one was open for 2% of the time, Pallas kernels for 28%

profile of v9, /device:TPU:8, one launch (start us, length us, event | category | flops | bytes accessed | tf_op | source)
XLA Modules:
  0.0 152.3 jit_solution(3150996186825902986)
XLA Ops:
  1.3 2.6 %collective-permute-start = (bf16[128,3584]{1,0:T(8,128)(2,1)}, bf16[128,3584]{1,0:T(8,128)(2,1)S(1)}, u32[]{:S(2)}, u32[]{:S(2)}) collective-permute-start(bf16[128,3584]{1,0:T(8,128)(2,1)} %refs_0_.3), channel_id=1, source_target_pairs={{0,8},{2,10},{4,12},{6,14},{8,0},{10,2},{12,4},{14,6},{1,9},{3,11}... | collective-permute-start | bytes 2752520 | tf_op jit(solution)/shard_map/ppermute | solution.py:146
  3.9 0.7 convert_reduce_fusion.2
  4.9 0.8 select_reduce_fusion.5
  5.7 1.2 copy-done.4
  6.9 1.2 copy-done.6
  8.1 1.1 dispatch.4
  9.9 2.8 %collective-permute-done.3.refs_4_ = bf16[1,3584,512]{2,1,0:T(8,128)(2,1)} collective-permute-done((bf16[1,3584,512]{2,1,0:T(8,128)(2,1)}, bf16[1,3584,512]{2,1,0:T(8,128)(2,1)}, u32[]{:S(2)}, u32[]{:S(2)}) %collective-permute-start.3) | collective-permute-done | bytes 3670048 | tf_op jit(solution)/shard_map/ppermute | solution.py:30
  12.7 5.2 %collective-permute-done.4.refs_5_ = bf16[1,512,3584]{2,1,0:T(8,128)(2,1)} collective-permute-done((bf16[1,512,3584]{2,1,0:T(8,128)(2,1)}, bf16[1,512,3584]{2,1,0:T(8,128)(2,1)}, u32[]{:S(2)}, u32[]{:S(2)}) %collective-permute-start.4) | collective-permute-done | bytes 3670048 | tf_op jit(solution)/shard_map/ppermute | solution.py:30
  17.9 1.5 collective-permute-start.7
  19.5 2.7 %collective-permute-start.5 = (s32[2,128]{1,0:T(2,128)S(1)}, s32[2,128]{1,0:T(2,128)S(1)}, u32[]{:S(2)}, u32[]{:S(2)}) collective-permute-start(s32[2,128]{1,0:T(2,128)S(1)} %add_bitcast_fusion.index_ref), channel_id=1, source_target_pairs={{0,8},{2,10},{4,12},{6,14},{8,0},{10,2},{12,4},{14,6},{1,9},{3,11}... | collective-permute-start | bytes 3080 | tf_op jit(solution)/shard_map/ppermute | solution.py:146
  22.8 21.2 %collective-permute-done.refs_0_ = bf16[128,3584]{1,0:T(8,128)(2,1)S(1)} collective-permute-done((bf16[128,3584]{1,0:T(8,128)(2,1)}, bf16[128,3584]{1,0:T(8,128)(2,1)S(1)}, u32[]{:S(2)}, u32[]{:S(2)}) %collective-permute-start) | collective-permute-done | bytes 917536 | tf_op jit(solution)/shard_map/ppermute | solution.py:146
  44.0 3.3 %collective-permute-start.1 = (bf16[40,3584]{1,0:T(8,128)(2,1)S(1)}, bf16[40,3584]{1,0:T(8,128)(2,1)S(1)}, u32[]{:S(2)}, u32[]{:S(2)}) collective-permute-start(bf16[40,3584]{1,0:T(8,128)(2,1)S(1)} %bitcast.37), channel_id=1, source_target_pairs={{0,8},{2,10},{4,12},{6,14},{8,0},{10,2},{12,4},{14,6},{1,9},{3,11}... | collective-permute-start | bytes 860168 | tf_op jit(solution)/shard_map/ppermute | solution.py:146
  47.3 1.0 collective-permute-start.8
  49.6 1.8 %collective-permute-start.14 = (bf16[2,40,3584]{2,1,0:T(8,128)(2,1)S(1)}, bf16[2,40,3584]{2,1,0:T(8,128)(2,1)S(1)}, u32[]{:S(2)}, u32[]{:S(2)}) collective-permute-start(bf16[2,40,3584]{2,1,0:T(8,128)(2,1)S(1)} %get-tuple-element.120), channel_id=1, source_target_pairs={{0,6},{2,4},{4,2},{6,0},{8,14},{10,12},{12,10},{14,8},{1,7},{3,5},... | collective-permute-start | bytes 1720328 | tf_op jit(solution)/shard_map/ppermute | solution.py:146
  51.6 1.8 %copy-done = bf16[1,3584,512]{2,1,0:T(8,128)(2,1)S(1)} copy-done((bf16[1,3584,512]{2,1,0:T(8,128)(2,1)S(1)}, bf16[1,3584,512]{2,1,0:T(8,128)(2,1)}, u32[]{:S(2)}) %copy-start) | copy-done | bytes 3670040
  53.4 2.0 %copy-done.2 = bf16[1,512,3584]{2,1,0:T(8,128)(2,1)S(1)} copy-done((bf16[1,512,3584]{2,1,0:T(8,128)(2,1)S(1)}, bf16[1,512,3584]{2,1,0:T(8,128)(2,1)}, u32[]{:S(2)}) %copy-start.2) | copy-done | bytes 3670040
  55.4 13.5 %expert.3 = (bf16[40,3712]{1,0:T(8,128)(2,1)S(1)}, bf16[40,3712]{1,0:T(8,128)(2,1)S(1)}, bf16[40,3712]{1,0:T(8,128)(2,1)S(1)}) custom-call(bf16[120,3584]{1,0:T(8,128)(2,1)S(1)} %pad_maximum_fusion.tokens_ref, bf16[120,3584]{1,0:T(8,128)(2,1)S(1)} %pad_maximum_fusion.1.upstream_ref, bf16[1,3584,512]{2,1,0:T(8,128)(2,1)S(1)} %copy-done, ...), custom_call_target="tpu_custom_call" | custom-call | flops 1 | bytes 1 | tf_op jit(solution)/shard_map/expert/pallas_call | solution.py:93
  69.5 2.1 %collective-permute-start.9 = (bf16[40,3584]{1,0:T(8,128)(2,1)S(1)}, bf16[40,3584]{1,0:T(8,128)(2,1)S(1)}, u32[]{:S(2)}, u32[]{:S(2)}) collective-permute-start(bf16[40,3584]{1,0:T(8,128)(2,1)S(1)} %bitcast.33), channel_id=1, source_target_pairs={{0,12},{2,14},{4,8},{6,10},{8,4},{10,6},{12,0},{14,2},{1,13},{3,15... | collective-permute-start | bytes 860168 | tf_op jit(solution)/shard_map/ppermute | solution.py:146
  71.6 0.7 collective-permute-start.10
  72.3 5.5 %collective-permute-start.11 = (bf16[40,3584]{1,0:T(8,128)(2,1)S(1)}, bf16[40,3584]{1,0:T(8,128)(2,1)S(1)}, u32[]{:S(2)}, u32[]{:S(2)}) collective-permute-start(bf16[40,3584]{1,0:T(8,128)(2,1)S(1)} %bitcast.35), channel_id=1, source_target_pairs={{0,4},{2,6},{4,0},{6,2},{8,12},{10,14},{12,8},{14,10},{1,5},{3,7},... | collective-permute-start | bytes 860168 | tf_op jit(solution)/shard_map/ppermute | solution.py:146
  77.8 0.8 collective-permute-start.12
  78.9 1.8 %copy-done.3 = bf16[1,512,3584]{2,1,0:T(8,128)(2,1)S(1)} copy-done((bf16[1,512,3584]{2,1,0:T(8,128)(2,1)S(1)}, bf16[1,512,3584]{2,1,0:T(8,128)(2,1)}, u32[]{:S(2)}) %copy-start.3) | copy-done | bytes 3670040
  80.7 13.7 %expert.4 = (bf16[40,3712]{1,0:T(8,128)(2,1)S(1)}, bf16[40,3712]{1,0:T(8,128)(2,1)S(1)}, bf16[40,3712]{1,0:T(8,128)(2,1)S(1)}) custom-call(bf16[120,3584]{1,0:T(8,128)(2,1)S(1)} %pad_maximum_fusion.2.tokens_ref, bf16[120,3584]{1,0:T(8,128)(2,1)S(1)} %pad_maximum_fusion.3.upstream_ref, bf16[1,3584,512]{2,1,0:T(8,128)(2,1)S(1)} %copy-done, ...), custom_call_target="tpu_custom_call" | custom-call | flops 1 | bytes 1 | tf_op jit(solution)/shard_map/expert/pallas_call | solution.py:93
  94.4 14.8 %collective-permute-start.15 = (bf16[40,3712]{1,0:T(8,128)(2,1)S(1)}, bf16[40,3712]{1,0:T(8,128)(2,1)S(1)}, u32[]{:S(2)}, u32[]{:S(2)}) collective-permute-start(bf16[40,3712]{1,0:T(8,128)(2,1)S(1)} %get-tuple-element.126), channel_id=1, source_target_pairs={{0,8},{2,10},{4,12},{6,14},{8,0},{10,2},{12,4},{14,6},{1,9},{3,11}... | collective-permute-start | bytes 890888 | tf_op jit(solution)/shard_map/ppermute | solution.py:146
  109.1 1.1 collective-permute-start.16
  110.9 3.1 %collective-permute-start.19 = (bf16[40,3712]{1,0:T(8,128)(2,1)S(1)}, bf16[40,3712]{1,0:T(8,128)(2,1)S(1)}, u32[]{:S(2)}, u32[]{:S(2)}) collective-permute-start(bf16[40,3712]{1,0:T(8,128)(2,1)S(1)} %get-tuple-element.142), channel_id=1, source_target_pairs={{0,6},{2,4},{4,2},{6,0},{8,14},{10,12},{12,10},{14,8},{1,7},{3,5},... | collective-permute-start | bytes 890888 | tf_op jit(solution)/shard_map/ppermute | solution.py:146
  114.0 13.6 %expert.5 = (bf16[40,3712]{1,0:T(8,128)(2,1)S(1)}, bf16[40,3712]{1,0:T(8,128)(2,1)S(1)}) custom-call(bf16[80,3584]{1,0:T(8,128)(2,1)S(1)} %pad_maximum_fusion.4.tokens_ref, bf16[80,3584]{1,0:T(8,128)(2,1)S(1)} %pad_maximum_fusion.5.upstream_ref, bf16[1,3584,512]{2,1,0:T(8,128)(2,1)S(1)} %copy-done, bf16[1,3584,512]{2,1,0:T(8,128)(2,1)S(1)} %copy-done.1, ...), custom_call_target="tpu_custom_call" | custom-call | flops 1 | bytes 1 | tf_op jit(solution)/shard_map/expert/pallas_call | solution.py:93
  127.6 1.4 collective-permute-start.20
  129.8 1.3 collective-permute-done.19
  131.1 16.3 %collective-permute-done.20 = bf16[40,3712]{1,0:T(8,128)(2,1)S(1)} collective-permute-done((bf16[40,3712]{1,0:T(8,128)(2,1)S(1)}, bf16[40,3712]{1,0:T(8,128)(2,1)S(1)}, u32[]{:S(2)}, u32[]{:S(2)}) %collective-permute-start.20) | collective-permute-done | bytes 296992 | tf_op jit(solution)/shard_map/ppermute | solution.py:146
  148.7 2.0 %collective-permute-done.21 = bf16[40,3712]{1,0:T(8,128)(2,1)S(1)} collective-permute-done((bf16[40,3712]{1,0:T(8,128)(2,1)S(1)}, bf16[40,3712]{1,0:T(8,128)(2,1)S(1)}, u32[]{:S(2)}, u32[]{:S(2)}) %collective-permute-start.21) | collective-permute-done | bytes 296992 | tf_op jit(solution)/shard_map/ppermute | solution.py:146
  151.0 1.3 finish.1
  (77 shorter events, 7.7 us)
Async XLA Ops:
  0.6 9.2 %collective-permute-start.2 = (bf16[1,3584,512]{2,1,0:T(8,128)(2,1)}, bf16[1,3584,512]{2,1,0:T(8,128)(2,1)}, u32[]{:S(2)}, u32[]{:S(2)}) collective-permute-start(bf16[1,3584,512]{2,1,0:T(8,128)(2,1)} %refs_0_.6), channel_id=1, source_target_pairs={{0,1},{1,0},{2,3},{3,2},{4,5},{5,4},{6,7},{7,6},{8,9},{9,8},{10,11... | collective-permute-start | bytes 11010056 | tf_op jit(solution)/shard_map/ppermute | solution.py:30
  0.7 12.0 %collective-permute-start.3 = (bf16[1,3584,512]{2,1,0:T(8,128)(2,1)}, bf16[1,3584,512]{2,1,0:T(8,128)(2,1)}, u32[]{:S(2)}, u32[]{:S(2)}) collective-permute-start(bf16[1,3584,512]{2,1,0:T(8,128)(2,1)} %refs_1_.4), channel_id=1, source_target_pairs={{0,1},{1,0},{2,3},{3,2},{4,5},{5,4},{6,7},{7,6},{8,9},{9,8},{10,11... | collective-permute-start | bytes 11010056 | tf_op jit(solution)/shard_map/ppermute | solution.py:30
  1.2 16.7 %collective-permute-start.4 = (bf16[1,512,3584]{2,1,0:T(8,128)(2,1)}, bf16[1,512,3584]{2,1,0:T(8,128)(2,1)}, u32[]{:S(2)}, u32[]{:S(2)}) collective-permute-start(bf16[1,512,3584]{2,1,0:T(8,128)(2,1)} %refs_2_.2), channel_id=1, source_target_pairs={{0,1},{1,0},{2,3},{3,2},{4,5},{5,4},{6,7},{7,6},{8,9},{9,8},{10,11... | collective-permute-start | bytes 11010056 | tf_op jit(solution)/shard_map/ppermute | solution.py:30
  1.3 42.7 %collective-permute-start = (bf16[128,3584]{1,0:T(8,128)(2,1)}, bf16[128,3584]{1,0:T(8,128)(2,1)S(1)}, u32[]{:S(2)}, u32[]{:S(2)}) collective-permute-start(bf16[128,3584]{1,0:T(8,128)(2,1)} %refs_0_.3), channel_id=1, source_target_pairs={{0,8},{2,10},{4,12},{6,14},{8,0},{10,2},{12,4},{14,6},{1,9},{3,11}... | collective-permute-start | bytes 2752520 | tf_op jit(solution)/shard_map/ppermute | solution.py:146
  5.7 1.2 copy-start.4
  6.9 1.2 copy-start.6
  8.1 14.1 %copy-start.5 = (bf16[128,3584]{1,0:T(8,128)(2,1)S(1)}, bf16[128,3584]{1,0:T(8,128)(2,1)}, u32[]{:S(2)}) copy-start(bf16[128,3584]{1,0:T(8,128)(2,1)} %refs_1_.1) | copy-start | bytes 2752516
  9.2 38.1 %collective-permute-start.6 = (bf16[2,40,3584]{2,1,0:T(8,128)(2,1)S(1)}, bf16[2,40,3584]{2,1,0:T(8,128)(2,1)S(1)}, u32[]{:S(2)}, u32[]{:S(2)}) collective-permute-start(bf16[2,40,3584]{2,1,0:T(8,128)(2,1)S(1)} %get-tuple-element.84), channel_id=1, source_target_pairs={{0,4},{2,6},{4,0},{6,2},{8,12},{10,14},{12,8},{14,10},{1,5},{3,7},... | collective-permute-start | bytes 1720328 | tf_op jit(solution)/shard_map/ppermute | solution.py:146
  17.9 29.3 %collective-permute-start.7 = (bf16[2,40,3584]{2,1,0:T(8,128)(2,1)S(1)}, bf16[2,40,3584]{2,1,0:T(8,128)(2,1)S(1)}, u32[]{:S(2)}, u32[]{:S(2)}) collective-permute-start(bf16[2,40,3584]{2,1,0:T(8,128)(2,1)S(1)} %get-tuple-element.86), channel_id=1, source_target_pairs={{0,2},{2,0},{4,6},{6,4},{8,10},{10,8},{12,14},{14,12},{1,3},{3,1},... | collective-permute-start | bytes 1720328 | tf_op jit(solution)/shard_map/ppermute | solution.py:146
  19.5 27.7 %collective-permute-start.5 = (s32[2,128]{1,0:T(2,128)S(1)}, s32[2,128]{1,0:T(2,128)S(1)}, u32[]{:S(2)}, u32[]{:S(2)}) collective-permute-start(s32[2,128]{1,0:T(2,128)S(1)} %add_bitcast_fusion.index_ref), channel_id=1, source_target_pairs={{0,8},{2,10},{4,12},{6,14},{8,0},{10,2},{12,4},{14,6},{1,9},{3,11}... | collective-permute-start | bytes 3080 | tf_op jit(solution)/shard_map/ppermute | solution.py:146
  44.0 25.0 %collective-permute-start.1 = (bf16[40,3584]{1,0:T(8,128)(2,1)S(1)}, bf16[40,3584]{1,0:T(8,128)(2,1)S(1)}, u32[]{:S(2)}, u32[]{:S(2)}) collective-permute-start(bf16[40,3584]{1,0:T(8,128)(2,1)S(1)} %bitcast.37), channel_id=1, source_target_pairs={{0,8},{2,10},{4,12},{6,14},{8,0},{10,2},{12,4},{14,6},{1,9},{3,11}... | collective-permute-start | bytes 860168 | tf_op jit(solution)/shard_map/ppermute | solution.py:146
  47.3 22.2 %collective-permute-start.8 = (bf16[40,3584]{1,0:T(8,128)(2,1)S(1)}, bf16[40,3584]{1,0:T(8,128)(2,1)S(1)}, u32[]{:S(2)}, u32[]{:S(2)}) collective-permute-start(bf16[40,3584]{1,0:T(8,128)(2,1)S(1)} %bitcast.36), channel_id=1, source_target_pairs={{0,10},{2,8},{4,14},{6,12},{8,2},{10,0},{12,6},{14,4},{1,11},{3,9}... | collective-permute-start | bytes 860168 | tf_op jit(solution)/shard_map/ppermute | solution.py:146
  48.3 3.3 %copy-start.1 = (bf16[1,3584,512]{2,1,0:T(8,128)(2,1)S(1)}, bf16[1,3584,512]{2,1,0:T(8,128)(2,1)}, u32[]{:S(2)}) copy-start(bf16[1,3584,512]{2,1,0:T(8,128)(2,1)} %refs_1_.4) | copy-start | bytes 11010052
  48.9 28.9 %collective-permute-start.13 = (bf16[40,3584]{1,0:T(8,128)(2,1)S(1)}, bf16[40,3584]{1,0:T(8,128)(2,1)S(1)}, u32[]{:S(2)}, u32[]{:S(2)}) collective-permute-start(bf16[40,3584]{1,0:T(8,128)(2,1)S(1)} %bitcast.38), channel_id=1, source_target_pairs={{0,2},{2,0},{4,6},{6,4},{8,10},{10,8},{12,14},{14,12},{1,3},{3,1},... | collective-permute-start | bytes 860168 | tf_op jit(solution)/shard_map/ppermute | solution.py:146
  49.6 29.0 %collective-permute-start.14 = (bf16[2,40,3584]{2,1,0:T(8,128)(2,1)S(1)}, bf16[2,40,3584]{2,1,0:T(8,128)(2,1)S(1)}, u32[]{:S(2)}, u32[]{:S(2)}) collective-permute-start(bf16[2,40,3584]{2,1,0:T(8,128)(2,1)S(1)} %get-tuple-element.120), channel_id=1, source_target_pairs={{0,6},{2,4},{4,2},{6,0},{8,14},{10,12},{12,10},{14,8},{1,7},{3,5},... | collective-permute-start | bytes 1720328 | tf_op jit(solution)/shard_map/ppermute | solution.py:146
  51.4 2.0 %copy-start = (bf16[1,3584,512]{2,1,0:T(8,128)(2,1)S(1)}, bf16[1,3584,512]{2,1,0:T(8,128)(2,1)}, u32[]{:S(2)}) copy-start(bf16[1,3584,512]{2,1,0:T(8,128)(2,1)} %refs_0_.6) | copy-start | bytes 11010052
  53.4 2.0 %copy-start.2 = (bf16[1,512,3584]{2,1,0:T(8,128)(2,1)S(1)}, bf16[1,512,3584]{2,1,0:T(8,128)(2,1)}, u32[]{:S(2)}) copy-start(bf16[1,512,3584]{2,1,0:T(8,128)(2,1)} %refs_2_.2) | copy-start | bytes 11010052
  69.5 39.7 %collective-permute-start.9 = (bf16[40,3584]{1,0:T(8,128)(2,1)S(1)}, bf16[40,3584]{1,0:T(8,128)(2,1)S(1)}, u32[]{:S(2)}, u32[]{:S(2)}) collective-permute-start(bf16[40,3584]{1,0:T(8,128)(2,1)S(1)} %bitcast.33), channel_id=1, source_target_pairs={{0,12},{2,14},{4,8},{6,10},{8,4},{10,6},{12,0},{14,2},{1,13},{3,15... | collective-permute-start | bytes 860168 | tf_op jit(solution)/shard_map/ppermute | solution.py:146
  71.6 38.7 %collective-permute-start.10 = (bf16[40,3584]{1,0:T(8,128)(2,1)S(1)}, bf16[40,3584]{1,0:T(8,128)(2,1)S(1)}, u32[]{:S(2)}, u32[]{:S(2)}) collective-permute-start(bf16[40,3584]{1,0:T(8,128)(2,1)S(1)} %bitcast.32), channel_id=1, source_target_pairs={{0,14},{2,12},{4,10},{6,8},{8,6},{10,4},{12,2},{14,0},{1,15},{3,13... | collective-permute-start | bytes 860168 | tf_op jit(solution)/shard_map/ppermute | solution.py:146
  72.3 38.0 %collective-permute-start.11 = (bf16[40,3584]{1,0:T(8,128)(2,1)S(1)}, bf16[40,3584]{1,0:T(8,128)(2,1)S(1)}, u32[]{:S(2)}, u32[]{:S(2)}) collective-permute-start(bf16[40,3584]{1,0:T(8,128)(2,1)S(1)} %bitcast.35), channel_id=1, source_target_pairs={{0,4},{2,6},{4,0},{6,2},{8,12},{10,14},{12,8},{14,10},{1,5},{3,7},... | collective-permute-start | bytes 860168 | tf_op jit(solution)/shard_map/ppermute | solution.py:146
  77.8 32.5 %collective-permute-start.12 = (bf16[40,3584]{1,0:T(8,128)(2,1)S(1)}, bf16[40,3584]{1,0:T(8,128)(2,1)S(1)}, u32[]{:S(2)}, u32[]{:S(2)}) collective-permute-start(bf16[40,3584]{1,0:T(8,128)(2,1)S(1)} %bitcast.34), channel_id=1, source_target_pairs={{0,6},{2,4},{4,2},{6,0},{8,14},{10,12},{12,10},{14,8},{1,7},{3,5},... | collective-permute-start | bytes 860168 | tf_op jit(solution)/shard_map/ppermute | solution.py:146
  78.6 2.0 %copy-start.3 = (bf16[1,512,3584]{2,1,0:T(8,128)(2,1)S(1)}, bf16[1,512,3584]{2,1,0:T(8,128)(2,1)}, u32[]{:S(2)}) copy-start(bf16[1,512,3584]{2,1,0:T(8,128)(2,1)} %refs_2_.2) | copy-start | bytes 11010052
  94.4 33.2 %collective-permute-start.15 = (bf16[40,3712]{1,0:T(8,128)(2,1)S(1)}, bf16[40,3712]{1,0:T(8,128)(2,1)S(1)}, u32[]{:S(2)}, u32[]{:S(2)}) collective-permute-start(bf16[40,3712]{1,0:T(8,128)(2,1)S(1)} %get-tuple-element.126), channel_id=1, source_target_pairs={{0,8},{2,10},{4,12},{6,14},{8,0},{10,2},{12,4},{14,6},{1,9},{3,11}... | collective-permute-start | bytes 890888 | tf_op jit(solution)/shard_map/ppermute | solution.py:146
  109.1 20.0 %collective-permute-start.16 = (bf16[40,3712]{1,0:T(8,128)(2,1)S(1)}, bf16[40,3712]{1,0:T(8,128)(2,1)S(1)}, u32[]{:S(2)}, u32[]{:S(2)}) collective-permute-start(bf16[40,3712]{1,0:T(8,128)(2,1)S(1)} %get-tuple-element.127), channel_id=1, source_target_pairs={{0,10},{2,8},{4,14},{6,12},{8,2},{10,0},{12,6},{14,4},{1,11},{3,9}... | collective-permute-start | bytes 890888 | tf_op jit(solution)/shard_map/ppermute | solution.py:146
  110.3 19.5 %collective-permute-start.17 = (bf16[40,3712]{1,0:T(8,128)(2,1)S(1)}, bf16[40,3712]{1,0:T(8,128)(2,1)S(1)}, u32[]{:S(2)}, u32[]{:S(2)}) collective-permute-start(bf16[40,3712]{1,0:T(8,128)(2,1)S(1)} %get-tuple-element.140), channel_id=1, source_target_pairs={{0,2},{2,0},{4,6},{6,4},{8,10},{10,8},{12,14},{14,12},{1,3},{3,1},... | collective-permute-start | bytes 890888 | tf_op jit(solution)/shard_map/ppermute | solution.py:146
  110.8 18.9 %collective-permute-start.18 = (bf16[40,3712]{1,0:T(8,128)(2,1)S(1)}, bf16[40,3712]{1,0:T(8,128)(2,1)S(1)}, u32[]{:S(2)}, u32[]{:S(2)}) collective-permute-start(bf16[40,3712]{1,0:T(8,128)(2,1)S(1)} %get-tuple-element.141), channel_id=1, source_target_pairs={{0,4},{2,6},{4,0},{6,2},{8,12},{10,14},{12,8},{14,10},{1,5},{3,7},... | collective-permute-start | bytes 890888 | tf_op jit(solution)/shard_map/ppermute | solution.py:146
  110.9 20.2 %collective-permute-start.19 = (bf16[40,3712]{1,0:T(8,128)(2,1)S(1)}, bf16[40,3712]{1,0:T(8,128)(2,1)S(1)}, u32[]{:S(2)}, u32[]{:S(2)}) collective-permute-start(bf16[40,3712]{1,0:T(8,128)(2,1)S(1)} %get-tuple-element.142), channel_id=1, source_target_pairs={{0,6},{2,4},{4,2},{6,0},{8,14},{10,12},{12,10},{14,8},{1,7},{3,5},... | collective-permute-start | bytes 890888 | tf_op jit(solution)/shard_map/ppermute | solution.py:146
  127.6 19.9 %collective-permute-start.20 = (bf16[40,3712]{1,0:T(8,128)(2,1)S(1)}, bf16[40,3712]{1,0:T(8,128)(2,1)S(1)}, u32[]{:S(2)}, u32[]{:S(2)}) collective-permute-start(bf16[40,3712]{1,0:T(8,128)(2,1)S(1)} %get-tuple-element.143), channel_id=1, source_target_pairs={{0,12},{2,14},{4,8},{6,10},{8,4},{10,6},{12,0},{14,2},{1,13},{3,15... | collective-permute-start | bytes 890888 | tf_op jit(solution)/shard_map/ppermute | solution.py:146
  129.1 21.5 %collective-permute-start.21 = (bf16[40,3712]{1,0:T(8,128)(2,1)S(1)}, bf16[40,3712]{1,0:T(8,128)(2,1)S(1)}, u32[]{:S(2)}, u32[]{:S(2)}) collective-permute-start(bf16[40,3712]{1,0:T(8,128)(2,1)S(1)} %get-tuple-element.151), channel_id=1, source_target_pairs={{0,14},{2,12},{4,10},{6,8},{8,6},{10,4},{12,2},{14,0},{1,15},{3,13... | collective-permute-start | bytes 890888 | tf_op jit(solution)/shard_map/ppermute | solution.py:146
  147.5 0.7 copy-start.7
